TPU v7x, 256 devices: a whole 4x4x8 slice. The times are simulated.
256 devices in a mesh: dp: 16 (over y, x_lo, core), grad: 16 (over x_hi, z).
Axes of the slice: x: 4 (x_hi: 2, x_lo: 2; x = x_hi * 2 + x_lo), y: 4, z: 8, core: 2. Of those that a mesh axis runs over, the one named last changes fastest.
Arguments:
- acts: bfloat16 [1, 32768, 2560], P(None, 'dp', 'grad'), may hold values from -6 to 6
- out_grads: bfloat16 [1, 32768, 2560], P(None, 'dp', 'grad'), may hold values from -6 to 6
- factor_in: float32 [1, 2560, 2560], P(None, 'dp', 'grad'), may hold values from -3 to 3
- factor_out: float32 [1, 2560, 2560], P(None, 'dp', 'grad'), may hold values from -3 to 3
- basis_in: bfloat16 [1, 2560, 2560], P(None, 'dp'), may hold values from -0.125 to 0.125
- basis_out: bfloat16 [1, 2560, 2560], P(None, 'grad'), may hold values from -0.125 to 0.125
- eig_in: float32 [1, 2560], P(None, 'dp'), may hold values from 0.01 to 1
- eig_out: float32 [1, 2560], P(None, 'grad'), may hold values from 0.01 to 1
Outputs:
- new_factor_in: float32 [1, 2560, 2560], P(None, 'dp', 'grad')
- new_factor_out: float32 [1, 2560, 2560], P(None, 'dp', 'grad')
- precond: bfloat16 [1, 2560, 2560], P(None, 'dp', 'grad')
All inputs are finite; a program needn't handle non-finite values.
Results may differ from a plain program's by a relative error of at most 0.009.
Values may be sent and summed in bfloat16 or wider, within the bound.
No kernel may reach another device: no remote copies, remote signals or barrier semaphores. Data moves between devices by JAX's collectives and lax.ppermute only.
A program may use at most 128 MiB of HBM per device.

v0:
```python
import functools

import jax
import jax.numpy as jnp
from jax import lax
from jax.experimental import pallas as pl
from jax.experimental.pallas import tpu as pltpu
from jax.sharding import Mesh, PartitionSpec as P

decay = 0.5
damping = 0.001
AXES = ("y", "xl", "c", "xh", "z")
DP = ("y", "xl", "c")
GRAD = ("xh", "z")
ROW = ("xh", "y", "xl")
COL = ("z", "c")
bf16 = jnp.bfloat16
f32 = jnp.float32


def dot(left, right, contract):
    return lax.dot_general(left, right, ((contract[:1], contract[1:]), ((), ())), preferred_element_type=f32)


def pack(rest):
    rows = rest.shape[0] // 4
    return jnp.concatenate([rest[rows * q : rows * (q + 1)] for q in range(4)], axis=1)


def unpack(value):
    rows, lanes = value.shape[0] * 4 // 5, value.shape[1]
    part = lanes // 4
    rest = jnp.concatenate([value[rows:, part * q : part * (q + 1)] for q in range(4)], axis=0)
    return jnp.concatenate([value[:rows], rest], axis=1)


class Emit:
    def __init__(self, out, slots, sems):
        self.out, self.slots, self.sems, self.copies = out, slots, sems, []

    def send(self, slot, index):
        number = len(self.copies)
        copy = pltpu.make_async_copy(self.slots.at[slot], self.out.at[index], self.sems.at[number])
        copy.start()
        self.copies.append(copy)

    def put(self, index, value):
        slot = len(self.copies)
        self.slots[slot] = value.astype(self.slots.dtype)
        self.send(slot, index)

    def parts(self, index, main, rest):
        slot = len(self.copies)
        rows = main.shape[0]
        self.slots[slot, :rows] = main.astype(bf16)
        self.slots[slot, rows:] = pack(rest).astype(bf16)
        self.send(slot, index)

    def __call__(self, index, value):
        self.parts(index, value[:, :128], value[:, 128:])

    def everywhere(self, value):
        self(0, value)
        for index in range(1, self.out.shape[0]):
            self.send(0, index)


def call(kernel, ins, outs, after=(), small=(), alias=(), scratch=(), flops=0):
    n, s, a, t, o = len(ins), len(small), len(alias), len(after), len(outs)

    def wrapped(*refs):
        in_refs, small_refs = refs[:n], refs[n : n + s]
        rest = refs[n + s + a + t :]
        out_refs, rest = rest[:o], rest[o:]
        held, in_sems, rest = rest[:n], rest[n], rest[n + 1 :]
        copies = [pltpu.make_async_copy(in_refs[k], held[k], in_sems.at[k]) for k in range(n)]
        for copy in copies:
            copy.start()
        waited = set()

        def get(k):
            if k not in waited:
                copies[k].wait()
                waited.add(k)
            return held[k]

        emits = [Emit(out_refs[k], rest[2 * k], rest[2 * k + 1]) for k in range(o)]
        kernel(get, small_refs, *emits, *rest[2 * o :])
        for k in range(n):
            get(k)
        for emit in emits:
            for copy in emit.copies:
                copy.wait()

    hbm, vmem = pl.BlockSpec(memory_space=pltpu.HBM), pl.BlockSpec(memory_space=pltpu.VMEM)
    space = [pltpu.VMEM(x.shape, x.dtype) for x in ins] + [pltpu.SemaphoreType.DMA((n,))]
    for shape, slots, dtype in outs:
        space += [pltpu.VMEM((slots,) + shape[1:], dtype), pltpu.SemaphoreType.DMA((max(slots, shape[0]),))]
    size = sum(x.size * x.dtype.itemsize for x in ins)
    return pl.pallas_call(
        wrapped,
        out_shape=[jax.ShapeDtypeStruct(shape, dtype) for shape, _, dtype in outs],
        in_specs=[hbm] * n + [vmem] * s + [hbm] * (a + t),
        out_specs=[hbm] * o,
        scratch_shapes=space + [pltpu.VMEM(shape, dtype) for shape, dtype in scratch],
        input_output_aliases={n + s + k: k for k in range(a)},
        compiler_params=pltpu.CompilerParams(vmem_limit_bytes=20 * 2**20),
        cost_estimate=pl.CostEstimate(flops=flops, bytes_accessed=size, transcendentals=0),
    )(*ins, *small, *alias, *after)


def shift(value, axis, step):
    size = lax.axis_size(axis)
    return lax.ppermute(value, axis, [(i, (i + step) % size) for i in range(size)])


def exchange(chunks, axes):
    return lax.all_to_all(chunks, axes, 0, 0, tiled=True)


def pairs_of(there):
    pairs = []
    for y in range(4):
        for xl in range(2):
            for c in range(2):
                for xh in range(2):
                    for z in range(8):
                        here = (((y * 2 + xl) * 2 + c) * 2 + xh) * 8 + z
                        to = there(y, xl, c, xh, z)
                        if to is not None:
                            pairs.append((here, to))
    return pairs


def to_output(y, xl, c, xh, z):
    return (xh * 8 + y * 2 + xl) * 16 + c * 8 + z


def cross_core(y, xl, c, xh, z):
    return (((y * 2 + xl) * 2 + xh) * 2 + c) * 8 + z


def swapped(y, xl, c, xh, z):
    return ((((xh * 2 + y % 2) * 2 + xl) * 2 + c) * 2 + y // 2) * 8 + z


def window_place(transposed):
    def there(y, xl, c, xh, z):
        cross, distance = y // 2, (y % 2 * 2 + xl) * 2 + c
        if distance > 4 or (transposed and distance not in (1, 2, 3)):
            return None
        row = ((xh + cross) % 2) * 8 + (z - 2) % 8
        column = xh * 8 + (z - 2 + distance) % 8
        return column * 16 + row if transposed else row * 16 + column

    return there


def order(*values):
    return lax.optimization_barrier(values)


def body(acts, out_grads, factor_in, factor_out, basis_in, basis_out, eig_in, eig_out):
    total_tokens = acts.shape[1] * lax.axis_size(DP)
    width = acts.shape[2]
    full = basis_in.shape[2]
    count = full // width
    rest = width - 128
    square = (width, width)
    packed = (width * width // 128, 128)
    chunked = (count,) + packed
    act, grad = acts[0].T, out_grads[0].T
    square_flops = 2 * count * width**3
    pair_flops = 2 * width * width * act.shape[1]
    half = width // 2

    def reorder_kernel(get, small, *outs):
        for which, out in enumerate(outs):
            for k in range(count):
                start = k * width
                out.slots[0, :, k * 128 : (k + 1) * 128] = get(which)[:, start : start + 128]
            for k in range(0, count, 4):
                pieces = [get(which)[:, q * width + 128 : (q + 1) * width] for q in range(k, k + 4)]
                out.slots[0, :, count * 128 + k * rest : count * 128 + (k + 4) * rest] = jnp.concatenate(pieces, axis=1)
            out.send(0, 0)

    up1, down1 = shift(act, "z", 1), shift(act, "z", -1)
    grad_flip = shift(grad, "xh", 1)
    act_flip = shift(act, "xh", 1)
    rows = call(reorder_kernel, [basis_out[0], basis_in[0]], [((1, width, full), 1, bf16)] * 2)
    up1, down1, rows_out, rows_in = order(up1, down1, *rows)
    up2, down2 = shift(up1, "z", 1), shift(down1, "z", -1)
    rows_out = lax.ppermute(rows_out[0], AXES, pairs_of(cross_core))
    rows_in = lax.ppermute(rows_in[0], AXES, [(b, a) for a, b in pairs_of(to_output)])
    up2, down2, grad_flip, act_flip = order(up2, down2, grad_flip, act_flip)
    up3, down3 = shift(up2, "z", 1), shift(down2, "z", -1)

    def products(blocks, alias=(), after=()):
        pieces = [piece for parts in blocks.values() for piece in parts]
        own = [k for k, piece in enumerate(pieces) if piece is act]
        moved = [piece for piece in pieces if piece is not act]

        def kernel(get, small, weight_out, cov_out):
            z, xh = lax.axis_index("z"), lax.axis_index("xh")
            at = 0
            for distance, parts in blocks.items():
                place = lax.rem(z + distance, 8)
                if distance:
                    held = [small[at + k][...] for k in range(len(parts))]
                    at += len(parts)
                else:
                    held = [get(0)[...]]

                def product(right):
                    values = [dot(piece, get(right)[...], (1, 1)) for piece in held]
                    return values[0] if len(values) == 1 else jnp.concatenate(values, axis=0)

                weight_out(place * 2 + xh, product(2))
                weight_out(place * 2 + 1 - xh, product(3))
                cov_out(xh * 8 + place, product(0))
                cov_out((1 - xh) * 8 + place, product(1))

        shapes = [(chunked, 2 * len(blocks), bf16)] * 2
        flops = 4 * len(blocks) * pair_flops
        return call(kernel, [act, act_flip, grad, grad_flip], shapes, after, moved, alias, flops=flops)

    parts = products({0: [act], 1: [down1], 7: [up1], 2: [down2], 6: [up2]})
    up3, down3, rows_out, rows_in, *parts = order(up3, down3, rows_out, rows_in, *parts)
    down4, up4 = shift(down3[:half], "z", -1), shift(up3[half:], "z", 1)
    parts = products({3: [down3], 5: [up3]}, parts)
    weight_parts, in_parts = products({4: [down4, up4]}, parts)

    grad_late, weight_parts = order(grad, weight_parts)
    grad_up1, grad_down1 = shift(grad_late, "z", 1), shift(grad_late, "z", -1)
    eigs = lax.ppermute(
        jnp.concatenate([eig_in, eig_out], axis=0), AXES, [(b, a) for a, b in pairs_of(to_output)]
    )

    def total_of(got):
        total = got[0].astype(f32)
        for k in range(1, count):
            total = total + got[k].astype(f32)
        return unpack(total)

    def wide(value, rows_ref, out, index):
        for k in range(0, count, 4):
            main = dot(value, rows_ref[:, k * 128 : (k + 4) * 128], (1, 0))
            start = count * 128 + k * rest
            others = dot(value, rows_ref[:, start : start + 4 * rest], (1, 0))
            for q in range(4):
                out.parts(index(k + q), main[:, q * 128 : (q + 1) * 128], others[:, q * rest : (q + 1) * rest])

    def stacked(got, whole, block):
        for k in range(count):
            value = unpack(got[k].astype(f32)).astype(bf16)
            j = block(k)
            whole[j * 128 : (j + 1) * 128] = value[:128]
            whole[count * 128 + j * rest : count * 128 + (j + 1) * rest] = value[128:]
        return whole[...]

    got = exchange(weight_parts, DP)
    got, grad_up1, grad_down1, in_parts, eigs = order(got, grad_up1, grad_down1, in_parts, eigs)

    def weight_kernel(get, small, out):
        value = (total_of(get(0)) * (1.0 / total_tokens)).astype(bf16)
        wide(value, get(1), out, lambda k: k % 8 * 2 + k // 8)

    (mixed,) = call(weight_kernel, [got, rows_out], [(chunked, count, bf16)], flops=square_flops)
    got = exchange(mixed, COL)
    got, grad_up1, grad_down1 = order(got, grad_up1, grad_down1)

    def mixed_kernel(get, small, out):
        wide(total_of(get(0)).T.astype(bf16), get(1), out, lambda k: k)

    (eigen,) = call(mixed_kernel, [got, rows_in], [(chunked, count, bf16)], flops=square_flops)
    grad_up2, grad_down2 = shift(grad_up1, "z", 1), shift(grad_down1, "z", -1)
    got = exchange(eigen, ROW)
    got, grad_up2, grad_down2 = order(got, grad_up2, grad_down2)
    grad_cross = shift(grad_up2, "xh", 1)

    def eigen_kernel(get, small, out):
        eigs_ref, column_ref = small
        scale = 1.0 / (column_ref[...] * eigs_ref[0:1, :] + damping)
        out(0, total_of(get(0)) * scale)

    (scaled,) = call(eigen_kernel, [got], [((1,) + packed, 1, bf16)], (), [eigs, eigs[1][:, None]])
    scaled = lax.all_gather(scaled, COL, axis=0, tiled=True)

    def back_kernel(get, small, out, whole):
        value = dot(get(1)[...], stacked(get(0), whole, lambda k: k % 2 * 8 + k // 2), (1, 0))
        out.everywhere(value.T)

    space = [((full, width), bf16)]
    (back,) = call(back_kernel, [scaled, rows_out], [(chunked, 1, bf16)], (), (), (), space, square_flops)
    back = exchange(back, ROW)

    def cov_kernel(get, small, out):
        for cross in range(2):
            for distance in range(8):
                if distance < 5:
                    out(cross * 8 + distance, dot(get(5 if cross else 0)[...], get(distance)[...], (1, 1)))
                else:
                    out(cross * 8 + distance, jnp.zeros(square, f32))

    window = [grad_up2, grad_up1, grad_late, grad_down1, grad_down2, grad_cross]
    (out_parts,) = call(cov_kernel, window, [(chunked, count, bf16)], flops=10 * pair_flops)
    back, out_parts = order(back, out_parts)

    def last_kernel(get, small, out, whole):
        out.put(0, dot(get(1)[...], stacked(get(0), whole, lambda k: k), (1, 0)))

    (precond,) = call(
        last_kernel, [back, rows_in], [((1,) + square, 1, bf16)], (), (), (), space, square_flops
    )
    precond = lax.ppermute(precond, AXES, pairs_of(to_output))

    def unpack_kernel(get, small, out):
        out.put(0, unpack(get(0)[...].astype(f32)))

    new_in = lax.psum_scatter(in_parts.reshape(-1, 128), DP, scatter_dimension=0, tiled=True)
    (new_in,) = call(unpack_kernel, [new_in], [((1,) + square, 1, bf16)])
    new_in = lax.ppermute(new_in, AXES, pairs_of(swapped)).astype(f32)

    def sum_kernel(get, small, out):
        out.put(0, total_of(get(0)))

    (out_cov,) = call(sum_kernel, [exchange(out_parts, DP)], [((1,) + square, 1, bf16)])
    new_out = lax.ppermute(out_cov, AXES, pairs_of(window_place(False))).astype(f32)
    new_out = new_out + lax.ppermute(out_cov, AXES, pairs_of(window_place(True))).astype(f32).transpose(0, 2, 1)

    def factor(old, cov):
        return decay * old + ((1.0 - decay) / total_tokens) * cov

    return factor(factor_in, new_in), factor(factor_out, new_out), precond


def solution(mesh):
    fine = Mesh(mesh.devices.reshape(4, 2, 2, 2, 8), AXES)
    block = P(None, DP, GRAD)
    placed = (block, block, block, block, P(None, DP, None), P(None, GRAD, None), P(None, DP), P(None, GRAD))
    return jax.shard_map(body, mesh=fine, in_specs=placed, out_specs=(block, block, block), check_vma=False)
```

profile of v0, /device:TPU:6, one launch (start us, length us, event | category | flops | bytes accessed | tf_op | source)
XLA Modules:
  0.0 272.7 jit_solution(16253904867518695418)
XLA Ops:
  9.2 4.0 %collective-permute-start.1 = (bf16[160,2048]{1,0:T(8,128)(2,1)}, bf16[160,2048]{1,0:T(8,128)(2,1)S(1)}, u32[]{:S(2)}, u32[]{:S(2)}) collective-permute-start(bf16[160,2048]{1,0:T(8,128)(2,1)} %bitcast.28), channel_id=1, source_target_pairs={{0,7},{1,0},{2,1},{3,2},{4,3},{5,4},{6,5},{7,6},{8,15},{9,8},{10,9... | collective-permute-start | bytes 1966088 | tf_op jit(solution)/shard_map/ppermute | solution.py:114
  14.6 2.1 collective-permute-start.4
  20.2 7.8 %collective-permute-done.refs_5_ = bf16[160,2048]{1,0:T(8,128)(2,1)S(1)} collective-permute-done((bf16[160,2048]{1,0:T(8,128)(2,1)}, bf16[160,2048]{1,0:T(8,128)(2,1)S(1)}, u32[]{:S(2)}, u32[]{:S(2)}) %collective-permute-start) | collective-permute-done | bytes 655392 | tf_op jit(solution)/shard_map/ppermute | solution.py:114
  28.0 3.2 %collective-permute-start.3 = (bf16[160,2048]{1,0:T(8,128)(2,1)S(1)}, bf16[160,2048]{1,0:T(8,128)(2,1)S(1)}, u32[]{:S(2)}, u32[]{:S(2)}) collective-permute-start(bf16[160,2048]{1,0:T(8,128)(2,1)S(1)} %collective-permute-done.1.refs_4_), channel_id=1, source_target_pairs={{0,7},{1,0},{2,1},{3,2},{4,3},{5,4},{6,5},{7,6},{8,15},{9,8},{10,9... | collective-permute-start | bytes 1966088 | tf_op jit(solution)/shard_map/ppermute | solution.py:114
  33.2 6.1 %collective-permute-start.9 = (bf16[160,2560]{1,0:T(8,128)(2,1)S(1)}, bf16[160,2560]{1,0:T(8,128)(2,1)S(1)}, u32[]{:S(2)}, u32[]{:S(2)}) collective-permute-start(bf16[160,2560]{1,0:T(8,128)(2,1)S(1)} %bitcast.35), channel_id=1, source_target_pairs={{0,0},{1,1},{2,2},{3,3},{4,4},{5,5},{6,6},{7,7},{128,8},{129,9},{1... | collective-permute-start | bytes 2457608 | tf_op jit(solution)/shard_map/ppermute | solution.py:194
  39.3 7.3 %collective-permute-done.4.refs_3_ = bf16[160,2048]{1,0:T(8,128)(2,1)S(1)} collective-permute-done((bf16[160,2048]{1,0:T(8,128)(2,1)}, bf16[160,2048]{1,0:T(8,128)(2,1)S(1)}, u32[]{:S(2)}, u32[]{:S(2)}) %collective-permute-start.4) | collective-permute-done | bytes 655392 | tf_op jit(solution)/shard_map/ppermute | solution.py:114
  47.0 2.9 %collective-permute-start.7 = (bf16[160,2048]{1,0:T(8,128)(2,1)S(1)}, bf16[160,2048]{1,0:T(8,128)(2,1)S(1)}, u32[]{:S(2)}, u32[]{:S(2)}) collective-permute-start(bf16[160,2048]{1,0:T(8,128)(2,1)S(1)} %collective-permute-done.3.refs_6_), channel_id=1, source_target_pairs={{0,7},{1,0},{2,1},{3,2},{4,3},{5,4},{6,5},{7,6},{8,15},{9,8},{10,9... | collective-permute-start | bytes 1966088 | tf_op jit(solution)/shard_map/ppermute | solution.py:114
  49.9 6.2 %shard_map.104 = (bf16[16,200,128]{2,1,0:T(8,128)(2,1)}, bf16[16,200,128]{2,1,0:T(8,128)(2,1)}) custom-call(bf16[160,2048]{1,0:T(8,128)(2,1)S(1)} %bitcast.30, bf16[160,2048]{1,0:T(8,128)(2,1)S(1)} %collective-permute-done.5.refs_1_, bf16[160,2048]{1,0:T(8,128)(2,1)S(1)} %bitcast.21, bf16[160,2048]{1,0:T(8,128)(2,1)S(1)} %collective-permute-done.4.refs_3_, ...), custom_call_target="tpu_custom_call" | custom-call | flops 2097152000 | bytes 2621440 | tf_op jit(solution)/shard_map/pallas_call | solution.py:100
  56.1 5.1 %collective-permute-done.8.refs_1_ = bf16[160,2560]{1,0:T(8,128)(2,1)S(1)} collective-permute-done((bf16[160,2560]{1,0:T(8,128)(2,1)S(1)}, bf16[160,2560]{1,0:T(8,128)(2,1)S(1)}, u32[]{:S(2)}, u32[]{:S(2)}) %collective-permute-start.8) | collective-permute-done | bytes 819232 | tf_op jit(solution)/shard_map/ppermute | solution.py:193
  61.2 12.9 %collective-permute-done.9.refs_1_ = bf16[160,2560]{1,0:T(8,128)(2,1)S(1)} collective-permute-done((bf16[160,2560]{1,0:T(8,128)(2,1)S(1)}, bf16[160,2560]{1,0:T(8,128)(2,1)S(1)}, u32[]{:S(2)}, u32[]{:S(2)}) %collective-permute-start.9) | collective-permute-done | bytes 819232 | tf_op jit(solution)/shard_map/ppermute | solution.py:194
  76.5 4.7 %shard_map.105 = (bf16[16,200,128]{2,1,0:T(8,128)(2,1)}, bf16[16,200,128]{2,1,0:T(8,128)(2,1)}) custom-call(bf16[160,2048]{1,0:T(8,128)(2,1)S(1)} %bitcast.31, bf16[160,2048]{1,0:T(8,128)(2,1)S(1)} %collective-permute-done.5.refs_1_, bf16[160,2048]{1,0:T(8,128)(2,1)S(1)} %bitcast.22, ...), custom_call_target="tpu_custom_call", output_to_operand_aliasing={{0}: (6, {}), {1}: (7, {})} | custom-call | flops 838860800 | bytes 2621440 | tf_op jit(solution)/shard_map/pallas_call | solution.py:100
  81.3 3.1 %collective-permute-done.11.refs_5_ = bf16[80,2048]{1,0:T(8,128)(2,1)S(1)} collective-permute-done((bf16[80,2048]{1,0:T(8,128)(2,1)S(1)}, bf16[80,2048]{1,0:T(8,128)(2,1)S(1)}, u32[]{:S(2)}, u32[]{:S(2)}) %collective-permute-start.11) | collective-permute-done | bytes 327712 | tf_op jit(solution)/shard_map/ppermute | solution.py:114
  84.4 4.3 %shard_map.106 = (bf16[16,200,128]{2,1,0:T(8,128)(2,1)}, bf16[16,200,128]{2,1,0:T(8,128)(2,1)}) custom-call(bf16[160,2048]{1,0:T(8,128)(2,1)S(1)} %bitcast.32, bf16[160,2048]{1,0:T(8,128)(2,1)S(1)} %collective-permute-done.5.refs_1_, bf16[160,2048]{1,0:T(8,128)(2,1)S(1)} %bitcast.23, ...), custom_call_target="tpu_custom_call", output_to_operand_aliasing={{0}: (6, {}), {1}: (7, {})} | custom-call | flops 419430400 | bytes 2621440 | tf_op jit(solution)/shard_map/pallas_call | solution.py:100
  88.8 4.0 %all-to-all-start = ((bf16[16,200,128]{2,1,0:T(8,128)(2,1)}), bf16[16,200,128]{2,1,0:T(8,128)(2,1)S(1)}, u32[]{:S(2)}, u32[]{:S(2)}) async-start(bf16[16,200,128]{2,1,0:T(8,128)(2,1)} %get-tuple-element.59), calls=%async_computation | async-start | bytes 1638400 | tf_op jit(solution)/shard_map/all_to_all | solution.py:118
  92.8 3.2 %collective-permute-start.13 = (bf16[160,2048]{1,0:T(8,128)(2,1)S(1)}, bf16[160,2048]{1,0:T(8,128)(2,1)}, u32[]{:S(2)}, u32[]{:S(2)}) collective-permute-start(bf16[160,2048]{1,0:T(8,128)(2,1)S(1)} %bitcast.25), channel_id=1, source_target_pairs={{0,7},{1,0},{2,1},{3,2},{4,3},{5,4},{6,5},{7,6},{8,15},{9,8},{10,9... | collective-permute-start | bytes 1966088 | tf_op jit(solution)/shard_map/ppermute | solution.py:114
  96.1 3.8 %collective-permute-start.14 = (f32[2,160]{1,0:T(2,128)S(1)}, f32[2,160]{1,0:T(2,128)S(1)}, u32[]{:S(2)}, u32[]{:S(2)}) collective-permute-start(f32[2,160]{1,0:T(2,128)S(1)} %pad_maximum_fusion), channel_id=1, source_target_pairs={{0,0},{1,1},{2,2},{3,3},{4,4},{5,5},{6,6},{7,7},{128,8},{129,9},{1... | collective-permute-start | bytes 3848 | tf_op jit(solution)/shard_map/ppermute | solution.py:235
  99.8 4.8 %collective-permute-done.14.refs_1_ = f32[2,160]{1,0:T(2,128)S(1)} collective-permute-done((f32[2,160]{1,0:T(2,128)S(1)}, f32[2,160]{1,0:T(2,128)S(1)}, u32[]{:S(2)}, u32[]{:S(2)}) %collective-permute-start.14) | collective-permute-done | bytes 1312 | tf_op jit(solution)/shard_map/ppermute | solution.py:235
  104.7 6.1 %collective-permute-done.12.refs_1_ = bf16[160,2048]{1,0:T(8,128)(2,1)S(1)} collective-permute-done((bf16[160,2048]{1,0:T(8,128)(2,1)S(1)}, bf16[160,2048]{1,0:T(8,128)(2,1)S(1)}, u32[]{:S(2)}, u32[]{:S(2)}) %collective-permute-start.12) | collective-permute-done | bytes 655392 | tf_op jit(solution)/shard_map/ppermute | solution.py:114
  111.6 3.6 %shard_map.108 = bf16[16,200,128]{2,1,0:T(8,128)(2,1)S(1)} custom-call(bf16[16,200,128]{2,1,0:T(8,128)(2,1)S(1)} %all-to-all-done.refs_0_, bf16[160,2560]{1,0:T(8,128)(2,1)S(1)} %collective-permute-done.8.refs_1_), custom_call_target="tpu_custom_call" | custom-call | flops 131072000 | bytes 1638400 | tf_op jit(solution)/shard_map/pallas_call | solution.py:100
  115.3 27.0 %all_to_all.25.refs_0_ = bf16[16,200,128]{2,1,0:T(8,128)(2,1)S(1)} all-to-all(bf16[16,200,128]{2,1,0:T(8,128)(2,1)S(1)} %shard_map.108), channel_id=1, replica_groups=mesh['y'=4,'xl'=2,'c'=2,'xh'=2,'z'=8] {'z','c'}, dimensions={0} | all-to-all | bytes 1638400 | tf_op jit(solution)/shard_map/all_to_all | solution.py:118
  144.1 7.0 %all-to-all-start.2 = ((bf16[16,200,128]{2,1,0:T(8,128)(2,1)}), bf16[16,200,128]{2,1,0:T(8,128)(2,1)S(1)}, u32[]{:S(2)}, u32[]{:S(2)}) async-start(bf16[16,200,128]{2,1,0:T(8,128)(2,1)} %shard_map.109), calls=%async_computation.2 | async-start | bytes 1638400 | tf_op jit(solution)/shard_map/all_to_all | solution.py:118
  151.6 2.8 %collective-permute-start.17 = (bf16[160,2048]{1,0:T(8,128)(2,1)}, bf16[160,2048]{1,0:T(8,128)(2,1)}, u32[]{:S(2)}, u32[]{:S(2)}) collective-permute-start(bf16[160,2048]{1,0:T(8,128)(2,1)} %collective-permute-done.13.refs_3_), channel_id=1, source_target_pairs={{0,7},{1,0},{2,1},{3,2},{4,3},{5,4},{6,5},{7,6},{8,15},{9,8},{10,9... | collective-permute-start | bytes 1966088 | tf_op jit(solution)/shard_map/ppermute | solution.py:114
  154.6 15.2 %collective-permute-done.16.refs_0_ = bf16[160,2048]{1,0:T(8,128)(2,1)} collective-permute-done((bf16[160,2048]{1,0:T(8,128)(2,1)}, bf16[160,2048]{1,0:T(8,128)(2,1)}, u32[]{:S(2)}, u32[]{:S(2)}) %collective-permute-start.16) | collective-permute-done | bytes 655392 | tf_op jit(solution)/shard_map/ppermute | solution.py:114
  170.4 19.3 %all_gather.3.refs_0_ = bf16[16,200,128]{2,1,0:T(8,128)(2,1)S(1)} all-gather(bf16[1,200,128]{2,1,0:T(8,128)(2,1)S(1)} %shard_map.110), channel_id=1, replica_groups=mesh['y'=4,'xl'=2,'c'=2,'xh'=2,'z'=8] {'z','c'}, dimensions={0}, use_global_device_ids=true | all-gather | bytes 870400 | tf_op jit(solution)/shard_map/all_gather | solution.py:287
  191.7 7.4 %all-to-all-start.3 = ((bf16[16,200,128]{2,1,0:T(8,128)(2,1)}), bf16[16,200,128]{2,1,0:T(8,128)(2,1)S(1)}, u32[]{:S(2)}, u32[]{:S(2)}) async-start(bf16[16,200,128]{2,1,0:T(8,128)(2,1)} %shard_map.111), calls=%async_computation.3 | async-start | bytes 1638400 | tf_op jit(solution)/shard_map/all_to_all | solution.py:118
  200.6 25.7 %collective-permute-done.18.refs_5_ = bf16[160,2048]{1,0:T(8,128)(2,1)S(1)} collective-permute-done((bf16[160,2048]{1,0:T(8,128)(2,1)}, bf16[160,2048]{1,0:T(8,128)(2,1)S(1)}, u32[]{:S(2)}, u32[]{:S(2)}) %collective-permute-start.18) | collective-permute-done | bytes 655392 | tf_op jit(solution)/shard_map/ppermute | solution.py:114
  226.2 6.2 %shard_map.112 = bf16[16,200,128]{2,1,0:T(8,128)(2,1)} custom-call(bf16[160,2048]{1,0:T(8,128)(2,1)} %collective-permute-done.16.refs_0_, bf16[160,2048]{1,0:T(8,128)(2,1)S(1)} %copy-done.5, bf16[160,2048]{1,0:T(8,128)(2,1)S(1)} %bitcast.26, bf16[160,2048]{1,0:T(8,128)(2,1)} %collective-permute-done.13.refs_3_, ...), custom_call_target="tpu_custom_call" | custom-call | flops 1048576000 | bytes 3932160 | tf_op jit(solution)/shard_map/pallas_call | solution.py:100
  232.4 5.6 %all-to-all-start.4 = ((bf16[16,200,128]{2,1,0:T(8,128)(2,1)}), bf16[16,200,128]{2,1,0:T(8,128)(2,1)S(1)}, u32[]{:S(2)}, u32[]{:S(2)}) async-start(bf16[16,200,128]{2,1,0:T(8,128)(2,1)} %shard_map.112), calls=%async_computation.4 | async-start | bytes 1638400 | tf_op jit(solution)/shard_map/all_to_all | solution.py:118
  239.2 6.8 %collective-permute-start.15 = (bf16[1,160,160]{1,2,0:T(8,128)(2,1)S(1)}, bf16[1,160,160]{1,2,0:T(8,128)(2,1)S(1)}, u32[]{:S(2)}, u32[]{:S(2)}) collective-permute-start(bf16[1,160,160]{1,2,0:T(8,128)(2,1)S(1)} %copy.29), channel_id=1, source_target_pairs={{0,0},{1,1},{2,2},{3,3},{4,4},{5,5},{6,6},{7,7},{8,128},{9,129},{1... | collective-permute-start | bytes 153608 | tf_op jit(solution)/shard_map/ppermute | solution.py:322
  247.1 2.1 collective-permute-start.21
  251.4 4.2 %collective-permute-start.20 = (bf16[1,160,160]{2,1,0:T(8,128)(2,1)S(1)}, bf16[1,160,160]{2,1,0:T(8,128)(2,1)S(1)}, u32[]{:S(2)}, u32[]{:S(2)}) collective-permute-start(bf16[1,160,160]{2,1,0:T(8,128)(2,1)S(1)} %shard_map.113), channel_id=1, source_target_pairs={{16,118},{17,7},{18,16},{19,33},{20,50},{21,67},{22,84},{23,101},{... | collective-permute-start | bytes 153608 | tf_op jit(solution)/shard_map/ppermute | solution.py:329
  259.4 5.0 %collective-permute-done.20 = bf16[1,160,160]{2,1,0:T(8,128)(2,1)S(1)} collective-permute-done((bf16[1,160,160]{2,1,0:T(8,128)(2,1)S(1)}, bf16[1,160,160]{2,1,0:T(8,128)(2,1)S(1)}, u32[]{:S(2)}, u32[]{:S(2)}) %collective-permute-start.20) | collective-permute-done | bytes 51232 | tf_op jit(solution)/shard_map/ppermute | solution.py:329
  (73 shorter events, 28.6 us)
Async XLA Ops:
  7.2 20.9 %collective-permute-start = (bf16[160,2048]{1,0:T(8,128)(2,1)}, bf16[160,2048]{1,0:T(8,128)(2,1)S(1)}, u32[]{:S(2)}, u32[]{:S(2)}) collective-permute-start(bf16[160,2048]{1,0:T(8,128)(2,1)} %bitcast.27), channel_id=1, source_target_pairs={{0,1},{1,2},{2,3},{3,4},{4,5},{5,6},{6,7},{7,0},{8,9},{9,10},{10,1... | collective-permute-start | bytes 1966088 | tf_op jit(solution)/shard_map/ppermute | solution.py:114
  9.2 18.9 %collective-permute-start.1 = (bf16[160,2048]{1,0:T(8,128)(2,1)}, bf16[160,2048]{1,0:T(8,128)(2,1)S(1)}, u32[]{:S(2)}, u32[]{:S(2)}) collective-permute-start(bf16[160,2048]{1,0:T(8,128)(2,1)} %bitcast.28), channel_id=1, source_target_pairs={{0,7},{1,0},{2,1},{3,2},{4,3},{5,4},{6,5},{7,6},{8,15},{9,8},{10,9... | collective-permute-start | bytes 1966088 | tf_op jit(solution)/shard_map/ppermute | solution.py:114
  13.2 20.0 %collective-permute-start.5 = (bf16[160,2048]{1,0:T(8,128)(2,1)}, bf16[160,2048]{1,0:T(8,128)(2,1)S(1)}, u32[]{:S(2)}, u32[]{:S(2)}) collective-permute-start(bf16[160,2048]{1,0:T(8,128)(2,1)} %bitcast.29), channel_id=1, source_target_pairs={{0,8},{8,0},{1,9},{9,1},{2,10},{10,2},{3,11},{11,3},{4,12},{12,4},... | collective-permute-start | bytes 1966088 | tf_op jit(solution)/shard_map/ppermute | solution.py:114
  14.6 32.0 %collective-permute-start.4 = (bf16[160,2048]{1,0:T(8,128)(2,1)}, bf16[160,2048]{1,0:T(8,128)(2,1)S(1)}, u32[]{:S(2)}, u32[]{:S(2)}) collective-permute-start(bf16[160,2048]{1,0:T(8,128)(2,1)} %bitcast.20), channel_id=1, source_target_pairs={{0,8},{8,0},{1,9},{9,1},{2,10},{10,2},{3,11},{11,3},{4,12},{12,4},... | collective-permute-start | bytes 1966088 | tf_op jit(solution)/shard_map/ppermute | solution.py:114
  19.0 30.8 %copy-start = (bf16[1,2048,160]{1,2,0:T(8,128)(2,1)S(1)}, bf16[1,2048,160]{1,2,0:T(8,128)(2,1)}, u32[]{:S(2)}) copy-start(bf16[1,2048,160]{1,2,0:T(8,128)(2,1)} %param.9) | copy-start | bytes 1966084
  19.0 30.8 %copy-start.1 = (bf16[1,2048,160]{1,2,0:T(8,128)(2,1)S(1)}, bf16[1,2048,160]{1,2,0:T(8,128)(2,1)}, u32[]{:S(2)}) copy-start(bf16[1,2048,160]{1,2,0:T(8,128)(2,1)} %param.8) | copy-start | bytes 1966084
  28.0 18.6 %collective-permute-start.2 = (bf16[160,2048]{1,0:T(8,128)(2,1)S(1)}, bf16[160,2048]{1,0:T(8,128)(2,1)S(1)}, u32[]{:S(2)}, u32[]{:S(2)}) collective-permute-start(bf16[160,2048]{1,0:T(8,128)(2,1)S(1)} %collective-permute-done.refs_5_), channel_id=1, source_target_pairs={{0,1},{1,2},{2,3},{3,4},{4,5},{5,6},{6,7},{7,0},{8,9},{9,10},{10,1... | collective-permute-start | bytes 1966088 | tf_op jit(solution)/shard_map/ppermute | solution.py:114
  28.0 18.6 %collective-permute-start.3 = (bf16[160,2048]{1,0:T(8,128)(2,1)S(1)}, bf16[160,2048]{1,0:T(8,128)(2,1)S(1)}, u32[]{:S(2)}, u32[]{:S(2)}) collective-permute-start(bf16[160,2048]{1,0:T(8,128)(2,1)S(1)} %collective-permute-done.1.refs_4_), channel_id=1, source_target_pairs={{0,7},{1,0},{2,1},{3,2},{4,3},{5,4},{6,5},{7,6},{8,15},{9,8},{10,9... | collective-permute-start | bytes 1966088 | tf_op jit(solution)/shard_map/ppermute | solution.py:114
  31.3 29.9 %collective-permute-start.8 = (bf16[160,2560]{1,0:T(8,128)(2,1)S(1)}, bf16[160,2560]{1,0:T(8,128)(2,1)S(1)}, u32[]{:S(2)}, u32[]{:S(2)}) collective-permute-start(bf16[160,2560]{1,0:T(8,128)(2,1)S(1)} %bitcast.36), channel_id=1, source_target_pairs={{0,0},{1,1},{2,2},{3,3},{4,4},{5,5},{6,6},{7,7},{8,16},{9,17},{10,... | collective-permute-start | bytes 2457608 | tf_op jit(solution)/shard_map/ppermute | solution.py:193
  33.2 40.9 %collective-permute-start.9 = (bf16[160,2560]{1,0:T(8,128)(2,1)S(1)}, bf16[160,2560]{1,0:T(8,128)(2,1)S(1)}, u32[]{:S(2)}, u32[]{:S(2)}) collective-permute-start(bf16[160,2560]{1,0:T(8,128)(2,1)S(1)} %bitcast.35), channel_id=1, source_target_pairs={{0,0},{1,1},{2,2},{3,3},{4,4},{5,5},{6,6},{7,7},{128,8},{129,9},{1... | collective-permute-start | bytes 2457608 | tf_op jit(solution)/shard_map/ppermute | solution.py:194
  46.6 27.5 %collective-permute-start.6 = (bf16[160,2048]{1,0:T(8,128)(2,1)S(1)}, bf16[160,2048]{1,0:T(8,128)(2,1)S(1)}, u32[]{:S(2)}, u32[]{:S(2)}) collective-permute-start(bf16[160,2048]{1,0:T(8,128)(2,1)S(1)} %collective-permute-done.2.refs_7_), channel_id=1, source_target_pairs={{0,1},{1,2},{2,3},{3,4},{4,5},{5,6},{6,7},{7,0},{8,9},{9,10},{10,1... | collective-permute-start | bytes 1966088 | tf_op jit(solution)/shard_map/ppermute | solution.py:114
  47.0 27.1 %collective-permute-start.7 = (bf16[160,2048]{1,0:T(8,128)(2,1)S(1)}, bf16[160,2048]{1,0:T(8,128)(2,1)S(1)}, u32[]{:S(2)}, u32[]{:S(2)}) collective-permute-start(bf16[160,2048]{1,0:T(8,128)(2,1)S(1)} %collective-permute-done.3.refs_6_), channel_id=1, source_target_pairs={{0,7},{1,0},{2,1},{3,2},{4,3},{5,4},{6,5},{7,6},{8,15},{9,8},{10,9... | collective-permute-start | bytes 1966088 | tf_op jit(solution)/shard_map/ppermute | solution.py:114
  74.1 7.2 %collective-permute-start.10 = (bf16[80,2048]{1,0:T(8,128)(2,1)S(1)}, bf16[80,2048]{1,0:T(8,128)(2,1)S(1)}, u32[]{:S(2)}, u32[]{:S(2)}) collective-permute-start(bf16[80,2048]{1,0:T(8,128)(2,1)S(1)} %slice.9), channel_id=1, source_target_pairs={{0,7},{1,0},{2,1},{3,2},{4,3},{5,4},{6,5},{7,6},{8,15},{9,8},{10,9... | collective-permute-start | bytes 983048 | tf_op jit(solution)/shard_map/ppermute | solution.py:114
  75.9 8.5 %collective-permute-start.11 = (bf16[80,2048]{1,0:T(8,128)(2,1)S(1)}, bf16[80,2048]{1,0:T(8,128)(2,1)S(1)}, u32[]{:S(2)}, u32[]{:S(2)}) collective-permute-start(bf16[80,2048]{1,0:T(8,128)(2,1)S(1)} %slice.10), channel_id=1, source_target_pairs={{0,1},{1,2},{2,3},{3,4},{4,5},{5,6},{6,7},{7,0},{8,9},{9,10},{10,1... | collective-permute-start | bytes 983048 | tf_op jit(solution)/shard_map/ppermute | solution.py:114
  88.7 7.3 %copy-start.9 = (f32[1,160]{1,0:T(1,128)S(1)}, f32[1,160]{1,0:T(1,128)}, u32[]{:S(2)}) copy-start(f32[1,160]{1,0:T(1,128)} %param.15) | copy-start | bytes 1924
  88.8 7.3 %copy-start.10 = (f32[1,160]{1,0:T(1,128)S(1)}, f32[1,160]{1,0:T(1,128)}, u32[]{:S(2)}) copy-start(f32[1,160]{1,0:T(1,128)} %param.14) | copy-start | bytes 1924
  88.8 22.9 %all-to-all-start = ((bf16[16,200,128]{2,1,0:T(8,128)(2,1)}), bf16[16,200,128]{2,1,0:T(8,128)(2,1)S(1)}, u32[]{:S(2)}, u32[]{:S(2)}) async-start(bf16[16,200,128]{2,1,0:T(8,128)(2,1)} %get-tuple-element.59), calls=%async_computation | async-start | bytes 1638400 | tf_op jit(solution)/shard_map/all_to_all | solution.py:118
  92.8 18.0 %collective-permute-start.12 = (bf16[160,2048]{1,0:T(8,128)(2,1)S(1)}, bf16[160,2048]{1,0:T(8,128)(2,1)S(1)}, u32[]{:S(2)}, u32[]{:S(2)}) collective-permute-start(bf16[160,2048]{1,0:T(8,128)(2,1)S(1)} %bitcast.24), channel_id=1, source_target_pairs={{0,1},{1,2},{2,3},{3,4},{4,5},{5,6},{6,7},{7,0},{8,9},{9,10},{10,1... | collective-permute-start | bytes 1966088 | tf_op jit(solution)/shard_map/ppermute | solution.py:114
  92.8 18.8 %collective-permute-start.13 = (bf16[160,2048]{1,0:T(8,128)(2,1)S(1)}, bf16[160,2048]{1,0:T(8,128)(2,1)}, u32[]{:S(2)}, u32[]{:S(2)}) collective-permute-start(bf16[160,2048]{1,0:T(8,128)(2,1)S(1)} %bitcast.25), channel_id=1, source_target_pairs={{0,7},{1,0},{2,1},{3,2},{4,3},{5,4},{6,5},{7,6},{8,15},{9,8},{10,9... | collective-permute-start | bytes 1966088 | tf_op jit(solution)/shard_map/ppermute | solution.py:114
  96.1 8.6 %collective-permute-start.14 = (f32[2,160]{1,0:T(2,128)S(1)}, f32[2,160]{1,0:T(2,128)S(1)}, u32[]{:S(2)}, u32[]{:S(2)}) collective-permute-start(f32[2,160]{1,0:T(2,128)S(1)} %pad_maximum_fusion), channel_id=1, source_target_pairs={{0,0},{1,1},{2,2},{3,3},{4,4},{5,5},{6,6},{7,7},{128,8},{129,9},{1... | collective-permute-start | bytes 3848 | tf_op jit(solution)/shard_map/ppermute | solution.py:235
  144.1 25.7 %all-to-all-start.2 = ((bf16[16,200,128]{2,1,0:T(8,128)(2,1)}), bf16[16,200,128]{2,1,0:T(8,128)(2,1)S(1)}, u32[]{:S(2)}, u32[]{:S(2)}) async-start(bf16[16,200,128]{2,1,0:T(8,128)(2,1)} %shard_map.109), calls=%async_computation.2 | async-start | bytes 1638400 | tf_op jit(solution)/shard_map/all_to_all | solution.py:118
  151.1 87.0 %reduce-scatter.5.cloned.1.call-start = ((), (), s32[]{:S(2)}) async-start(), calls=%async_computation.6 | async-start | bytes 870400
  151.1 18.7 %collective-permute-start.16 = (bf16[160,2048]{1,0:T(8,128)(2,1)}, bf16[160,2048]{1,0:T(8,128)(2,1)}, u32[]{:S(2)}, u32[]{:S(2)}) collective-permute-start(bf16[160,2048]{1,0:T(8,128)(2,1)} %copy-done.4), channel_id=1, source_target_pairs={{0,1},{1,2},{2,3},{3,4},{4,5},{5,6},{6,7},{7,0},{8,9},{9,10},{10,1... | collective-permute-start | bytes 1966088 | tf_op jit(solution)/shard_map/ppermute | solution.py:114
  151.6 18.2 %collective-permute-start.17 = (bf16[160,2048]{1,0:T(8,128)(2,1)}, bf16[160,2048]{1,0:T(8,128)(2,1)}, u32[]{:S(2)}, u32[]{:S(2)}) collective-permute-start(bf16[160,2048]{1,0:T(8,128)(2,1)} %collective-permute-done.13.refs_3_), channel_id=1, source_target_pairs={{0,7},{1,0},{2,1},{3,2},{4,3},{5,4},{6,5},{7,6},{8,15},{9,8},{10,9... | collective-permute-start | bytes 1966088 | tf_op jit(solution)/shard_map/ppermute | solution.py:114
  191.7 34.5 %copy-start.5 = (bf16[160,2048]{1,0:T(8,128)(2,1)S(1)}, bf16[160,2048]{1,0:T(8,128)(2,1)}, u32[]{:S(2)}) copy-start(bf16[160,2048]{1,0:T(8,128)(2,1)} %copy-done.4) | copy-start | bytes 1966084
  191.7 40.7 %all-to-all-start.3 = ((bf16[16,200,128]{2,1,0:T(8,128)(2,1)}), bf16[16,200,128]{2,1,0:T(8,128)(2,1)S(1)}, u32[]{:S(2)}, u32[]{:S(2)}) async-start(bf16[16,200,128]{2,1,0:T(8,128)(2,1)} %shard_map.111), calls=%async_computation.3 | async-start | bytes 1638400 | tf_op jit(solution)/shard_map/all_to_all | solution.py:118
  199.1 27.1 %collective-permute-start.18 = (bf16[160,2048]{1,0:T(8,128)(2,1)}, bf16[160,2048]{1,0:T(8,128)(2,1)S(1)}, u32[]{:S(2)}, u32[]{:S(2)}) collective-permute-start(bf16[160,2048]{1,0:T(8,128)(2,1)} %collective-permute-done.16.refs_0_), channel_id=1, source_target_pairs={{0,8},{8,0},{1,9},{9,1},{2,10},{10,2},{3,11},{11,3},{4,12},{12,4},... | collective-permute-start | bytes 1966088 | tf_op jit(solution)/shard_map/ppermute | solution.py:114
  232.4 18.5 %all-to-all-start.4 = ((bf16[16,200,128]{2,1,0:T(8,128)(2,1)}), bf16[16,200,128]{2,1,0:T(8,128)(2,1)S(1)}, u32[]{:S(2)}, u32[]{:S(2)}) async-start(bf16[16,200,128]{2,1,0:T(8,128)(2,1)} %shard_map.112), calls=%async_computation.4 | async-start | bytes 1638400 | tf_op jit(solution)/shard_map/all_to_all | solution.py:118
  239.2 17.6 %collective-permute-start.15 = (bf16[1,160,160]{1,2,0:T(8,128)(2,1)S(1)}, bf16[1,160,160]{1,2,0:T(8,128)(2,1)S(1)}, u32[]{:S(2)}, u32[]{:S(2)}) collective-permute-start(bf16[1,160,160]{1,2,0:T(8,128)(2,1)S(1)} %copy.29), channel_id=1, source_target_pairs={{0,0},{1,1},{2,2},{3,3},{4,4},{5,5},{6,6},{7,7},{8,128},{9,129},{1... | collective-permute-start | bytes 153608 | tf_op jit(solution)/shard_map/ppermute | solution.py:322
  247.1 10.6 %collective-permute-start.21 = (bf16[1,160,160]{2,1,0:T(8,128)(2,1)S(1)}, bf16[1,160,160]{2,1,0:T(8,128)(2,1)S(1)}, u32[]{:S(2)}, u32[]{:S(2)}) collective-permute-start(bf16[1,160,160]{2,1,0:T(8,128)(2,1)S(1)} %shard_map.114), channel_id=1, source_target_pairs={{0,0},{1,1},{2,2},{3,3},{4,4},{5,5},{6,6},{7,7},{8,128},{9,129},{1... | collective-permute-start | bytes 153608 | tf_op jit(solution)/shard_map/ppermute | solution.py:315
  251.4 13.0 %collective-permute-start.20 = (bf16[1,160,160]{2,1,0:T(8,128)(2,1)S(1)}, bf16[1,160,160]{2,1,0:T(8,128)(2,1)S(1)}, u32[]{:S(2)}, u32[]{:S(2)}) collective-permute-start(bf16[1,160,160]{2,1,0:T(8,128)(2,1)S(1)} %shard_map.113), channel_id=1, source_target_pairs={{16,118},{17,7},{18,16},{19,33},{20,50},{21,67},{22,84},{23,101},{... | collective-permute-start | bytes 153608 | tf_op jit(solution)/shard_map/ppermute | solution.py:329
  255.5 3.8 %collective-permute-start.19 = (bf16[1,160,160]{1,2,0:T(8,128)(2,1)S(1)}, bf16[1,160,160]{1,2,0:T(8,128)(2,1)S(1)}, u32[]{:S(2)}, u32[]{:S(2)}) collective-permute-start(bf16[1,160,160]{1,2,0:T(8,128)(2,1)S(1)} %copy.32), channel_id=1, source_target_pairs={{0,102},{1,119},{2,0},{3,17},{4,34},{5,51},{6,68},{7,85},{8,238},{... | collective-permute-start | bytes 153608 | tf_op jit(solution)/shard_map/ppermute | solution.py:328
  (6 other events, 18.0 us)
Sparse Core Ops, SparseCore 0:
  154.7 59.8 reduce-scatter.4
where the time goes:
time: 275 us; the launch traced here: 273 us
  waiting for transfers between devices  96.6 us (35%)
  starting transfers between devices  76.6 us (28%)
  blocking collectives  46.3 us (17%)
  Pallas kernels  32.1 us (12%)
  between operations  14.4 us (5%)
  local copies, waits for them, and re-layouts  6.7 us (2%)
    ppermute x15, waiting for transfers between devices, shift(): lax.ppermute(value, axis, [(i, (i + step) % size) for i in range(size)])  65.3 us
    pallas_call x12, Pallas kernels, call(): pl.pallas_call(wrapped, out_shape=[jax.ShapeDtypeStruct(shape, dtype) for...  32.1 us
    all_to_all x1, blocking collectives, exchange(): return lax.all_to_all(chunks, axes, 0, 0, tiled=True)  27 us
    ppermute x15, starting transfers between devices, shift(): lax.ppermute(value, axis, [(i, (i + step) % size) for i in range(size)])  26.4 us
    all_to_all x4, starting transfers between devices, exchange(): return lax.all_to_all(chunks, axes, 0, 0, tiled=True)  24 us
    all_gather x1, blocking collectives, body(): scaled = lax.all_gather(scaled, COL, axis=0, tiled=True)  19.3 us
    ppermute x1, waiting for transfers between devices, body(): lax.ppermute(rows_in[0], AXES, [(b, a) for a, b in pairs_of(to_output)])  12.9 us
    ppermute x1, starting transfers between devices, body(): new_in = lax.ppermute(new_in, AXES, pairs_of(swapped)).astype(f32)  6.76 us
  transfers between devices with their start and end apart: 27, of which 12 were waited for; matrix products, arithmetic and copies ran while one was open for 0% of the time, Pallas kernels for 8%

commit v1 on v0

--- a/solution.py
+++ b/solution.py
@@ -93,7 +93,7 @@
                 copy.wait()
 
     hbm, vmem = pl.BlockSpec(memory_space=pltpu.HBM), pl.BlockSpec(memory_space=pltpu.VMEM)
-    space = [pltpu.VMEM(x.shape, x.dtype) for x in ins] + [pltpu.SemaphoreType.DMA((n,))]
+    space = [pltpu.VMEM(x.shape, x.dtype) for x in ins] + [pltpu.SemaphoreType.DMA((max(n, 1),))]
     for shape, slots, dtype in outs:
         space += [pltpu.VMEM((slots,) + shape[1:], dtype), pltpu.SemaphoreType.DMA((max(slots, shape[0]),))]
     size = sum(x.size * x.dtype.itemsize for x in ins)
@@ -195,50 +195,62 @@
     up2, down2, grad_flip, act_flip = order(up2, down2, grad_flip, act_flip)
     up3, down3 = shift(up2, "z", 1), shift(down2, "z", -1)
 
-    def products(blocks, alias=(), after=()):
+    def products(blocks, alias=()):
         pieces = [piece for parts in blocks.values() for piece in parts]
-        own = [k for k, piece in enumerate(pieces) if piece is act]
-        moved = [piece for piece in pieces if piece is not act]
 
         def kernel(get, small, weight_out, cov_out):
             z, xh = lax.axis_index("z"), lax.axis_index("xh")
-            at = 0
+            y, xl, c = lax.axis_index("y"), lax.axis_index("xl"), lax.axis_index("c")
+            at = 4
+
+            def staged(other, place):
+                to_y, to_xl, to_c = other * 2 + place // 4, lax.rem(place // 2, 2), lax.rem(place, 2)
+                return lax.rem(to_c + c, 2) * 8 + lax.rem(to_xl + xl, 2) * 4 + lax.rem(to_y - y + 4, 4)
+
             for distance, parts in blocks.items():
                 place = lax.rem(z + distance, 8)
-                if distance:
-                    held = [small[at + k][...] for k in range(len(parts))]
-                    at += len(parts)
-                else:
-                    held = [get(0)[...]]
+                held = [small[at + k][...] for k in range(len(parts))]
+                at += len(parts)
 
                 def product(right):
-                    values = [dot(piece, get(right)[...], (1, 1)) for piece in held]
+                    values = [dot(piece, small[right][...], (1, 1)) for piece in held]
                     return values[0] if len(values) == 1 else jnp.concatenate(values, axis=0)
 
                 weight_out(place * 2 + xh, product(2))
                 weight_out(place * 2 + 1 - xh, product(3))
-                cov_out(xh * 8 + place, product(0))
-                cov_out((1 - xh) * 8 + place, product(1))
+                cov_out(staged(xh, place), product(0))
+                cov_out(staged(1 - xh, place), product(1))
 
         shapes = [(chunked, 2 * len(blocks), bf16)] * 2
         flops = 4 * len(blocks) * pair_flops
-        return call(kernel, [act, act_flip, grad, grad_flip], shapes, after, moved, alias, flops=flops)
+        return call(kernel, [], shapes, (), [act, act_flip, grad, grad_flip, *pieces], alias, flops=flops)
 
     parts = products({0: [act], 1: [down1], 7: [up1], 2: [down2], 6: [up2]})
-    up3, down3, rows_out, rows_in, *parts = order(up3, down3, rows_out, rows_in, *parts)
+    up3, down3, *parts = order(up3, down3, *parts)
     down4, up4 = shift(down3[:half], "z", -1), shift(up3[half:], "z", 1)
     parts = products({3: [down3], 5: [up3]}, parts)
+    grad_late, *parts = order(grad, *parts)
     weight_parts, in_parts = products({4: [down4, up4]}, parts)
 
-    grad_late, weight_parts = order(grad, weight_parts)
     grad_up1, grad_down1 = shift(grad_late, "z", 1), shift(grad_late, "z", -1)
     eigs = lax.ppermute(
         jnp.concatenate([eig_in, eig_out], axis=0), AXES, [(b, a) for a, b in pairs_of(to_output)]
     )
 
+    def pair_sum(chunks, axis):
+        half = chunks.shape[0] // 2
+        other = shift(chunks[half:], axis, 1)
+
+        def kernel(get, small, out):
+            for k in range(half):
+                out.put(k, get(0)[k].astype(f32) + get(1)[k].astype(f32))
+
+        (total,) = call(kernel, [chunks[:half], other], [((half,) + packed, half, bf16)])
+        return total
+
     def total_of(got):
         total = got[0].astype(f32)
-        for k in range(1, count):
+        for k in range(1, got.shape[0]):
             total = total + got[k].astype(f32)
         return unpack(total)
 
@@ -251,23 +263,27 @@
                 out.parts(index(k + q), main[:, q * 128 : (q + 1) * 128], others[:, q * rest : (q + 1) * rest])
 
     def stacked(got, whole, block):
-        for k in range(count):
+        for k in range(got.shape[0]):
             value = unpack(got[k].astype(f32)).astype(bf16)
             j = block(k)
-            whole[j * 128 : (j + 1) * 128] = value[:128]
-            whole[count * 128 + j * rest : count * 128 + (j + 1) * rest] = value[128:]
-        return whole[...]
+            whole[pl.ds(pl.multiple_of(j * 128, 128), 128)] = value[:128]
+            whole[pl.ds(pl.multiple_of(count * 128 + j * rest, rest), rest)] = value[128:]
 
     got = exchange(weight_parts, DP)
-    got, grad_up1, grad_down1, in_parts, eigs = order(got, grad_up1, grad_down1, in_parts, eigs)
+    in_sum = pair_sum(in_parts, "c")
+    got, eigs, rows_out, rows_in, grad_up1, grad_down1, in_sum = order(
+        got, eigs, rows_out, rows_in, grad_up1, grad_down1, in_sum
+    )
 
     def weight_kernel(get, small, out):
         value = (total_of(get(0)) * (1.0 / total_tokens)).astype(bf16)
-        wide(value, get(1), out, lambda k: k % 8 * 2 + k // 8)
+        c = lax.axis_index("c")
+        wide(value, get(1), out, lambda k: lax.rem(k // 8 + c, 2) * 8 + k % 8)
 
     (mixed,) = call(weight_kernel, [got, rows_out], [(chunked, count, bf16)], flops=square_flops)
-    got = exchange(mixed, COL)
-    got, grad_up1, grad_down1 = order(got, grad_up1, grad_down1)
+    got = exchange(pair_sum(mixed, "c"), "z")
+    in_sum = pair_sum(in_sum, "xl")
+    got, in_sum = order(got, in_sum)
 
     def mixed_kernel(get, small, out):
         wide(total_of(get(0)).T.astype(bf16), get(1), out, lambda k: k)
@@ -275,63 +291,77 @@
     (eigen,) = call(mixed_kernel, [got, rows_in], [(chunked, count, bf16)], flops=square_flops)
     grad_up2, grad_down2 = shift(grad_up1, "z", 1), shift(grad_down1, "z", -1)
     got = exchange(eigen, ROW)
-    got, grad_up2, grad_down2 = order(got, grad_up2, grad_down2)
-    grad_cross = shift(grad_up2, "xh", 1)
-
     def eigen_kernel(get, small, out):
         eigs_ref, column_ref = small
         scale = 1.0 / (column_ref[...] * eigs_ref[0:1, :] + damping)
-        out(0, total_of(get(0)) * scale)
-
-    (scaled,) = call(eigen_kernel, [got], [((1,) + packed, 1, bf16)], (), [eigs, eigs[1][:, None]])
-    scaled = lax.all_gather(scaled, COL, axis=0, tiled=True)
+        out.everywhere(total_of(get(0)) * scale)
+
+    (scaled,) = call(eigen_kernel, [got], [((count // 2,) + packed, 1, bf16)], (), [eigs, eigs[1][:, None]])
+    scaled, grad_up2, grad_down2 = order(scaled, grad_up2, grad_down2)
+    grad_cross = shift(grad_up2, "xh", 1)
+    scaled = exchange(scaled, "z")
+    in_got = [in_sum[0]] + [shift(in_sum[k], "y", k) for k in range(1, 4)]
+    scaled, grad_cross, *in_got = order(scaled, grad_cross, *in_got)
+    scaled_other = shift(scaled, "c", 1)
 
     def back_kernel(get, small, out, whole):
-        value = dot(get(1)[...], stacked(get(0), whole, lambda k: k % 2 * 8 + k // 2), (1, 0))
-        out.everywhere(value.T)
+        c = lax.axis_index("c")
+        stacked(get(0), whole, lambda k: c * 8 + k)
+        stacked(get(1), whole, lambda k: (1 - c) * 8 + k)
+        out.everywhere(dot(get(2)[...], whole[...], (1, 0)).T)
 
     space = [((full, width), bf16)]
-    (back,) = call(back_kernel, [scaled, rows_out], [(chunked, 1, bf16)], (), (), (), space, square_flops)
+    (back,) = call(back_kernel, [scaled, scaled_other, rows_out], [(chunked, 1, bf16)], (), (), (), space, square_flops)
     back = exchange(back, ROW)
 
     def cov_kernel(get, small, out):
+        c = lax.axis_index("c")
         for cross in range(2):
             for distance in range(8):
+                index = lax.rem(distance + c, 2) * 8 + cross * 4 + distance // 2
                 if distance < 5:
-                    out(cross * 8 + distance, dot(get(5 if cross else 0)[...], get(distance)[...], (1, 1)))
+                    out(index, dot(get(5 if cross else 0)[...], get(distance)[...], (1, 1)))
                 else:
-                    out(cross * 8 + distance, jnp.zeros(square, f32))
+                    out(index, jnp.zeros(square, f32))
 
     window = [grad_up2, grad_up1, grad_late, grad_down1, grad_down2, grad_cross]
     (out_parts,) = call(cov_kernel, window, [(chunked, count, bf16)], flops=10 * pair_flops)
+    out_parts = pair_sum(out_parts, "c")
     back, out_parts = order(back, out_parts)
 
     def last_kernel(get, small, out, whole):
-        out.put(0, dot(get(1)[...], stacked(get(0), whole, lambda k: k), (1, 0)))
+        stacked(get(0), whole, lambda k: jnp.int32(k))
+        out.put(0, dot(get(1)[...], whole[...], (1, 0)))
 
     (precond,) = call(
         last_kernel, [back, rows_in], [((1,) + square, 1, bf16)], (), (), (), space, square_flops
     )
     precond = lax.ppermute(precond, AXES, pairs_of(to_output))
 
-    def unpack_kernel(get, small, out):
-        out.put(0, unpack(get(0)[...].astype(f32)))
-
-    new_in = lax.psum_scatter(in_parts.reshape(-1, 128), DP, scatter_dimension=0, tiled=True)
-    (new_in,) = call(unpack_kernel, [new_in], [((1,) + square, 1, bf16)])
-    new_in = lax.ppermute(new_in, AXES, pairs_of(swapped)).astype(f32)
-
     def sum_kernel(get, small, out):
         out.put(0, total_of(get(0)))
 
-    (out_cov,) = call(sum_kernel, [exchange(out_parts, DP)], [((1,) + square, 1, bf16)])
-    new_out = lax.ppermute(out_cov, AXES, pairs_of(window_place(False))).astype(f32)
-    new_out = new_out + lax.ppermute(out_cov, AXES, pairs_of(window_place(True))).astype(f32).transpose(0, 2, 1)
-
-    def factor(old, cov):
-        return decay * old + ((1.0 - decay) / total_tokens) * cov
-
-    return factor(factor_in, new_in), factor(factor_out, new_out), precond
+    def staged_kernel(get, small, out):
+        total = get(0)[...].astype(f32)
+        for k in range(1, 4):
+            total = total + get(k)[...].astype(f32)
+        out.put(0, unpack(total))
+
+    (in_cov,) = call(staged_kernel, in_got, [((1,) + square, 1, bf16)])
+    in_cov = lax.ppermute(in_cov, AXES, pairs_of(swapped))
+    (out_cov,) = call(sum_kernel, [exchange(out_parts, ("y", "xl"))], [((1,) + square, 1, bf16)])
+    out_cov = [lax.ppermute(out_cov, AXES, pairs_of(window_place(mirror))) for mirror in (False, True)]
+
+    def factor(old, *covs):
+        def kernel(get, small, out):
+            cov = small[1][0].astype(f32)
+            if len(covs) > 1:
+                cov = cov + small[2][0].astype(f32).T
+            out.put(0, decay * small[0][0] + ((1.0 - decay) / total_tokens) * cov)
+
+        return call(kernel, [], [(old.shape, 1, f32)], (), [old, *covs])[0]
+
+    return factor(factor_in, in_cov), factor(factor_out, *out_cov), precond
 
 
 def solution(mesh):

time: 275 us -> 237 us (0.86)
  blocking collectives: 46.3 us -> 0 us
  starting transfers between devices: 76.6 us -> 99.9 us
  between operations: 14.4 us -> 1.05 us
  waiting for transfers between devices: 96.6 us -> 85.4 us
  Pallas kernels: 32.1 us -> 42.8 us
    all_to_all x1 -> x0, blocking collectives: 27 us -> none  [exchange(): return lax.all_to_all(chunks, axes, 0, 0, tiled=True)]
    all_to_all x4 -> x6, waiting for transfers between devices: 1.7 us -> 21.1 us  [exchange(): return lax.all_to_all(chunks, axes, 0, 0, tiled=True)]
    all_gather x1 -> x0, blocking collectives: 19.3 us -> none  [body(): scaled = lax.all_gather(scaled, COL, axis=0, tiled=True)]
    ppermute x15 -> x23, waiting for transfers between devices: 65.3 us -> 51.6 us  [shift(): lax.ppermute(value, axis, [(i, (i + step) % size) for i in range(size)])]
    ppermute x1, waiting for transfers between devices: 12.9 us -> 0.01 us  [body(): lax.ppermute(rows_in[0], AXES, [(b, a) for a, b in pairs_of(to_output)])]
    pallas_call x12 -> x18, Pallas kernels: 32.1 us -> 42.8 us  [call(): pl.pallas_call(wrapped, out_shape=[jax.ShapeDtypeStruct(shape, dtype) for...]
    all_to_all x4 -> x6, starting transfers between devices: 24 us -> 34.3 us  [exchange(): return lax.all_to_all(chunks, axes, 0, 0, tiled=True)]
    ppermute x15 -> x23, starting transfers between devices: 26.4 us -> 33.6 us  [shift(): lax.ppermute(value, axis, [(i, (i + step) % size) for i in range(size)])]
  transfers between devices with their start and end apart: 27 -> 36, of which waited for: 12 -> 19; matrix products, arithmetic and copies ran while one was open for 0% -> 0% of each run, Pallas kernels for 8% -> 14%
where the time goes in v1:
time: 237 us; the launch traced here: 235 us
  starting transfers between devices  99.9 us (42%)
  waiting for transfers between devices  85.4 us (36%)
  Pallas kernels  42.8 us (18%)
  local copies, waits for them, and re-layouts  5.59 us (2%)
    ppermute x23, waiting for transfers between devices, shift(): lax.ppermute(value, axis, [(i, (i + step) % size) for i in range(size)])  51.6 us
    pallas_call x18, Pallas kernels, call(): pl.pallas_call(wrapped, out_shape=[jax.ShapeDtypeStruct(shape, dtype) for...  42.8 us
    all_to_all x6, starting transfers between devices, exchange(): return lax.all_to_all(chunks, axes, 0, 0, tiled=True)  34.3 us
    ppermute x23, starting transfers between devices, shift(): lax.ppermute(value, axis, [(i, (i + step) % size) for i in range(size)])  33.6 us
    all_to_all x6, waiting for transfers between devices, exchange(): return lax.all_to_all(chunks, axes, 0, 0, tiled=True)  21.1 us
    ppermute x2, starting transfers between devices, body(): lax.ppermute(out_cov, AXES, pairs_of(window_place(mirror)))  12 us
    ppermute x1, waiting for transfers between devices, body(): lax.ppermute(jnp.concatenate([eig_in, eig_out], axis=0), AXES, [(b, a) fo...  8.82 us
    ppermute x1, starting transfers between devices, body(): in_cov = lax.ppermute(in_cov, AXES, pairs_of(swapped))  6.28 us
  transfers between devices with their start and end apart: 36, of which 19 were waited for; matrix products, arithmetic and copies ran while one was open for 0% of the time, Pallas kernels for 14%

profile of v1, /device:TPU:6, one launch (start us, length us, event | category | flops | bytes accessed | tf_op | source)
XLA Modules:
  0.0 234.7 jit_solution(14271794711417761468)
XLA Ops:
  2.6 4.0 %collective-permute-start.1 = (bf16[160,2048]{1,0:T(8,128)(2,1)}, bf16[160,2048]{1,0:T(8,128)(2,1)S(1)}, u32[]{:S(2)}, u32[]{:S(2)}) collective-permute-start(bf16[160,2048]{1,0:T(8,128)(2,1)} %bitcast.28), channel_id=1, source_target_pairs={{0,7},{1,0},{2,1},{3,2},{4,3},{5,4},{6,5},{7,6},{8,15},{9,8},{10,9... | collective-permute-start | bytes 1966088 | tf_op jit(solution)/shard_map/ppermute | solution.py:114
  14.3 7.2 %collective-permute-done.refs_6_ = bf16[160,2048]{1,0:T(8,128)(2,1)S(1)} collective-permute-done((bf16[160,2048]{1,0:T(8,128)(2,1)}, bf16[160,2048]{1,0:T(8,128)(2,1)S(1)}, u32[]{:S(2)}, u32[]{:S(2)}) %collective-permute-start) | collective-permute-done | bytes 655392 | tf_op jit(solution)/shard_map/ppermute | solution.py:114
  21.5 3.2 %collective-permute-start.3 = (bf16[160,2048]{1,0:T(8,128)(2,1)S(1)}, bf16[160,2048]{1,0:T(8,128)(2,1)S(1)}, u32[]{:S(2)}, u32[]{:S(2)}) collective-permute-start(bf16[160,2048]{1,0:T(8,128)(2,1)S(1)} %collective-permute-done.1.refs_5_), channel_id=1, source_target_pairs={{0,7},{1,0},{2,1},{3,2},{4,3},{5,4},{6,5},{7,6},{8,15},{9,8},{10,9... | collective-permute-start | bytes 1966088 | tf_op jit(solution)/shard_map/ppermute | solution.py:114
  26.0 12.6 %collective-permute-done.4.refs_3_ = bf16[160,2048]{1,0:T(8,128)(2,1)S(1)} collective-permute-done((bf16[160,2048]{1,0:T(8,128)(2,1)}, bf16[160,2048]{1,0:T(8,128)(2,1)S(1)}, u32[]{:S(2)}, u32[]{:S(2)}) %collective-permute-start.4) | collective-permute-done | bytes 655392 | tf_op jit(solution)/shard_map/ppermute | solution.py:114
  41.9 8.2 %shard_map.104 = (bf16[16,200,128]{2,1,0:T(8,128)(2,1)}, bf16[16,200,128]{2,1,0:T(8,128)(2,1)S(1)}) custom-call(bf16[160,2048]{1,0:T(8,128)(2,1)S(1)} %bitcast.30, bf16[160,2048]{1,0:T(8,128)(2,1)S(1)} %collective-permute-done.5.refs_1_, bf16[160,2048]{1,0:T(8,128)(2,1)S(1)} %bitcast.21, bf16[160,2048]{1,0:T(8,128)(2,1)S(1)} %collective-permute-done.4.refs_3_, ...), custom_call_target="tpu_custom_call" | custom-call | flops 2097152000 | tf_op jit(solution)/shard_map/pallas_call | solution.py:100
  50.1 5.0 %collective-permute-done.6.refs_5_ = bf16[160,2048]{1,0:T(8,128)(2,1)S(1)} collective-permute-done((bf16[160,2048]{1,0:T(8,128)(2,1)S(1)}, bf16[160,2048]{1,0:T(8,128)(2,1)S(1)}, u32[]{:S(2)}, u32[]{:S(2)}) %collective-permute-start.6) | collective-permute-done | bytes 655392 | tf_op jit(solution)/shard_map/ppermute | solution.py:114
  55.1 3.0 %collective-permute-start.8 = (bf16[80,2048]{1,0:T(8,128)(2,1)S(1)}, bf16[80,2048]{1,0:T(8,128)(2,1)S(1)}, u32[]{:S(2)}, u32[]{:S(2)}) collective-permute-start(bf16[80,2048]{1,0:T(8,128)(2,1)S(1)} %slice.45), channel_id=1, source_target_pairs={{0,7},{1,0},{2,1},{3,2},{4,3},{5,4},{6,5},{7,6},{8,15},{9,8},{10,9... | collective-permute-start | bytes 983048 | tf_op jit(solution)/shard_map/ppermute | solution.py:114
  60.4 6.1 %collective-permute-start.12 = (bf16[160,2560]{1,0:T(8,128)(2,1)}, bf16[160,2560]{1,0:T(8,128)(2,1)}, u32[]{:S(2)}, u32[]{:S(2)}) collective-permute-start(bf16[160,2560]{1,0:T(8,128)(2,1)} %bitcast.9), channel_id=1, source_target_pairs={{0,0},{1,1},{2,2},{3,3},{4,4},{5,5},{6,6},{7,7},{128,8},{129,9},{1... | collective-permute-start | bytes 2457608 | tf_op jit(solution)/shard_map/ppermute | solution.py:194
  66.5 3.5 %shard_map.105 = (bf16[16,200,128]{2,1,0:T(8,128)(2,1)}, bf16[16,200,128]{2,1,0:T(8,128)(2,1)S(1)}) custom-call(bf16[160,2048]{1,0:T(8,128)(2,1)S(1)} %bitcast.32, bf16[160,2048]{1,0:T(8,128)(2,1)S(1)} %collective-permute-done.5.refs_1_, bf16[160,2048]{1,0:T(8,128)(2,1)S(1)} %bitcast.22, ...), custom_call_target="tpu_custom_call", output_to_operand_aliasing={{0}: (6, {}), {1}: (7, {})} | custom-call | flops 838860800 | tf_op jit(solution)/shard_map/pallas_call | solution.py:100
  70.0 2.5 %shard_map.106 = (bf16[16,200,128]{2,1,0:T(8,128)(2,1)}, bf16[16,200,128]{2,1,0:T(8,128)(2,1)S(1)}) custom-call(bf16[160,2048]{1,0:T(8,128)(2,1)S(1)} %bitcast.33, bf16[160,2048]{1,0:T(8,128)(2,1)S(1)} %collective-permute-done.5.refs_1_, bf16[160,2048]{1,0:T(8,128)(2,1)S(1)} %bitcast.23, ...), custom_call_target="tpu_custom_call", output_to_operand_aliasing={{0}: (6, {}), {1}: (7, {})} | custom-call | flops 419430400 | tf_op jit(solution)/shard_map/pallas_call | solution.py:100
  72.5 5.1 %all-to-all-start = ((bf16[16,200,128]{2,1,0:T(8,128)(2,1)}), bf16[16,200,128]{2,1,0:T(8,128)(2,1)S(1)}, u32[]{:S(2)}, u32[]{:S(2)}) async-start(bf16[16,200,128]{2,1,0:T(8,128)(2,1)} %get-tuple-element.64), calls=%async_computation | async-start | bytes 1638400 | tf_op jit(solution)/shard_map/all_to_all | solution.py:118
  82.8 3.4 %collective-permute-start.10 = (f32[2,160]{1,0:T(2,128)S(1)}, f32[2,160]{1,0:T(2,128)S(1)}, u32[]{:S(2)}, u32[]{:S(2)}) collective-permute-start(f32[2,160]{1,0:T(2,128)S(1)} %pad_maximum_fusion), channel_id=1, source_target_pairs={{0,0},{1,1},{2,2},{3,3},{4,4},{5,5},{6,6},{7,7},{128,8},{129,9},{1... | collective-permute-start | bytes 3848 | tf_op jit(solution)/shard_map/ppermute | solution.py:236
  87.4 8.8 %collective-permute-done.10.refs_1_ = f32[2,160]{1,0:T(2,128)S(1)} collective-permute-done((f32[2,160]{1,0:T(2,128)S(1)}, f32[2,160]{1,0:T(2,128)S(1)}, u32[]{:S(2)}, u32[]{:S(2)}) %collective-permute-start.10) | collective-permute-done | bytes 1312 | tf_op jit(solution)/shard_map/ppermute | solution.py:236
  99.1 3.6 %shard_map.108 = bf16[16,200,128]{2,1,0:T(8,128)(2,1)S(1)} custom-call(bf16[16,200,128]{2,1,0:T(8,128)(2,1)S(1)} %all-to-all-done.refs_0_, bf16[160,2560]{1,0:T(8,128)(2,1)S(1)} %collective-permute-done.11.refs_1_.refs_2_), custom_call_target="tpu_custom_call" | custom-call | flops 131072000 | bytes 1638400 | tf_op jit(solution)/shard_map/pallas_call | solution.py:100
  105.9 5.9 %all-to-all-start.1 = ((bf16[8,200,128]{2,1,0:T(8,128)(2,1)}), bf16[8,200,128]{2,1,0:T(8,128)(2,1)S(1)}, u32[]{:S(2)}, u32[]{:S(2)}) async-start(bf16[8,200,128]{2,1,0:T(8,128)(2,1)} %shard_map.109), calls=%async_computation.1 | async-start | bytes 819200 | tf_op jit(solution)/shard_map/all_to_all | solution.py:118
  111.9 6.8 %collective-permute-done.17.refs_1_ = bf16[4,200,128]{2,1,0:T(8,128)(2,1)S(1)} collective-permute-done((bf16[4,200,128]{2,1,0:T(8,128)(2,1)S(1)}, bf16[4,200,128]{2,1,0:T(8,128)(2,1)S(1)}, u32[]{:S(2)}, u32[]{:S(2)}) %collective-permute-start.17) | collective-permute-done | bytes 204832 | tf_op jit(solution)/shard_map/ppermute | solution.py:114
  119.6 7.5 %all-to-all-done.1.refs_0_ = bf16[8,200,128]{2,1,0:T(8,128)(2,1)S(1)} async-done(((bf16[8,200,128]{2,1,0:T(8,128)(2,1)}), bf16[8,200,128]{2,1,0:T(8,128)(2,1)S(1)}, u32[]{:S(2)}, u32[]{:S(2)}) %all-to-all-start.1) | async-done | bytes 409632 | tf_op jit(solution)/shard_map/all_to_all | solution.py:118
  127.1 2.7 %shard_map.111 = bf16[16,200,128]{2,1,0:T(8,128)(2,1)} custom-call(bf16[8,200,128]{2,1,0:T(8,128)(2,1)S(1)} %all-to-all-done.1.refs_0_, bf16[160,2560]{1,0:T(8,128)(2,1)} %collective-permute-done.12.refs_1_), custom_call_target="tpu_custom_call" | custom-call | flops 131072000 | bytes 1228800 | tf_op jit(solution)/shard_map/pallas_call | solution.py:100
  129.8 6.6 %all-to-all-start.2 = ((bf16[16,200,128]{2,1,0:T(8,128)(2,1)}), bf16[16,200,128]{2,1,0:T(8,128)(2,1)S(1)}, u32[]{:S(2)}, u32[]{:S(2)}) async-start(bf16[16,200,128]{2,1,0:T(8,128)(2,1)} %shard_map.111), calls=%async_computation.2 | async-start | bytes 1638400 | tf_op jit(solution)/shard_map/all_to_all | solution.py:118
  137.1 2.7 %collective-permute-start.19 = (bf16[160,2048]{1,0:T(8,128)(2,1)}, bf16[160,2048]{1,0:T(8,128)(2,1)}, u32[]{:S(2)}, u32[]{:S(2)}) collective-permute-start(bf16[160,2048]{1,0:T(8,128)(2,1)} %collective-permute-done.14.refs_3_), channel_id=1, source_target_pairs={{0,7},{1,0},{2,1},{3,2},{4,3},{5,4},{6,5},{7,6},{8,15},{9,8},{10,9... | collective-permute-start | bytes 1966088 | tf_op jit(solution)/shard_map/ppermute | solution.py:114
  139.9 9.7 %all-to-all-done.2.refs_0_ = bf16[16,200,128]{2,1,0:T(8,128)(2,1)S(1)} async-done(((bf16[16,200,128]{2,1,0:T(8,128)(2,1)}), bf16[16,200,128]{2,1,0:T(8,128)(2,1)S(1)}, u32[]{:S(2)}, u32[]{:S(2)}) %all-to-all-start.2) | async-done | bytes 819232 | tf_op jit(solution)/shard_map/all_to_all | solution.py:118
  150.9 3.3 %collective-permute-done.18.refs_0_ = bf16[160,2048]{1,0:T(8,128)(2,1)} collective-permute-done((bf16[160,2048]{1,0:T(8,128)(2,1)S(1)}, bf16[160,2048]{1,0:T(8,128)(2,1)}, u32[]{:S(2)}, u32[]{:S(2)}) %collective-permute-start.18) | collective-permute-done | bytes 655392 | tf_op jit(solution)/shard_map/ppermute | solution.py:114
  154.1 4.4 %all-to-all-start.3 = ((bf16[8,200,128]{2,1,0:T(8,128)(2,1)}), bf16[8,200,128]{2,1,0:T(8,128)(2,1)S(1)}, u32[]{:S(2)}, u32[]{:S(2)}) async-start(bf16[8,200,128]{2,1,0:T(8,128)(2,1)} %shard_map.112), calls=%async_computation.3 | async-start | bytes 819200 | tf_op jit(solution)/shard_map/all_to_all | solution.py:118
  161.8 2.7 %collective-permute-start.22 = (bf16[200,128]{1,0:T(8,128)(2,1)S(1)}, bf16[200,128]{1,0:T(8,128)(2,1)S(1)}, u32[]{:S(2)}, u32[]{:S(2)}) collective-permute-start(bf16[200,128]{1,0:T(8,128)(2,1)S(1)} %get-tuple-element.98), channel_id=1, source_target_pairs={{0,128},{64,192},{128,0},{192,64},{1,129},{65,193},{129,1},{193,65... | collective-permute-start | bytes 153608 | tf_op jit(solution)/shard_map/ppermute | solution.py:114
  168.6 6.5 %collective-permute-done.20.refs_5_ = bf16[160,2048]{1,0:T(8,128)(2,1)S(1)} collective-permute-done((bf16[160,2048]{1,0:T(8,128)(2,1)}, bf16[160,2048]{1,0:T(8,128)(2,1)S(1)}, u32[]{:S(2)}, u32[]{:S(2)}) %collective-permute-start.20) | collective-permute-done | bytes 655392 | tf_op jit(solution)/shard_map/ppermute | solution.py:114
  180.1 7.4 %all-to-all-start.4 = ((bf16[16,200,128]{2,1,0:T(8,128)(2,1)}), bf16[16,200,128]{2,1,0:T(8,128)(2,1)S(1)}, u32[]{:S(2)}, u32[]{:S(2)}) async-start(bf16[16,200,128]{2,1,0:T(8,128)(2,1)} %shard_map.115), calls=%async_computation.4 | async-start | bytes 1638400 | tf_op jit(solution)/shard_map/all_to_all | solution.py:118
  187.5 8.0 %shard_map.116 = bf16[16,200,128]{2,1,0:T(8,128)(2,1)S(1)} custom-call(bf16[160,2048]{1,0:T(8,128)(2,1)} %collective-permute-done.18.refs_0_, bf16[160,2048]{1,0:T(8,128)(2,1)S(1)} %copy-done.5, bf16[160,2048]{1,0:T(8,128)(2,1)S(1)} %bitcast.26, bf16[160,2048]{1,0:T(8,128)(2,1)} %collective-permute-done.14.refs_3_, ...), custom_call_target="tpu_custom_call" | custom-call | flops 1048576000 | bytes 3932160 | tf_op jit(solution)/shard_map/pallas_call | solution.py:100
  200.6 4.9 %all-to-all-start.5 = ((bf16[8,200,128]{2,1,0:T(8,128)(2,1)}), bf16[8,200,128]{2,1,0:T(8,128)(2,1)S(1)}, u32[]{:S(2)}, u32[]{:S(2)}) async-start(bf16[8,200,128]{2,1,0:T(8,128)(2,1)} %shard_map.117), calls=%async_computation.5 | async-start | bytes 819200 | tf_op jit(solution)/shard_map/all_to_all | solution.py:118
  206.0 6.3 %collective-permute-start.24 = (bf16[1,160,160]{2,1,0:T(8,128)(2,1)S(1)}, bf16[1,160,160]{2,1,0:T(8,128)(2,1)S(1)}, u32[]{:S(2)}, u32[]{:S(2)}) collective-permute-start(bf16[1,160,160]{2,1,0:T(8,128)(2,1)S(1)} %shard_map.113), channel_id=1, source_target_pairs={{0,0},{1,1},{2,2},{3,3},{4,4},{5,5},{6,6},{7,7},{8,128},{9,129},{1... | collective-permute-start | bytes 153608 | tf_op jit(solution)/shard_map/ppermute | solution.py:351
  216.5 2.6 %collective-permute-start.27 = (bf16[1,160,160]{2,1,0:T(8,128)(2,1)S(1)}, bf16[1,160,160]{2,1,0:T(8,128)(2,1)S(1)}, u32[]{:S(2)}, u32[]{:S(2)}) collective-permute-start(bf16[1,160,160]{2,1,0:T(8,128)(2,1)S(1)} %shard_map.118), channel_id=1, source_target_pairs={{0,102},{1,119},{2,0},{3,17},{4,34},{5,51},{6,68},{7,85},{8,238},{... | collective-permute-start | bytes 153608 | tf_op jit(solution)/shard_map/ppermute | solution.py:353
  219.2 9.4 %collective-permute-start.28 = (bf16[1,160,160]{2,1,0:T(8,128)(2,1)S(1)}, bf16[1,160,160]{2,1,0:T(8,128)(2,1)S(1)}, u32[]{:S(2)}, u32[]{:S(2)}) collective-permute-start(bf16[1,160,160]{2,1,0:T(8,128)(2,1)S(1)} %shard_map.118), channel_id=1, source_target_pairs={{16,118},{17,7},{18,16},{19,33},{20,50},{21,67},{22,84},{23,101},{... | collective-permute-start | bytes 153608 | tf_op jit(solution)/shard_map/ppermute | solution.py:353
  229.3 4.0 %collective-permute-done.28.refs_2_ = bf16[1,160,160]{2,1,0:T(8,128)(2,1)S(1)} collective-permute-done((bf16[1,160,160]{2,1,0:T(8,128)(2,1)S(1)}, bf16[1,160,160]{2,1,0:T(8,128)(2,1)S(1)}, u32[]{:S(2)}, u32[]{:S(2)}) %collective-permute-start.28) | collective-permute-done | bytes 51232 | tf_op jit(solution)/shard_map/ppermute | solution.py:353
  (93 shorter events, 56.0 us)
Async XLA Ops:
  0.6 20.9 %collective-permute-start = (bf16[160,2048]{1,0:T(8,128)(2,1)}, bf16[160,2048]{1,0:T(8,128)(2,1)S(1)}, u32[]{:S(2)}, u32[]{:S(2)}) collective-permute-start(bf16[160,2048]{1,0:T(8,128)(2,1)} %bitcast.27), channel_id=1, source_target_pairs={{0,1},{1,2},{2,3},{3,4},{4,5},{5,6},{6,7},{7,0},{8,9},{9,10},{10,1... | collective-permute-start | bytes 1966088 | tf_op jit(solution)/shard_map/ppermute | solution.py:114
  2.6 18.9 %collective-permute-start.1 = (bf16[160,2048]{1,0:T(8,128)(2,1)}, bf16[160,2048]{1,0:T(8,128)(2,1)S(1)}, u32[]{:S(2)}, u32[]{:S(2)}) collective-permute-start(bf16[160,2048]{1,0:T(8,128)(2,1)} %bitcast.28), channel_id=1, source_target_pairs={{0,7},{1,0},{2,1},{3,2},{4,3},{5,4},{6,5},{7,6},{8,15},{9,8},{10,9... | collective-permute-start | bytes 1966088 | tf_op jit(solution)/shard_map/ppermute | solution.py:114
  6.7 19.4 %collective-permute-start.5 = (bf16[160,2048]{1,0:T(8,128)(2,1)}, bf16[160,2048]{1,0:T(8,128)(2,1)S(1)}, u32[]{:S(2)}, u32[]{:S(2)}) collective-permute-start(bf16[160,2048]{1,0:T(8,128)(2,1)} %bitcast.29), channel_id=1, source_target_pairs={{0,8},{8,0},{1,9},{9,1},{2,10},{10,2},{3,11},{11,3},{4,12},{12,4},... | collective-permute-start | bytes 1966088 | tf_op jit(solution)/shard_map/ppermute | solution.py:114
  8.1 30.5 %collective-permute-start.4 = (bf16[160,2048]{1,0:T(8,128)(2,1)}, bf16[160,2048]{1,0:T(8,128)(2,1)S(1)}, u32[]{:S(2)}, u32[]{:S(2)}) collective-permute-start(bf16[160,2048]{1,0:T(8,128)(2,1)} %bitcast.20), channel_id=1, source_target_pairs={{0,8},{8,0},{1,9},{9,1},{2,10},{10,2},{3,11},{11,3},{4,12},{12,4},... | collective-permute-start | bytes 1966088 | tf_op jit(solution)/shard_map/ppermute | solution.py:114
  21.5 17.1 %collective-permute-start.2 = (bf16[160,2048]{1,0:T(8,128)(2,1)S(1)}, bf16[160,2048]{1,0:T(8,128)(2,1)S(1)}, u32[]{:S(2)}, u32[]{:S(2)}) collective-permute-start(bf16[160,2048]{1,0:T(8,128)(2,1)S(1)} %collective-permute-done.refs_6_), channel_id=1, source_target_pairs={{0,1},{1,2},{2,3},{3,4},{4,5},{5,6},{6,7},{7,0},{8,9},{9,10},{10,1... | collective-permute-start | bytes 1966088 | tf_op jit(solution)/shard_map/ppermute | solution.py:114
  21.5 17.1 %collective-permute-start.3 = (bf16[160,2048]{1,0:T(8,128)(2,1)S(1)}, bf16[160,2048]{1,0:T(8,128)(2,1)S(1)}, u32[]{:S(2)}, u32[]{:S(2)}) collective-permute-start(bf16[160,2048]{1,0:T(8,128)(2,1)S(1)} %collective-permute-done.1.refs_5_), channel_id=1, source_target_pairs={{0,7},{1,0},{2,1},{3,2},{4,3},{5,4},{6,5},{7,6},{8,15},{9,8},{10,9... | collective-permute-start | bytes 1966088 | tf_op jit(solution)/shard_map/ppermute | solution.py:114
  38.6 16.5 %collective-permute-start.6 = (bf16[160,2048]{1,0:T(8,128)(2,1)S(1)}, bf16[160,2048]{1,0:T(8,128)(2,1)S(1)}, u32[]{:S(2)}, u32[]{:S(2)}) collective-permute-start(bf16[160,2048]{1,0:T(8,128)(2,1)S(1)} %collective-permute-done.2.refs_8_), channel_id=1, source_target_pairs={{0,1},{1,2},{2,3},{3,4},{4,5},{5,6},{6,7},{7,0},{8,9},{9,10},{10,1... | collective-permute-start | bytes 1966088 | tf_op jit(solution)/shard_map/ppermute | solution.py:114
  40.5 14.6 %collective-permute-start.7 = (bf16[160,2048]{1,0:T(8,128)(2,1)S(1)}, bf16[160,2048]{1,0:T(8,128)(2,1)S(1)}, u32[]{:S(2)}, u32[]{:S(2)}) collective-permute-start(bf16[160,2048]{1,0:T(8,128)(2,1)S(1)} %collective-permute-done.3.refs_7_), channel_id=1, source_target_pairs={{0,7},{1,0},{2,1},{3,2},{4,3},{5,4},{6,5},{7,6},{8,15},{9,8},{10,9... | collective-permute-start | bytes 1966088 | tf_op jit(solution)/shard_map/ppermute | solution.py:114
  55.1 14.9 %collective-permute-start.8 = (bf16[80,2048]{1,0:T(8,128)(2,1)S(1)}, bf16[80,2048]{1,0:T(8,128)(2,1)S(1)}, u32[]{:S(2)}, u32[]{:S(2)}) collective-permute-start(bf16[80,2048]{1,0:T(8,128)(2,1)S(1)} %slice.45), channel_id=1, source_target_pairs={{0,7},{1,0},{2,1},{3,2},{4,3},{5,4},{6,5},{7,6},{8,15},{9,8},{10,9... | collective-permute-start | bytes 983048 | tf_op jit(solution)/shard_map/ppermute | solution.py:114
  58.2 11.8 %collective-permute-start.9 = (bf16[80,2048]{1,0:T(8,128)(2,1)S(1)}, bf16[80,2048]{1,0:T(8,128)(2,1)S(1)}, u32[]{:S(2)}, u32[]{:S(2)}) collective-permute-start(bf16[80,2048]{1,0:T(8,128)(2,1)S(1)} %slice.46), channel_id=1, source_target_pairs={{0,1},{1,2},{2,3},{3,4},{4,5},{5,6},{6,7},{7,0},{8,9},{9,10},{10,1... | collective-permute-start | bytes 983048 | tf_op jit(solution)/shard_map/ppermute | solution.py:114
  58.3 37.9 %collective-permute-start.11 = (bf16[160,2560]{1,0:T(8,128)(2,1)}, bf16[160,2560]{1,0:T(8,128)(2,1)S(1)}, u32[]{:S(2)}, u32[]{:S(2)}) collective-permute-start(bf16[160,2560]{1,0:T(8,128)(2,1)} %bitcast.8), channel_id=1, source_target_pairs={{0,0},{1,1},{2,2},{3,3},{4,4},{5,5},{6,6},{7,7},{8,16},{9,17},{10,... | collective-permute-start | bytes 2457608 | tf_op jit(solution)/shard_map/ppermute | solution.py:193
  60.4 35.8 %collective-permute-start.12 = (bf16[160,2560]{1,0:T(8,128)(2,1)}, bf16[160,2560]{1,0:T(8,128)(2,1)}, u32[]{:S(2)}, u32[]{:S(2)}) collective-permute-start(bf16[160,2560]{1,0:T(8,128)(2,1)} %bitcast.9), channel_id=1, source_target_pairs={{0,0},{1,1},{2,2},{3,3},{4,4},{5,5},{6,6},{7,7},{128,8},{129,9},{1... | collective-permute-start | bytes 2457608 | tf_op jit(solution)/shard_map/ppermute | solution.py:194
  72.5 26.5 %all-to-all-start = ((bf16[16,200,128]{2,1,0:T(8,128)(2,1)}), bf16[16,200,128]{2,1,0:T(8,128)(2,1)S(1)}, u32[]{:S(2)}, u32[]{:S(2)}) async-start(bf16[16,200,128]{2,1,0:T(8,128)(2,1)} %get-tuple-element.64), calls=%async_computation | async-start | bytes 1638400 | tf_op jit(solution)/shard_map/all_to_all | solution.py:118
  77.6 18.6 %collective-permute-start.13 = (bf16[160,2048]{1,0:T(8,128)(2,1)S(1)}, bf16[160,2048]{1,0:T(8,128)(2,1)S(1)}, u32[]{:S(2)}, u32[]{:S(2)}) collective-permute-start(bf16[160,2048]{1,0:T(8,128)(2,1)S(1)} %bitcast.24), channel_id=1, source_target_pairs={{0,1},{1,2},{2,3},{3,4},{4,5},{5,6},{6,7},{7,0},{8,9},{9,10},{10,1... | collective-permute-start | bytes 1966088 | tf_op jit(solution)/shard_map/ppermute | solution.py:114
  78.5 18.5 %collective-permute-start.14 = (bf16[160,2048]{1,0:T(8,128)(2,1)S(1)}, bf16[160,2048]{1,0:T(8,128)(2,1)}, u32[]{:S(2)}, u32[]{:S(2)}) collective-permute-start(bf16[160,2048]{1,0:T(8,128)(2,1)S(1)} %bitcast.25), channel_id=1, source_target_pairs={{0,7},{1,0},{2,1},{3,2},{4,3},{5,4},{6,5},{7,6},{8,15},{9,8},{10,9... | collective-permute-start | bytes 1966088 | tf_op jit(solution)/shard_map/ppermute | solution.py:114
  82.8 13.4 %collective-permute-start.10 = (f32[2,160]{1,0:T(2,128)S(1)}, f32[2,160]{1,0:T(2,128)S(1)}, u32[]{:S(2)}, u32[]{:S(2)}) collective-permute-start(f32[2,160]{1,0:T(2,128)S(1)} %pad_maximum_fusion), channel_id=1, source_target_pairs={{0,0},{1,1},{2,2},{3,3},{4,4},{5,5},{6,6},{7,7},{128,8},{129,9},{1... | collective-permute-start | bytes 3848 | tf_op jit(solution)/shard_map/ppermute | solution.py:236
  105.9 21.2 %all-to-all-start.1 = ((bf16[8,200,128]{2,1,0:T(8,128)(2,1)}), bf16[8,200,128]{2,1,0:T(8,128)(2,1)S(1)}, u32[]{:S(2)}, u32[]{:S(2)}) async-start(bf16[8,200,128]{2,1,0:T(8,128)(2,1)} %shard_map.109), calls=%async_computation.1 | async-start | bytes 819200 | tf_op jit(solution)/shard_map/all_to_all | solution.py:118
  111.8 6.9 %collective-permute-start.17 = (bf16[4,200,128]{2,1,0:T(8,128)(2,1)S(1)}, bf16[4,200,128]{2,1,0:T(8,128)(2,1)S(1)}, u32[]{:S(2)}, u32[]{:S(2)}) collective-permute-start(bf16[4,200,128]{2,1,0:T(8,128)(2,1)S(1)} %get-tuple-element.95), channel_id=1, source_target_pairs={{0,32},{32,0},{1,33},{33,1},{2,34},{34,2},{3,35},{35,3},{4,36},{36... | collective-permute-start | bytes 614408 | tf_op jit(solution)/shard_map/ppermute | solution.py:114
  129.8 19.8 %all-to-all-start.2 = ((bf16[16,200,128]{2,1,0:T(8,128)(2,1)}), bf16[16,200,128]{2,1,0:T(8,128)(2,1)S(1)}, u32[]{:S(2)}, u32[]{:S(2)}) async-start(bf16[16,200,128]{2,1,0:T(8,128)(2,1)} %shard_map.111), calls=%async_computation.2 | async-start | bytes 1638400 | tf_op jit(solution)/shard_map/all_to_all | solution.py:118
  136.5 17.6 %collective-permute-start.18 = (bf16[160,2048]{1,0:T(8,128)(2,1)S(1)}, bf16[160,2048]{1,0:T(8,128)(2,1)}, u32[]{:S(2)}, u32[]{:S(2)}) collective-permute-start(bf16[160,2048]{1,0:T(8,128)(2,1)S(1)} %copy-done.5), channel_id=1, source_target_pairs={{0,1},{1,2},{2,3},{3,4},{4,5},{5,6},{6,7},{7,0},{8,9},{9,10},{10,1... | collective-permute-start | bytes 1966088 | tf_op jit(solution)/shard_map/ppermute | solution.py:114
  137.1 17.0 %collective-permute-start.19 = (bf16[160,2048]{1,0:T(8,128)(2,1)}, bf16[160,2048]{1,0:T(8,128)(2,1)}, u32[]{:S(2)}, u32[]{:S(2)}) collective-permute-start(bf16[160,2048]{1,0:T(8,128)(2,1)} %collective-permute-done.14.refs_3_), channel_id=1, source_target_pairs={{0,7},{1,0},{2,1},{3,2},{4,3},{5,4},{6,5},{7,6},{8,15},{9,8},{10,9... | collective-permute-start | bytes 1966088 | tf_op jit(solution)/shard_map/ppermute | solution.py:114
  154.1 21.8 %all-to-all-start.3 = ((bf16[8,200,128]{2,1,0:T(8,128)(2,1)}), bf16[8,200,128]{2,1,0:T(8,128)(2,1)S(1)}, u32[]{:S(2)}, u32[]{:S(2)}) async-start(bf16[8,200,128]{2,1,0:T(8,128)(2,1)} %shard_map.112), calls=%async_computation.3 | async-start | bytes 819200 | tf_op jit(solution)/shard_map/all_to_all | solution.py:118
  158.6 16.5 %collective-permute-start.20 = (bf16[160,2048]{1,0:T(8,128)(2,1)}, bf16[160,2048]{1,0:T(8,128)(2,1)S(1)}, u32[]{:S(2)}, u32[]{:S(2)}) collective-permute-start(bf16[160,2048]{1,0:T(8,128)(2,1)} %collective-permute-done.18.refs_0_), channel_id=1, source_target_pairs={{0,8},{8,0},{1,9},{9,1},{2,10},{10,2},{3,11},{11,3},{4,12},{12,4},... | collective-permute-start | bytes 1966088 | tf_op jit(solution)/shard_map/ppermute | solution.py:114
  160.0 5.9 %collective-permute-start.21 = (bf16[200,128]{1,0:T(8,128)(2,1)S(1)}, bf16[200,128]{1,0:T(8,128)(2,1)S(1)}, u32[]{:S(2)}, u32[]{:S(2)}) collective-permute-start(bf16[200,128]{1,0:T(8,128)(2,1)S(1)} %get-tuple-element.99), channel_id=1, source_target_pairs={{0,64},{64,128},{128,192},{192,0},{1,65},{65,129},{129,193},{193,1... | collective-permute-start | bytes 153608 | tf_op jit(solution)/shard_map/ppermute | solution.py:114
  161.8 5.6 %collective-permute-start.22 = (bf16[200,128]{1,0:T(8,128)(2,1)S(1)}, bf16[200,128]{1,0:T(8,128)(2,1)S(1)}, u32[]{:S(2)}, u32[]{:S(2)}) collective-permute-start(bf16[200,128]{1,0:T(8,128)(2,1)S(1)} %get-tuple-element.98), channel_id=1, source_target_pairs={{0,128},{64,192},{128,0},{192,64},{1,129},{65,193},{129,1},{193,65... | collective-permute-start | bytes 153608 | tf_op jit(solution)/shard_map/ppermute | solution.py:114
  164.5 4.1 %collective-permute-start.23 = (bf16[200,128]{1,0:T(8,128)(2,1)S(1)}, bf16[200,128]{1,0:T(8,128)(2,1)S(1)}, u32[]{:S(2)}, u32[]{:S(2)}) collective-permute-start(bf16[200,128]{1,0:T(8,128)(2,1)S(1)} %get-tuple-element.97), channel_id=1, source_target_pairs={{0,192},{64,0},{128,64},{192,128},{1,193},{65,1},{129,65},{193,129... | collective-permute-start | bytes 153608 | tf_op jit(solution)/shard_map/ppermute | solution.py:114
  180.1 20.5 %all-to-all-start.4 = ((bf16[16,200,128]{2,1,0:T(8,128)(2,1)}), bf16[16,200,128]{2,1,0:T(8,128)(2,1)S(1)}, u32[]{:S(2)}, u32[]{:S(2)}) async-start(bf16[16,200,128]{2,1,0:T(8,128)(2,1)} %shard_map.115), calls=%async_computation.4 | async-start | bytes 1638400 | tf_op jit(solution)/shard_map/all_to_all | solution.py:118
  200.6 15.5 %all-to-all-start.5 = ((bf16[8,200,128]{2,1,0:T(8,128)(2,1)}), bf16[8,200,128]{2,1,0:T(8,128)(2,1)S(1)}, u32[]{:S(2)}, u32[]{:S(2)}) async-start(bf16[8,200,128]{2,1,0:T(8,128)(2,1)} %shard_map.117), calls=%async_computation.5 | async-start | bytes 819200 | tf_op jit(solution)/shard_map/all_to_all | solution.py:118
  206.0 22.6 %collective-permute-start.24 = (bf16[1,160,160]{2,1,0:T(8,128)(2,1)S(1)}, bf16[1,160,160]{2,1,0:T(8,128)(2,1)S(1)}, u32[]{:S(2)}, u32[]{:S(2)}) collective-permute-start(bf16[1,160,160]{2,1,0:T(8,128)(2,1)S(1)} %shard_map.113), channel_id=1, source_target_pairs={{0,0},{1,1},{2,2},{3,3},{4,4},{5,5},{6,6},{7,7},{8,128},{9,129},{1... | collective-permute-start | bytes 153608 | tf_op jit(solution)/shard_map/ppermute | solution.py:351
  214.0 15.3 %collective-permute-start.29 = (bf16[1,160,160]{2,1,0:T(8,128)(2,1)S(1)}, bf16[1,160,160]{2,1,0:T(8,128)(2,1)S(1)}, u32[]{:S(2)}, u32[]{:S(2)}) collective-permute-start(bf16[1,160,160]{2,1,0:T(8,128)(2,1)S(1)} %shard_map.120), channel_id=1, source_target_pairs={{0,0},{1,1},{2,2},{3,3},{4,4},{5,5},{6,6},{7,7},{8,128},{9,129},{1... | collective-permute-start | bytes 153608 | tf_op jit(solution)/shard_map/ppermute | solution.py:339
  216.5 12.8 %collective-permute-start.27 = (bf16[1,160,160]{2,1,0:T(8,128)(2,1)S(1)}, bf16[1,160,160]{2,1,0:T(8,128)(2,1)S(1)}, u32[]{:S(2)}, u32[]{:S(2)}) collective-permute-start(bf16[1,160,160]{2,1,0:T(8,128)(2,1)S(1)} %shard_map.118), channel_id=1, source_target_pairs={{0,102},{1,119},{2,0},{3,17},{4,34},{5,51},{6,68},{7,85},{8,238},{... | collective-permute-start | bytes 153608 | tf_op jit(solution)/shard_map/ppermute | solution.py:353
  219.2 14.1 %collective-permute-start.28 = (bf16[1,160,160]{2,1,0:T(8,128)(2,1)S(1)}, bf16[1,160,160]{2,1,0:T(8,128)(2,1)S(1)}, u32[]{:S(2)}, u32[]{:S(2)}) collective-permute-start(bf16[1,160,160]{2,1,0:T(8,128)(2,1)S(1)} %shard_map.118), channel_id=1, source_target_pairs={{16,118},{17,7},{18,16},{19,33},{20,50},{21,67},{22,84},{23,101},{... | collective-permute-start | bytes 153608 | tf_op jit(solution)/shard_map/ppermute | solution.py:353
  (16 other events, 116.8 us)

commit v2 on v1

--- a/solution.py
+++ b/solution.py
@@ -35,8 +35,8 @@
 
 
 class Emit:
-    def __init__(self, out, slots, sems):
-        self.out, self.slots, self.sems, self.copies = out, slots, sems, []
+    def __init__(self, out, slots, sems, whole):
+        self.out, self.slots, self.sems, self.whole, self.copies = out, slots, sems, whole, []
 
     def send(self, slot, index):
         number = len(self.copies)
@@ -44,25 +44,38 @@
         copy.start()
         self.copies.append(copy)
 
+    def place(self, index, main, packed=None):
+        slot = index if self.whole else len(self.copies)
+        if packed is None:
+            self.slots[slot] = main.astype(self.slots.dtype)
+        else:
+            rows = main.shape[0]
+            self.slots[slot, :rows] = main.astype(bf16)
+            self.slots[slot, rows:] = packed.astype(bf16)
+        if not self.whole:
+            self.send(slot, index)
+
     def put(self, index, value):
-        slot = len(self.copies)
-        self.slots[slot] = value.astype(self.slots.dtype)
-        self.send(slot, index)
+        self.place(index, value)
 
     def parts(self, index, main, rest):
-        slot = len(self.copies)
-        rows = main.shape[0]
-        self.slots[slot, :rows] = main.astype(bf16)
-        self.slots[slot, rows:] = pack(rest).astype(bf16)
-        self.send(slot, index)
+        self.place(index, main, pack(rest))
 
     def __call__(self, index, value):
         self.parts(index, value[:, :128], value[:, 128:])
 
     def everywhere(self, value):
-        self(0, value)
-        for index in range(1, self.out.shape[0]):
-            self.send(0, index)
+        main, packed = value[:, :128].astype(bf16), pack(value[:, 128:]).astype(bf16)
+        for index in range(self.out.shape[0]):
+            self.place(index, main, packed)
+
+    def finish(self):
+        if self.whole:
+            copy = pltpu.make_async_copy(self.slots, self.out, self.sems.at[0])
+            copy.start()
+            self.copies.append(copy)
+        for copy in self.copies:
+            copy.wait()
 
 
 def call(kernel, ins, outs, after=(), small=(), alias=(), scratch=(), flops=0):
@@ -84,13 +97,12 @@
                 waited.add(k)
             return held[k]
 
-        emits = [Emit(out_refs[k], rest[2 * k], rest[2 * k + 1]) for k in range(o)]
+        emits = [Emit(out_refs[k], rest[2 * k], rest[2 * k + 1], outs[k][1] == outs[k][0][0]) for k in range(o)]
         kernel(get, small_refs, *emits, *rest[2 * o :])
         for k in range(n):
             get(k)
         for emit in emits:
-            for copy in emit.copies:
-                copy.wait()
+            emit.finish()
 
     hbm, vmem = pl.BlockSpec(memory_space=pltpu.HBM), pl.BlockSpec(memory_space=pltpu.VMEM)
     space = [pltpu.VMEM(x.shape, x.dtype) for x in ins] + [pltpu.SemaphoreType.DMA((max(n, 1),))]
@@ -132,8 +144,16 @@
     return pairs
 
 
+def row_of(y, xl):
+    return (y & 1) * 4 + xl * 2 + (y >> 1)
+
+
+def spot_of(block):
+    return (block & 1) * 4 + (block >> 2) * 2 + (block >> 1 & 1)
+
+
 def to_output(y, xl, c, xh, z):
-    return (xh * 8 + y * 2 + xl) * 16 + c * 8 + z
+    return (xh * 8 + row_of(y, xl)) * 16 + c * 8 + z
 
 
 def cross_core(y, xl, c, xh, z):
@@ -144,16 +164,11 @@
     return ((((xh * 2 + y % 2) * 2 + xl) * 2 + c) * 2 + y // 2) * 8 + z
 
 
-def window_place(transposed):
-    def there(y, xl, c, xh, z):
-        cross, distance = y // 2, (y % 2 * 2 + xl) * 2 + c
-        if distance > 4 or (transposed and distance not in (1, 2, 3)):
-            return None
-        row = ((xh + cross) % 2) * 8 + (z - 2) % 8
-        column = xh * 8 + (z - 2 + distance) % 8
-        return column * 16 + row if transposed else row * 16 + column
-
-    return there
+def window_place(y, xl, c, xh, z):
+    cross, distance = y // 2, (y % 2 * 2 + xl) * 2 + c
+    row = ((xh + cross) % 2) * 8 + (z - 2) % 8
+    column = xh * 8 + (z - 2 + min(distance, 8 - distance)) % 8
+    return column * 16 + row if distance > 4 else row * 16 + column
 
 
 def order(*values):
@@ -182,7 +197,6 @@
             for k in range(0, count, 4):
                 pieces = [get(which)[:, q * width + 128 : (q + 1) * width] for q in range(k, k + 4)]
                 out.slots[0, :, count * 128 + k * rest : count * 128 + (k + 4) * rest] = jnp.concatenate(pieces, axis=1)
-            out.send(0, 0)
 
     up1, down1 = shift(act, "z", 1), shift(act, "z", -1)
     grad_flip = shift(grad, "xh", 1)
@@ -191,7 +205,6 @@
     up1, down1, rows_out, rows_in = order(up1, down1, *rows)
     up2, down2 = shift(up1, "z", 1), shift(down1, "z", -1)
     rows_out = lax.ppermute(rows_out[0], AXES, pairs_of(cross_core))
-    rows_in = lax.ppermute(rows_in[0], AXES, [(b, a) for a, b in pairs_of(to_output)])
     up2, down2, grad_flip, act_flip = order(up2, down2, grad_flip, act_flip)
     up3, down3 = shift(up2, "z", 1), shift(down2, "z", -1)
 
@@ -204,11 +217,14 @@
             at = 4
 
             def staged(other, place):
-                to_y, to_xl, to_c = other * 2 + place // 4, lax.rem(place // 2, 2), lax.rem(place, 2)
-                return lax.rem(to_c + c, 2) * 8 + lax.rem(to_xl + xl, 2) * 4 + lax.rem(to_y - y + 4, 4)
+                to_y, to_xl, to_c = other * 2 + (place >> 2), place >> 1, place
+                return ((to_c ^ c) & 1) * 8 + ((to_xl ^ xl) & 1) * 4 + ((to_y - y) & 3)
+
+            places = {distance: (z + distance) & 7 for distance in blocks}
+            steps = {distance: (staged(xh, places[distance]), staged(1 - xh, places[distance])) for distance in blocks}
 
             for distance, parts in blocks.items():
-                place = lax.rem(z + distance, 8)
+                place = places[distance]
                 held = [small[at + k][...] for k in range(len(parts))]
                 at += len(parts)
 
@@ -216,20 +232,21 @@
                     values = [dot(piece, small[right][...], (1, 1)) for piece in held]
                     return values[0] if len(values) == 1 else jnp.concatenate(values, axis=0)
 
-                weight_out(place * 2 + xh, product(2))
-                weight_out(place * 2 + 1 - xh, product(3))
-                cov_out(staged(xh, place), product(0))
-                cov_out(staged(1 - xh, place), product(1))
+                weight_out(spot_of(place) * 2 + xh, product(2))
+                weight_out(spot_of(place) * 2 + 1 - xh, product(3))
+                cov_out(steps[distance][0], product(0))
+                cov_out(steps[distance][1], product(1))
 
         shapes = [(chunked, 2 * len(blocks), bf16)] * 2
         flops = 4 * len(blocks) * pair_flops
         return call(kernel, [], shapes, (), [act, act_flip, grad, grad_flip, *pieces], alias, flops=flops)
 
     parts = products({0: [act], 1: [down1], 7: [up1], 2: [down2], 6: [up2]})
-    up3, down3, *parts = order(up3, down3, *parts)
+    rows_in = lax.ppermute(rows_in[0], AXES, [(b, a) for a, b in pairs_of(to_output)])
+    up3, down3, rows_out, *parts = order(up3, down3, rows_out, *parts)
     down4, up4 = shift(down3[:half], "z", -1), shift(up3[half:], "z", 1)
     parts = products({3: [down3], 5: [up3]}, parts)
-    grad_late, *parts = order(grad, *parts)
+    grad_late, rows_in, *parts = order(grad, rows_in, *parts)
     weight_parts, in_parts = products({4: [down4, up4]}, parts)
 
     grad_up1, grad_down1 = shift(grad_late, "z", 1), shift(grad_late, "z", -1)
@@ -266,42 +283,53 @@
         for k in range(got.shape[0]):
             value = unpack(got[k].astype(f32)).astype(bf16)
             j = block(k)
-            whole[pl.ds(pl.multiple_of(j * 128, 128), 128)] = value[:128]
-            whole[pl.ds(pl.multiple_of(count * 128 + j * rest, rest), rest)] = value[128:]
+            first = j * 128
+            second = count * 128 + j * rest
+            if not isinstance(j, int):
+                first, second = pl.multiple_of(first, 128), pl.multiple_of(second, rest)
+            whole[pl.ds(first, 128)] = value[:128]
+            whole[pl.ds(second, rest)] = value[128:]
 
     got = exchange(weight_parts, DP)
     in_sum = pair_sum(in_parts, "c")
-    got, eigs, rows_out, rows_in, grad_up1, grad_down1, in_sum = order(
-        got, eigs, rows_out, rows_in, grad_up1, grad_down1, in_sum
-    )
+    got, in_sum = order(got, in_sum)
 
     def weight_kernel(get, small, out):
         value = (total_of(get(0)) * (1.0 / total_tokens)).astype(bf16)
         c = lax.axis_index("c")
-        wide(value, get(1), out, lambda k: lax.rem(k // 8 + c, 2) * 8 + k % 8)
+        wide(value, get(1), out, lambda k: (k // 8 ^ c) * 8 + k % 8)
 
     (mixed,) = call(weight_kernel, [got, rows_out], [(chunked, count, bf16)], flops=square_flops)
-    got = exchange(pair_sum(mixed, "c"), "z")
+    mixed, grad_up1, grad_down1 = order(pair_sum(mixed, "c"), grad_up1, grad_down1)
+    got = exchange(mixed, "z")
     in_sum = pair_sum(in_sum, "xl")
-    got, in_sum = order(got, in_sum)
+    got, in_sum, eigs, grad_up1, grad_down1 = order(got, in_sum, eigs, grad_up1, grad_down1)
 
     def mixed_kernel(get, small, out):
-        wide(total_of(get(0)).T.astype(bf16), get(1), out, lambda k: k)
+        wide(total_of(get(0)).T.astype(bf16), get(1), out, lambda k: k // 8 * 8 + spot_of(k % 8))
 
     (eigen,) = call(mixed_kernel, [got, rows_in], [(chunked, count, bf16)], flops=square_flops)
     grad_up2, grad_down2 = shift(grad_up1, "z", 1), shift(grad_down1, "z", -1)
     got = exchange(eigen, ROW)
+    in_got = [in_sum[0]] + [shift(in_sum[k], "y", k) for k in range(1, 4)]
+    got, *in_got = order(got, *in_got)
     def eigen_kernel(get, small, out):
         eigs_ref, column_ref = small
         scale = 1.0 / (column_ref[...] * eigs_ref[0:1, :] + damping)
         out.everywhere(total_of(get(0)) * scale)
 
-    (scaled,) = call(eigen_kernel, [got], [((count // 2,) + packed, 1, bf16)], (), [eigs, eigs[1][:, None]])
+    (scaled,) = call(eigen_kernel, [got], [((count // 2,) + packed, count // 2, bf16)], (), [eigs, eigs[1][:, None]])
+    def staged_kernel(get, small, out):
+        total = get(0)[...].astype(f32)
+        for k in range(1, 4):
+            total = total + get(k)[...].astype(f32)
+        out.put(0, unpack(total))
+
+    (in_cov,) = call(staged_kernel, in_got, [((1,) + square, 1, bf16)])
+
     scaled, grad_up2, grad_down2 = order(scaled, grad_up2, grad_down2)
     grad_cross = shift(grad_up2, "xh", 1)
     scaled = exchange(scaled, "z")
-    in_got = [in_sum[0]] + [shift(in_sum[k], "y", k) for k in range(1, 4)]
-    scaled, grad_cross, *in_got = order(scaled, grad_cross, *in_got)
     scaled_other = shift(scaled, "c", 1)
 
     def back_kernel(get, small, out, whole):
@@ -311,18 +339,23 @@
         out.everywhere(dot(get(2)[...], whole[...], (1, 0)).T)
 
     space = [((full, width), bf16)]
-    (back,) = call(back_kernel, [scaled, scaled_other, rows_out], [(chunked, 1, bf16)], (), (), (), space, square_flops)
+    (back,) = call(back_kernel, [scaled, scaled_other, rows_out], [(chunked, count, bf16)], (), (), (), space, square_flops)
+    back, grad_cross, in_cov = order(back, grad_cross, in_cov)
     back = exchange(back, ROW)
+    in_cov = lax.ppermute(in_cov, AXES, pairs_of(swapped))
 
     def cov_kernel(get, small, out):
         c = lax.axis_index("c")
         for cross in range(2):
+            mirrors = {}
             for distance in range(8):
                 index = lax.rem(distance + c, 2) * 8 + cross * 4 + distance // 2
                 if distance < 5:
-                    out(index, dot(get(5 if cross else 0)[...], get(distance)[...], (1, 1)))
+                    value = dot(get(5 if cross else 0)[...], get(distance)[...], (1, 1))
+                    out(index, value)
+                    mirrors[distance] = value
                 else:
-                    out(index, jnp.zeros(square, f32))
+                    out(index, mirrors[8 - distance].T)
 
     window = [grad_up2, grad_up1, grad_late, grad_down1, grad_down2, grad_cross]
     (out_parts,) = call(cov_kernel, window, [(chunked, count, bf16)], flops=10 * pair_flops)
@@ -330,7 +363,7 @@
     back, out_parts = order(back, out_parts)
 
     def last_kernel(get, small, out, whole):
-        stacked(get(0), whole, lambda k: jnp.int32(k))
+        stacked(get(0), whole, lambda k: k // 8 * 8 + row_of(k % 8 // 2, k % 2))
         out.put(0, dot(get(1)[...], whole[...], (1, 0)))
 
     (precond,) = call(
@@ -341,27 +374,17 @@
     def sum_kernel(get, small, out):
         out.put(0, total_of(get(0)))
 
-    def staged_kernel(get, small, out):
-        total = get(0)[...].astype(f32)
-        for k in range(1, 4):
-            total = total + get(k)[...].astype(f32)
-        out.put(0, unpack(total))
-
-    (in_cov,) = call(staged_kernel, in_got, [((1,) + square, 1, bf16)])
-    in_cov = lax.ppermute(in_cov, AXES, pairs_of(swapped))
-    (out_cov,) = call(sum_kernel, [exchange(out_parts, ("y", "xl"))], [((1,) + square, 1, bf16)])
-    out_cov = [lax.ppermute(out_cov, AXES, pairs_of(window_place(mirror))) for mirror in (False, True)]
-
-    def factor(old, *covs):
+    out_got, in_cov = order(exchange(out_parts, ("y", "xl")), in_cov)
+    (out_cov,) = call(sum_kernel, [out_got], [((1,) + square, 1, bf16)])
+    out_cov = lax.ppermute(out_cov, AXES, pairs_of(window_place))
+
+    def factor(old, cov):
         def kernel(get, small, out):
-            cov = small[1][0].astype(f32)
-            if len(covs) > 1:
-                cov = cov + small[2][0].astype(f32).T
-            out.put(0, decay * small[0][0] + ((1.0 - decay) / total_tokens) * cov)
-
-        return call(kernel, [], [(old.shape, 1, f32)], (), [old, *covs])[0]
-
-    return factor(factor_in, in_cov), factor(factor_out, *out_cov), precond
+            out.put(0, decay * small[0][0] + ((1.0 - decay) / total_tokens) * small[1][0].astype(f32))
+
+        return call(kernel, [], [(old.shape, 1, f32)], (), [old, cov])[0]
+
+    return factor(factor_in, in_cov), factor(factor_out, out_cov), precond
 
 
 def solution(mesh):

time: 237 us -> 212 us (0.89)
  starting transfers between devices: 99.9 us -> 85.1 us
  Pallas kernels: 42.8 us -> 35.5 us
    ppermute x23, waiting for transfers between devices: 51.6 us -> 36.8 us  [shift(): lax.ppermute(value, axis, [(i, (i + step) % size) for i in range(size)])]
    ppermute x2 -> x1, starting transfers between devices: 12 us -> 2.05 us  [body(): out_cov = lax.ppermute(out_cov, AXES, pairs_of(window_place))]
    ppermute x1, waiting for transfers between devices: 0.01 us -> 7.66 us  [body(): lax.ppermute(rows_in[0], AXES, [(b, a) for a, b in pairs_of(to_output)])]
    pallas_call x18, Pallas kernels: 42.8 us -> 35.5 us  [call(): pl.pallas_call(wrapped, out_shape=[jax.ShapeDtypeStruct(shape, dtype) for...]
    all_to_all x6, waiting for transfers between devices: 21.1 us -> 28 us  [exchange(): return lax.all_to_all(chunks, axes, 0, 0, tiled=True)]
    ppermute x1, waiting for transfers between devices: 8.82 us -> 3.19 us  [body(): lax.ppermute(jnp.concatenate([eig_in, eig_out], axis=0), AXES, [(b, a) fo...]
    ppermute x1, starting transfers between devices: 6.13 us -> 1.91 us  [body(): lax.ppermute(rows_in[0], AXES, [(b, a) for a, b in pairs_of(to_output)])]
    ppermute x2 -> x1, waiting for transfers between devices: 3.96 us -> 7.84 us  [body(): out_cov = lax.ppermute(out_cov, AXES, pairs_of(window_place))]
  transfers between devices with their start and end apart: 36 -> 35, of which waited for: 19 -> 19; matrix products, arithmetic and copies ran while one was open for 0% -> 0% of each run, Pallas kernels for 14% -> 14%
where the time goes in v2:
time: 212 us; the launch traced here: 211 us
  starting transfers between devices  85.1 us (40%)
  waiting for transfers between devices  84.8 us (40%)
  Pallas kernels  35.5 us (17%)
  local copies, waits for them, and re-layouts  4.39 us (2%)
    ppermute x23, waiting for transfers between devices, shift(): lax.ppermute(value, axis, [(i, (i + step) % size) for i in range(size)])  36.8 us
    pallas_call x18, Pallas kernels, call(): pl.pallas_call(wrapped, out_shape=[jax.ShapeDtypeStruct(shape, dtype) for...  35.5 us
    ppermute x23, starting transfers between devices, shift(): lax.ppermute(value, axis, [(i, (i + step) % size) for i in range(size)])  34 us
    all_to_all x6, starting transfers between devices, exchange(): return lax.all_to_all(chunks, axes, 0, 0, tiled=True)  33.4 us
    all_to_all x6, waiting for transfers between devices, exchange(): return lax.all_to_all(chunks, axes, 0, 0, tiled=True)  28 us
    ppermute x1, waiting for transfers between devices, body(): out_cov = lax.ppermute(out_cov, AXES, pairs_of(window_place))  7.84 us
    ppermute x1, waiting for transfers between devices, body(): lax.ppermute(rows_in[0], AXES, [(b, a) for a, b in pairs_of(to_output)])  7.66 us
    ppermute x1, starting transfers between devices, body(): in_cov = lax.ppermute(in_cov, AXES, pairs_of(swapped))  6.27 us
  transfers between devices with their start and end apart: 35, of which 19 were waited for; matrix products, arithmetic and copies ran while one was open for 0% of the time, Pallas kernels for 14%

profile of v2, /device:TPU:6, one launch (start us, length us, event | category | flops | bytes accessed | tf_op | source)
XLA Modules:
  0.0 210.7 jit_solution(3475354800989886748)
XLA Ops:
  2.6 4.0 %collective-permute-start.1 = (bf16[160,2048]{1,0:T(8,128)(2,1)}, bf16[160,2048]{1,0:T(8,128)(2,1)S(1)}, u32[]{:S(2)}, u32[]{:S(2)}) collective-permute-start(bf16[160,2048]{1,0:T(8,128)(2,1)} %bitcast.28), channel_id=1, source_target_pairs={{0,7},{1,0},{2,1},{3,2},{4,3},{5,4},{6,5},{7,6},{8,15},{9,8},{10,9... | collective-permute-start | bytes 1966088 | tf_op jit(solution)/shard_map/ppermute | solution.py:126
  8.1 2.1 %collective-permute-start.4 = (bf16[160,2048]{1,0:T(8,128)(2,1)}, bf16[160,2048]{1,0:T(8,128)(2,1)S(1)}, u32[]{:S(2)}, u32[]{:S(2)}) collective-permute-start(bf16[160,2048]{1,0:T(8,128)(2,1)} %bitcast.20), channel_id=1, source_target_pairs={{0,8},{8,0},{1,9},{9,1},{2,10},{10,2},{3,11},{11,3},{4,12},{12,4},... | collective-permute-start | bytes 1966088 | tf_op jit(solution)/shard_map/ppermute | solution.py:126
  13.7 7.8 %collective-permute-done.refs_6_ = bf16[160,2048]{1,0:T(8,128)(2,1)S(1)} collective-permute-done((bf16[160,2048]{1,0:T(8,128)(2,1)}, bf16[160,2048]{1,0:T(8,128)(2,1)S(1)}, u32[]{:S(2)}, u32[]{:S(2)}) %collective-permute-start) | collective-permute-done | bytes 655392 | tf_op jit(solution)/shard_map/ppermute | solution.py:126
  21.5 3.2 %collective-permute-start.3 = (bf16[160,2048]{1,0:T(8,128)(2,1)S(1)}, bf16[160,2048]{1,0:T(8,128)(2,1)S(1)}, u32[]{:S(2)}, u32[]{:S(2)}) collective-permute-start(bf16[160,2048]{1,0:T(8,128)(2,1)S(1)} %collective-permute-done.1.refs_5_), channel_id=1, source_target_pairs={{0,7},{1,0},{2,1},{3,2},{4,3},{5,4},{6,5},{7,6},{8,15},{9,8},{10,9... | collective-permute-start | bytes 1966088 | tf_op jit(solution)/shard_map/ppermute | solution.py:126
  26.7 13.4 %collective-permute-done.4.refs_3_ = bf16[160,2048]{1,0:T(8,128)(2,1)S(1)} collective-permute-done((bf16[160,2048]{1,0:T(8,128)(2,1)}, bf16[160,2048]{1,0:T(8,128)(2,1)S(1)}, u32[]{:S(2)}, u32[]{:S(2)}) %collective-permute-start.4) | collective-permute-done | bytes 655392 | tf_op jit(solution)/shard_map/ppermute | solution.py:126
  40.5 2.9 %collective-permute-start.7 = (bf16[160,2048]{1,0:T(8,128)(2,1)S(1)}, bf16[160,2048]{1,0:T(8,128)(2,1)S(1)}, u32[]{:S(2)}, u32[]{:S(2)}) collective-permute-start(bf16[160,2048]{1,0:T(8,128)(2,1)S(1)} %collective-permute-done.3.refs_7_), channel_id=1, source_target_pairs={{0,7},{1,0},{2,1},{3,2},{4,3},{5,4},{6,5},{7,6},{8,15},{9,8},{10,9... | collective-permute-start | bytes 1966088 | tf_op jit(solution)/shard_map/ppermute | solution.py:126
  45.3 8.3 %shard_map.104 = (bf16[16,200,128]{2,1,0:T(8,128)(2,1)}, bf16[16,200,128]{2,1,0:T(8,128)(2,1)S(1)}) custom-call(bf16[160,2048]{1,0:T(8,128)(2,1)S(1)} %bitcast.30, bf16[160,2048]{1,0:T(8,128)(2,1)S(1)} %collective-permute-done.5.refs_1_, bf16[160,2048]{1,0:T(8,128)(2,1)S(1)} %bitcast.21, bf16[160,2048]{1,0:T(8,128)(2,1)S(1)} %collective-permute-done.4.refs_3_, ...), custom_call_target="tpu_custom_call" | custom-call | flops 2097152000 | tf_op jit(solution)/shard_map/pallas_call | solution.py:112
  56.5 2.2 %collective-permute-start.9 = (bf16[80,2048]{1,0:T(8,128)(2,1)S(1)}, bf16[80,2048]{1,0:T(8,128)(2,1)S(1)}, u32[]{:S(2)}, u32[]{:S(2)}) collective-permute-start(bf16[80,2048]{1,0:T(8,128)(2,1)S(1)} %slice.45), channel_id=1, source_target_pairs={{0,7},{1,0},{2,1},{3,2},{4,3},{5,4},{6,5},{7,6},{8,15},{9,8},{10,9... | collective-permute-start | bytes 983048 | tf_op jit(solution)/shard_map/ppermute | solution.py:126
  58.7 3.5 %shard_map.105 = (bf16[16,200,128]{2,1,0:T(8,128)(2,1)}, bf16[16,200,128]{2,1,0:T(8,128)(2,1)S(1)}) custom-call(bf16[160,2048]{1,0:T(8,128)(2,1)S(1)} %bitcast.32, bf16[160,2048]{1,0:T(8,128)(2,1)S(1)} %collective-permute-done.5.refs_1_, bf16[160,2048]{1,0:T(8,128)(2,1)S(1)} %bitcast.22, ...), custom_call_target="tpu_custom_call", output_to_operand_aliasing={{0}: (6, {}), {1}: (7, {})} | custom-call | flops 838860800 | tf_op jit(solution)/shard_map/pallas_call | solution.py:112
  62.2 7.7 %collective-permute-done.11.refs_1_ = bf16[160,2560]{1,0:T(8,128)(2,1)S(1)} collective-permute-done((bf16[160,2560]{1,0:T(8,128)(2,1)S(1)}, bf16[160,2560]{1,0:T(8,128)(2,1)S(1)}, u32[]{:S(2)}, u32[]{:S(2)}) %collective-permute-start.11) | collective-permute-done | bytes 819232 | tf_op jit(solution)/shard_map/ppermute | solution.py:245
  69.9 2.5 %shard_map.106 = (bf16[16,200,128]{2,1,0:T(8,128)(2,1)}, bf16[16,200,128]{2,1,0:T(8,128)(2,1)S(1)}) custom-call(bf16[160,2048]{1,0:T(8,128)(2,1)S(1)} %bitcast.33, bf16[160,2048]{1,0:T(8,128)(2,1)S(1)} %collective-permute-done.5.refs_1_, bf16[160,2048]{1,0:T(8,128)(2,1)S(1)} %bitcast.23, ...), custom_call_target="tpu_custom_call", output_to_operand_aliasing={{0}: (6, {}), {1}: (7, {})} | custom-call | flops 419430400 | tf_op jit(solution)/shard_map/pallas_call | solution.py:112
  72.4 4.2 %all-to-all-start = ((bf16[16,200,128]{2,1,0:T(8,128)(2,1)}), bf16[16,200,128]{2,1,0:T(8,128)(2,1)S(1)}, u32[]{:S(2)}, u32[]{:S(2)}) async-start(bf16[16,200,128]{2,1,0:T(8,128)(2,1)} %get-tuple-element.73), calls=%async_computation | async-start | bytes 1638400 | tf_op jit(solution)/shard_map/all_to_all | solution.py:130
  77.0 3.2 %collective-permute-start.15 = (bf16[160,2048]{1,0:T(8,128)(2,1)S(1)}, bf16[160,2048]{1,0:T(8,128)(2,1)}, u32[]{:S(2)}, u32[]{:S(2)}) collective-permute-start(bf16[160,2048]{1,0:T(8,128)(2,1)S(1)} %bitcast.25), channel_id=1, source_target_pairs={{0,7},{1,0},{2,1},{3,2},{4,3},{5,4},{6,5},{7,6},{8,15},{9,8},{10,9... | collective-permute-start | bytes 1966088 | tf_op jit(solution)/shard_map/ppermute | solution.py:126
  81.0 8.6 %all-to-all-done.refs_0_ = bf16[16,200,128]{2,1,0:T(8,128)(2,1)S(1)} async-done(((bf16[16,200,128]{2,1,0:T(8,128)(2,1)}), bf16[16,200,128]{2,1,0:T(8,128)(2,1)S(1)}, u32[]{:S(2)}, u32[]{:S(2)}) %all-to-all-start) | async-done | bytes 819232 | tf_op jit(solution)/shard_map/all_to_all | solution.py:130
  95.3 6.2 %all-to-all-start.1 = ((bf16[8,200,128]{2,1,0:T(8,128)(2,1)}), bf16[8,200,128]{2,1,0:T(8,128)(2,1)S(1)}, u32[]{:S(2)}, u32[]{:S(2)}) async-start(bf16[8,200,128]{2,1,0:T(8,128)(2,1)} %shard_map.109), calls=%async_computation.1 | async-start | bytes 819200 | tf_op jit(solution)/shard_map/all_to_all | solution.py:130
  104.2 3.4 %collective-permute-done.16.refs_1_ = bf16[4,200,128]{2,1,0:T(8,128)(2,1)S(1)} collective-permute-done((bf16[4,200,128]{2,1,0:T(8,128)(2,1)S(1)}, bf16[4,200,128]{2,1,0:T(8,128)(2,1)S(1)}, u32[]{:S(2)}, u32[]{:S(2)}) %collective-permute-start.16) | collective-permute-done | bytes 204832 | tf_op jit(solution)/shard_map/ppermute | solution.py:126
  108.5 3.2 %collective-permute-done.17.refs_1_ = f32[2,160]{1,0:T(2,128)S(1)} collective-permute-done((f32[2,160]{1,0:T(2,128)S(1)}, f32[2,160]{1,0:T(2,128)S(1)}, u32[]{:S(2)}, u32[]{:S(2)}) %collective-permute-start.17) | collective-permute-done | bytes 1312 | tf_op jit(solution)/shard_map/ppermute | solution.py:253
  111.7 4.3 %all-to-all-done.1.refs_0_ = bf16[8,200,128]{2,1,0:T(8,128)(2,1)S(1)} async-done(((bf16[8,200,128]{2,1,0:T(8,128)(2,1)}), bf16[8,200,128]{2,1,0:T(8,128)(2,1)S(1)}, u32[]{:S(2)}, u32[]{:S(2)}) %all-to-all-start.1) | async-done | bytes 409632 | tf_op jit(solution)/shard_map/all_to_all | solution.py:130
  118.0 7.0 %all-to-all-start.2 = ((bf16[16,200,128]{2,1,0:T(8,128)(2,1)}), bf16[16,200,128]{2,1,0:T(8,128)(2,1)S(1)}, u32[]{:S(2)}, u32[]{:S(2)}) async-start(bf16[16,200,128]{2,1,0:T(8,128)(2,1)} %shard_map.111), calls=%async_computation.2 | async-start | bytes 1638400 | tf_op jit(solution)/shard_map/all_to_all | solution.py:130
  125.5 2.7 %collective-permute-start.22 = (bf16[160,2048]{1,0:T(8,128)(2,1)}, bf16[160,2048]{1,0:T(8,128)(2,1)}, u32[]{:S(2)}, u32[]{:S(2)}) collective-permute-start(bf16[160,2048]{1,0:T(8,128)(2,1)} %collective-permute-done.15.refs_3_), channel_id=1, source_target_pairs={{0,7},{1,0},{2,1},{3,2},{4,3},{5,4},{6,5},{7,6},{8,15},{9,8},{10,9... | collective-permute-start | bytes 1966088 | tf_op jit(solution)/shard_map/ppermute | solution.py:126
  130.3 2.7 %collective-permute-start.19 = (bf16[200,128]{1,0:T(8,128)(2,1)S(1)}, bf16[200,128]{1,0:T(8,128)(2,1)S(1)}, u32[]{:S(2)}, u32[]{:S(2)}) collective-permute-start(bf16[200,128]{1,0:T(8,128)(2,1)S(1)} %get-tuple-element.112), channel_id=1, source_target_pairs={{0,128},{64,192},{128,0},{192,64},{1,129},{65,193},{129,1},{193,65... | collective-permute-start | bytes 153608 | tf_op jit(solution)/shard_map/ppermute | solution.py:126
  135.3 2.5 %collective-permute-done.19.refs_2_ = bf16[200,128]{1,0:T(8,128)(2,1)S(1)} collective-permute-done((bf16[200,128]{1,0:T(8,128)(2,1)S(1)}, bf16[200,128]{1,0:T(8,128)(2,1)S(1)}, u32[]{:S(2)}, u32[]{:S(2)}) %collective-permute-start.19) | collective-permute-done | bytes 51232 | tf_op jit(solution)/shard_map/ppermute | solution.py:126
  140.5 4.2 %all-to-all-start.3 = ((bf16[8,200,128]{2,1,0:T(8,128)(2,1)}), bf16[8,200,128]{2,1,0:T(8,128)(2,1)S(1)}, u32[]{:S(2)}, u32[]{:S(2)}) async-start(bf16[8,200,128]{2,1,0:T(8,128)(2,1)} %shard_map.112), calls=%async_computation.3 | async-start | bytes 819200 | tf_op jit(solution)/shard_map/all_to_all | solution.py:130
  146.2 11.0 %all-to-all-done.3.refs_0_ = bf16[8,200,128]{2,1,0:T(8,128)(2,1)S(1)} async-done(((bf16[8,200,128]{2,1,0:T(8,128)(2,1)}), bf16[8,200,128]{2,1,0:T(8,128)(2,1)S(1)}, u32[]{:S(2)}, u32[]{:S(2)}) %all-to-all-start.3) | async-done | bytes 409632 | tf_op jit(solution)/shard_map/all_to_all | solution.py:130
  158.9 2.4 %shard_map.113 = bf16[16,200,128]{2,1,0:T(8,128)(2,1)} custom-call(bf16[8,200,128]{2,1,0:T(8,128)(2,1)S(1)} %all-to-all-done.3.refs_0_, bf16[8,200,128]{2,1,0:T(8,128)(2,1)S(1)} %collective-permute-done.23.refs_1_, bf16[160,2560]{1,0:T(8,128)(2,1)S(1)} %collective-permute-done.8.refs_1_.refs_2_), custom_call_target="tpu_custom_call" | custom-call | flops 131072000 | bytes 1638400 | tf_op jit(solution)/shard_map/pallas_call | solution.py:112
  161.4 6.9 %all-to-all-start.4 = ((bf16[16,200,128]{2,1,0:T(8,128)(2,1)}), bf16[16,200,128]{2,1,0:T(8,128)(2,1)S(1)}, u32[]{:S(2)}, u32[]{:S(2)}) async-start(bf16[16,200,128]{2,1,0:T(8,128)(2,1)} %shard_map.113), calls=%async_computation.4 | async-start | bytes 1638400 | tf_op jit(solution)/shard_map/all_to_all | solution.py:130
  168.3 5.6 %shard_map.115 = bf16[16,200,128]{2,1,0:T(8,128)(2,1)S(1)} custom-call(bf16[160,2048]{1,0:T(8,128)(2,1)} %collective-permute-done.21.refs_0_, bf16[160,2048]{1,0:T(8,128)(2,1)} %collective-permute-done.14.refs_1_, bf16[160,2048]{1,0:T(8,128)(2,1)S(1)} %bitcast.26, bf16[160,2048]{1,0:T(8,128)(2,1)} %collective-permute-done.15.refs_3_, ...), custom_call_target="tpu_custom_call" | custom-call | flops 1048576000 | bytes 3932160 | tf_op jit(solution)/shard_map/pallas_call | solution.py:112
  177.1 4.2 %all-to-all-done.4.refs_0_ = bf16[16,200,128]{2,1,0:T(8,128)(2,1)S(1)} async-done(((bf16[16,200,128]{2,1,0:T(8,128)(2,1)}), bf16[16,200,128]{2,1,0:T(8,128)(2,1)S(1)}, u32[]{:S(2)}, u32[]{:S(2)}) %all-to-all-start.4) | async-done | bytes 819232 | tf_op jit(solution)/shard_map/all_to_all | solution.py:130
  181.3 4.9 %all-to-all-start.5 = ((bf16[8,200,128]{2,1,0:T(8,128)(2,1)}), bf16[8,200,128]{2,1,0:T(8,128)(2,1)S(1)}, u32[]{:S(2)}, u32[]{:S(2)}) async-start(bf16[8,200,128]{2,1,0:T(8,128)(2,1)} %shard_map.116), calls=%async_computation.5 | async-start | bytes 819200 | tf_op jit(solution)/shard_map/all_to_all | solution.py:130
  186.2 6.3 %collective-permute-start.26 = (bf16[1,160,160]{2,1,0:T(8,128)(2,1)S(1)}, bf16[1,160,160]{2,1,0:T(8,128)(2,1)S(1)}, u32[]{:S(2)}, u32[]{:S(2)}) collective-permute-start(bf16[1,160,160]{2,1,0:T(8,128)(2,1)S(1)} %shard_map.114), channel_id=1, source_target_pairs={{0,0},{1,1},{2,2},{3,3},{4,4},{5,5},{6,6},{7,7},{8,128},{9,129},{1... | collective-permute-start | bytes 153608 | tf_op jit(solution)/shard_map/ppermute | solution.py:345
  193.4 3.6 %collective-permute-start.28 = (bf16[1,160,160]{2,1,0:T(8,128)(2,1)S(1)}, bf16[1,160,160]{2,1,0:T(8,128)(2,1)S(1)}, u32[]{:S(2)}, u32[]{:S(2)}) collective-permute-start(bf16[1,160,160]{2,1,0:T(8,128)(2,1)S(1)} %shard_map.120), channel_id=1, source_target_pairs={{0,0},{1,1},{2,2},{3,3},{4,4},{5,5},{6,6},{7,7},{8,128},{9,129},{1... | collective-permute-start | bytes 153608 | tf_op jit(solution)/shard_map/ppermute | solution.py:372
  201.5 7.8 %collective-permute-done.27.refs_1_ = bf16[1,160,160]{2,1,0:T(8,128)(2,1)S(1)} collective-permute-done((bf16[1,160,160]{2,1,0:T(8,128)(2,1)S(1)}, bf16[1,160,160]{2,1,0:T(8,128)(2,1)S(1)}, u32[]{:S(2)}, u32[]{:S(2)}) %collective-permute-start.27) | collective-permute-done | bytes 51232 | tf_op jit(solution)/shard_map/ppermute | solution.py:379
  (87 shorter events, 47.3 us)
Async XLA Ops:
  0.6 20.9 %collective-permute-start = (bf16[160,2048]{1,0:T(8,128)(2,1)}, bf16[160,2048]{1,0:T(8,128)(2,1)S(1)}, u32[]{:S(2)}, u32[]{:S(2)}) collective-permute-start(bf16[160,2048]{1,0:T(8,128)(2,1)} %bitcast.27), channel_id=1, source_target_pairs={{0,1},{1,2},{2,3},{3,4},{4,5},{5,6},{6,7},{7,0},{8,9},{9,10},{10,1... | collective-permute-start | bytes 1966088 | tf_op jit(solution)/shard_map/ppermute | solution.py:126
  2.6 18.9 %collective-permute-start.1 = (bf16[160,2048]{1,0:T(8,128)(2,1)}, bf16[160,2048]{1,0:T(8,128)(2,1)S(1)}, u32[]{:S(2)}, u32[]{:S(2)}) collective-permute-start(bf16[160,2048]{1,0:T(8,128)(2,1)} %bitcast.28), channel_id=1, source_target_pairs={{0,7},{1,0},{2,1},{3,2},{4,3},{5,4},{6,5},{7,6},{8,15},{9,8},{10,9... | collective-permute-start | bytes 1966088 | tf_op jit(solution)/shard_map/ppermute | solution.py:126
  6.7 20.0 %collective-permute-start.5 = (bf16[160,2048]{1,0:T(8,128)(2,1)}, bf16[160,2048]{1,0:T(8,128)(2,1)S(1)}, u32[]{:S(2)}, u32[]{:S(2)}) collective-permute-start(bf16[160,2048]{1,0:T(8,128)(2,1)} %bitcast.29), channel_id=1, source_target_pairs={{0,8},{8,0},{1,9},{9,1},{2,10},{10,2},{3,11},{11,3},{4,12},{12,4},... | collective-permute-start | bytes 1966088 | tf_op jit(solution)/shard_map/ppermute | solution.py:126
  8.1 32.0 %collective-permute-start.4 = (bf16[160,2048]{1,0:T(8,128)(2,1)}, bf16[160,2048]{1,0:T(8,128)(2,1)S(1)}, u32[]{:S(2)}, u32[]{:S(2)}) collective-permute-start(bf16[160,2048]{1,0:T(8,128)(2,1)} %bitcast.20), channel_id=1, source_target_pairs={{0,8},{8,0},{1,9},{9,1},{2,10},{10,2},{3,11},{11,3},{4,12},{12,4},... | collective-permute-start | bytes 1966088 | tf_op jit(solution)/shard_map/ppermute | solution.py:126
  21.5 18.6 %collective-permute-start.2 = (bf16[160,2048]{1,0:T(8,128)(2,1)S(1)}, bf16[160,2048]{1,0:T(8,128)(2,1)S(1)}, u32[]{:S(2)}, u32[]{:S(2)}) collective-permute-start(bf16[160,2048]{1,0:T(8,128)(2,1)S(1)} %collective-permute-done.refs_6_), channel_id=1, source_target_pairs={{0,1},{1,2},{2,3},{3,4},{4,5},{5,6},{6,7},{7,0},{8,9},{9,10},{10,1... | collective-permute-start | bytes 1966088 | tf_op jit(solution)/shard_map/ppermute | solution.py:126
  21.5 18.6 %collective-permute-start.3 = (bf16[160,2048]{1,0:T(8,128)(2,1)S(1)}, bf16[160,2048]{1,0:T(8,128)(2,1)S(1)}, u32[]{:S(2)}, u32[]{:S(2)}) collective-permute-start(bf16[160,2048]{1,0:T(8,128)(2,1)S(1)} %collective-permute-done.1.refs_5_), channel_id=1, source_target_pairs={{0,7},{1,0},{2,1},{3,2},{4,3},{5,4},{6,5},{7,6},{8,15},{9,8},{10,9... | collective-permute-start | bytes 1966088 | tf_op jit(solution)/shard_map/ppermute | solution.py:126
  24.7 28.8 %collective-permute-start.8 = (bf16[160,2560]{1,0:T(8,128)(2,1)S(1)}, bf16[160,2560]{1,0:T(8,128)(2,1)S(1)}, u32[]{:S(2)}, u32[]{:S(2)}) collective-permute-start(bf16[160,2560]{1,0:T(8,128)(2,1)S(1)} %bitcast.37), channel_id=1, source_target_pairs={{0,0},{1,1},{2,2},{3,3},{4,4},{5,5},{6,6},{7,7},{8,16},{9,17},{10,... | collective-permute-start | bytes 2457608 | tf_op jit(solution)/shard_map/ppermute | solution.py:207
  40.1 15.0 %collective-permute-start.6 = (bf16[160,2048]{1,0:T(8,128)(2,1)S(1)}, bf16[160,2048]{1,0:T(8,128)(2,1)S(1)}, u32[]{:S(2)}, u32[]{:S(2)}) collective-permute-start(bf16[160,2048]{1,0:T(8,128)(2,1)S(1)} %collective-permute-done.2.refs_8_), channel_id=1, source_target_pairs={{0,1},{1,2},{2,3},{3,4},{4,5},{5,6},{6,7},{7,0},{8,9},{9,10},{10,1... | collective-permute-start | bytes 1966088 | tf_op jit(solution)/shard_map/ppermute | solution.py:126
  40.5 14.6 %collective-permute-start.7 = (bf16[160,2048]{1,0:T(8,128)(2,1)S(1)}, bf16[160,2048]{1,0:T(8,128)(2,1)S(1)}, u32[]{:S(2)}, u32[]{:S(2)}) collective-permute-start(bf16[160,2048]{1,0:T(8,128)(2,1)S(1)} %collective-permute-done.3.refs_7_), channel_id=1, source_target_pairs={{0,7},{1,0},{2,1},{3,2},{4,3},{5,4},{6,5},{7,6},{8,15},{9,8},{10,9... | collective-permute-start | bytes 1966088 | tf_op jit(solution)/shard_map/ppermute | solution.py:126
  43.3 26.6 %collective-permute-start.11 = (bf16[160,2560]{1,0:T(8,128)(2,1)S(1)}, bf16[160,2560]{1,0:T(8,128)(2,1)S(1)}, u32[]{:S(2)}, u32[]{:S(2)}) collective-permute-start(bf16[160,2560]{1,0:T(8,128)(2,1)S(1)} %bitcast.36), channel_id=1, source_target_pairs={{0,0},{1,1},{2,2},{3,3},{4,4},{5,5},{6,6},{7,7},{128,8},{129,9},{1... | collective-permute-start | bytes 2457608 | tf_op jit(solution)/shard_map/ppermute | solution.py:245
  55.1 14.7 %collective-permute-start.10 = (bf16[80,2048]{1,0:T(8,128)(2,1)S(1)}, bf16[80,2048]{1,0:T(8,128)(2,1)S(1)}, u32[]{:S(2)}, u32[]{:S(2)}) collective-permute-start(bf16[80,2048]{1,0:T(8,128)(2,1)S(1)} %slice.46), channel_id=1, source_target_pairs={{0,1},{1,2},{2,3},{3,4},{4,5},{5,6},{6,7},{7,0},{8,9},{9,10},{10,1... | collective-permute-start | bytes 983048 | tf_op jit(solution)/shard_map/ppermute | solution.py:126
  56.5 13.4 %collective-permute-start.9 = (bf16[80,2048]{1,0:T(8,128)(2,1)S(1)}, bf16[80,2048]{1,0:T(8,128)(2,1)S(1)}, u32[]{:S(2)}, u32[]{:S(2)}) collective-permute-start(bf16[80,2048]{1,0:T(8,128)(2,1)S(1)} %slice.45), channel_id=1, source_target_pairs={{0,7},{1,0},{2,1},{3,2},{4,3},{5,4},{6,5},{7,6},{8,15},{9,8},{10,9... | collective-permute-start | bytes 983048 | tf_op jit(solution)/shard_map/ppermute | solution.py:126
  72.4 17.2 %all-to-all-start = ((bf16[16,200,128]{2,1,0:T(8,128)(2,1)}), bf16[16,200,128]{2,1,0:T(8,128)(2,1)S(1)}, u32[]{:S(2)}, u32[]{:S(2)}) async-start(bf16[16,200,128]{2,1,0:T(8,128)(2,1)} %get-tuple-element.73), calls=%async_computation | async-start | bytes 1638400 | tf_op jit(solution)/shard_map/all_to_all | solution.py:130
  76.7 3.5 %collective-permute-start.12 = (bf16[8,200,128]{2,1,0:T(8,128)(2,1)S(1)}, bf16[8,200,128]{2,1,0:T(8,128)(2,1)S(1)}, u32[]{:S(2)}, u32[]{:S(2)}) collective-permute-start(bf16[8,200,128]{2,1,0:T(8,128)(2,1)S(1)} %get-tuple-element.107), channel_id=1, source_target_pairs={{0,16},{16,0},{1,17},{17,1},{2,18},{18,2},{3,19},{19,3},{4,20},{20... | collective-permute-start | bytes 1228808 | tf_op jit(solution)/shard_map/ppermute | solution.py:126
  77.0 18.3 %collective-permute-start.14 = (bf16[160,2048]{1,0:T(8,128)(2,1)S(1)}, bf16[160,2048]{1,0:T(8,128)(2,1)}, u32[]{:S(2)}, u32[]{:S(2)}) collective-permute-start(bf16[160,2048]{1,0:T(8,128)(2,1)S(1)} %bitcast.24), channel_id=1, source_target_pairs={{0,1},{1,2},{2,3},{3,4},{4,5},{5,6},{6,7},{7,0},{8,9},{9,10},{10,1... | collective-permute-start | bytes 1966088 | tf_op jit(solution)/shard_map/ppermute | solution.py:126
  77.0 18.3 %collective-permute-start.15 = (bf16[160,2048]{1,0:T(8,128)(2,1)S(1)}, bf16[160,2048]{1,0:T(8,128)(2,1)}, u32[]{:S(2)}, u32[]{:S(2)}) collective-permute-start(bf16[160,2048]{1,0:T(8,128)(2,1)S(1)} %bitcast.25), channel_id=1, source_target_pairs={{0,7},{1,0},{2,1},{3,2},{4,3},{5,4},{6,5},{7,6},{8,15},{9,8},{10,9... | collective-permute-start | bytes 1966088 | tf_op jit(solution)/shard_map/ppermute | solution.py:126
  95.3 20.7 %all-to-all-start.1 = ((bf16[8,200,128]{2,1,0:T(8,128)(2,1)}), bf16[8,200,128]{2,1,0:T(8,128)(2,1)S(1)}, u32[]{:S(2)}, u32[]{:S(2)}) async-start(bf16[8,200,128]{2,1,0:T(8,128)(2,1)} %shard_map.109), calls=%async_computation.1 | async-start | bytes 819200 | tf_op jit(solution)/shard_map/all_to_all | solution.py:130
  101.5 6.1 %collective-permute-start.16 = (bf16[4,200,128]{2,1,0:T(8,128)(2,1)S(1)}, bf16[4,200,128]{2,1,0:T(8,128)(2,1)S(1)}, u32[]{:S(2)}, u32[]{:S(2)}) collective-permute-start(bf16[4,200,128]{2,1,0:T(8,128)(2,1)S(1)} %get-tuple-element.109), channel_id=1, source_target_pairs={{0,32},{32,0},{1,33},{33,1},{2,34},{34,2},{3,35},{35,3},{4,36},{36... | collective-permute-start | bytes 614408 | tf_op jit(solution)/shard_map/ppermute | solution.py:126
  102.3 9.4 %collective-permute-start.17 = (f32[2,160]{1,0:T(2,128)S(1)}, f32[2,160]{1,0:T(2,128)S(1)}, u32[]{:S(2)}, u32[]{:S(2)}) collective-permute-start(f32[2,160]{1,0:T(2,128)S(1)} %pad_maximum_fusion), channel_id=1, source_target_pairs={{0,0},{1,1},{2,2},{3,3},{4,4},{5,5},{6,6},{7,7},{128,8},{129,9},{1... | collective-permute-start | bytes 3848 | tf_op jit(solution)/shard_map/ppermute | solution.py:253
  118.0 19.8 %all-to-all-start.2 = ((bf16[16,200,128]{2,1,0:T(8,128)(2,1)}), bf16[16,200,128]{2,1,0:T(8,128)(2,1)S(1)}, u32[]{:S(2)}, u32[]{:S(2)}) async-start(bf16[16,200,128]{2,1,0:T(8,128)(2,1)} %shard_map.111), calls=%async_computation.2 | async-start | bytes 1638400 | tf_op jit(solution)/shard_map/all_to_all | solution.py:130
  125.0 15.5 %collective-permute-start.21 = (bf16[160,2048]{1,0:T(8,128)(2,1)}, bf16[160,2048]{1,0:T(8,128)(2,1)}, u32[]{:S(2)}, u32[]{:S(2)}) collective-permute-start(bf16[160,2048]{1,0:T(8,128)(2,1)} %collective-permute-done.14.refs_1_), channel_id=1, source_target_pairs={{0,1},{1,2},{2,3},{3,4},{4,5},{5,6},{6,7},{7,0},{8,9},{9,10},{10,1... | collective-permute-start | bytes 1966088 | tf_op jit(solution)/shard_map/ppermute | solution.py:126
  125.5 15.0 %collective-permute-start.22 = (bf16[160,2048]{1,0:T(8,128)(2,1)}, bf16[160,2048]{1,0:T(8,128)(2,1)}, u32[]{:S(2)}, u32[]{:S(2)}) collective-permute-start(bf16[160,2048]{1,0:T(8,128)(2,1)} %collective-permute-done.15.refs_3_), channel_id=1, source_target_pairs={{0,7},{1,0},{2,1},{3,2},{4,3},{5,4},{6,5},{7,6},{8,15},{9,8},{10,9... | collective-permute-start | bytes 1966088 | tf_op jit(solution)/shard_map/ppermute | solution.py:126
  128.9 6.5 %collective-permute-start.18 = (bf16[200,128]{1,0:T(8,128)(2,1)}, bf16[200,128]{1,0:T(8,128)(2,1)S(1)}, u32[]{:S(2)}, u32[]{:S(2)}) collective-permute-start(bf16[200,128]{1,0:T(8,128)(2,1)} %get-tuple-element.113), channel_id=1, source_target_pairs={{0,64},{64,128},{128,192},{192,0},{1,65},{65,129},{129,193},{193,1... | collective-permute-start | bytes 153608 | tf_op jit(solution)/shard_map/ppermute | solution.py:126
  130.3 7.5 %collective-permute-start.19 = (bf16[200,128]{1,0:T(8,128)(2,1)S(1)}, bf16[200,128]{1,0:T(8,128)(2,1)S(1)}, u32[]{:S(2)}, u32[]{:S(2)}) collective-permute-start(bf16[200,128]{1,0:T(8,128)(2,1)S(1)} %get-tuple-element.112), channel_id=1, source_target_pairs={{0,128},{64,192},{128,0},{192,64},{1,129},{65,193},{129,1},{193,65... | collective-permute-start | bytes 153608 | tf_op jit(solution)/shard_map/ppermute | solution.py:126
  133.0 4.8 %collective-permute-start.20 = (bf16[200,128]{1,0:T(8,128)(2,1)S(1)}, bf16[200,128]{1,0:T(8,128)(2,1)S(1)}, u32[]{:S(2)}, u32[]{:S(2)}) collective-permute-start(bf16[200,128]{1,0:T(8,128)(2,1)S(1)} %get-tuple-element.111), channel_id=1, source_target_pairs={{0,192},{64,0},{128,64},{192,128},{1,193},{65,1},{129,65},{193,129... | collective-permute-start | bytes 153608 | tf_op jit(solution)/shard_map/ppermute | solution.py:126
  140.5 16.7 %all-to-all-start.3 = ((bf16[8,200,128]{2,1,0:T(8,128)(2,1)}), bf16[8,200,128]{2,1,0:T(8,128)(2,1)S(1)}, u32[]{:S(2)}, u32[]{:S(2)}) async-start(bf16[8,200,128]{2,1,0:T(8,128)(2,1)} %shard_map.112), calls=%async_computation.3 | async-start | bytes 819200 | tf_op jit(solution)/shard_map/all_to_all | solution.py:130
  144.8 16.6 %collective-permute-start.24 = (bf16[160,2048]{1,0:T(8,128)(2,1)}, bf16[160,2048]{1,0:T(8,128)(2,1)}, u32[]{:S(2)}, u32[]{:S(2)}) collective-permute-start(bf16[160,2048]{1,0:T(8,128)(2,1)} %collective-permute-done.21.refs_0_), channel_id=1, source_target_pairs={{0,8},{8,0},{1,9},{9,1},{2,10},{10,2},{3,11},{11,3},{4,12},{12,4},... | collective-permute-start | bytes 1966088 | tf_op jit(solution)/shard_map/ppermute | solution.py:126
  161.4 19.9 %all-to-all-start.4 = ((bf16[16,200,128]{2,1,0:T(8,128)(2,1)}), bf16[16,200,128]{2,1,0:T(8,128)(2,1)S(1)}, u32[]{:S(2)}, u32[]{:S(2)}) async-start(bf16[16,200,128]{2,1,0:T(8,128)(2,1)} %shard_map.113), calls=%async_computation.4 | async-start | bytes 1638400 | tf_op jit(solution)/shard_map/all_to_all | solution.py:130
  181.3 15.7 %all-to-all-start.5 = ((bf16[8,200,128]{2,1,0:T(8,128)(2,1)}), bf16[8,200,128]{2,1,0:T(8,128)(2,1)S(1)}, u32[]{:S(2)}, u32[]{:S(2)}) async-start(bf16[8,200,128]{2,1,0:T(8,128)(2,1)} %shard_map.116), calls=%async_computation.5 | async-start | bytes 819200 | tf_op jit(solution)/shard_map/all_to_all | solution.py:130
  186.2 10.8 %collective-permute-start.26 = (bf16[1,160,160]{2,1,0:T(8,128)(2,1)S(1)}, bf16[1,160,160]{2,1,0:T(8,128)(2,1)S(1)}, u32[]{:S(2)}, u32[]{:S(2)}) collective-permute-start(bf16[1,160,160]{2,1,0:T(8,128)(2,1)S(1)} %shard_map.114), channel_id=1, source_target_pairs={{0,0},{1,1},{2,2},{3,3},{4,4},{5,5},{6,6},{7,7},{8,128},{9,129},{1... | collective-permute-start | bytes 153608 | tf_op jit(solution)/shard_map/ppermute | solution.py:345
  193.4 7.4 %collective-permute-start.28 = (bf16[1,160,160]{2,1,0:T(8,128)(2,1)S(1)}, bf16[1,160,160]{2,1,0:T(8,128)(2,1)S(1)}, u32[]{:S(2)}, u32[]{:S(2)}) collective-permute-start(bf16[1,160,160]{2,1,0:T(8,128)(2,1)S(1)} %shard_map.120), channel_id=1, source_target_pairs={{0,0},{1,1},{2,2},{3,3},{4,4},{5,5},{6,6},{7,7},{8,128},{9,129},{1... | collective-permute-start | bytes 153608 | tf_op jit(solution)/shard_map/ppermute | solution.py:372
  197.5 11.9 %collective-permute-start.27 = (bf16[1,160,160]{2,1,0:T(8,128)(2,1)S(1)}, bf16[1,160,160]{2,1,0:T(8,128)(2,1)S(1)}, u32[]{:S(2)}, u32[]{:S(2)}) collective-permute-start(bf16[1,160,160]{2,1,0:T(8,128)(2,1)S(1)} %shard_map.118), channel_id=1, source_target_pairs={{0,102},{1,119},{2,0},{3,17},{4,34},{5,51},{6,68},{7,85},{8,238},{... | collective-permute-start | bytes 153608 | tf_op jit(solution)/shard_map/ppermute | solution.py:379
  (13 other events, 116.8 us)

commit v3 on v2

--- a/solution.py
+++ b/solution.py
@@ -70,7 +70,7 @@
             self.place(index, main, packed)
 
     def finish(self):
-        if self.whole:
+        if self.whole and self.sems is not None:
             copy = pltpu.make_async_copy(self.slots, self.out, self.sems.at[0])
             copy.start()
             self.copies.append(copy)
@@ -78,42 +78,53 @@
             copy.wait()
 
 
-def call(kernel, ins, outs, after=(), small=(), alias=(), scratch=(), flops=0):
+def call(kernel, ins, outs, after=(), small=(), alias=(), scratch=(), flops=0, load=False):
     n, s, a, t, o = len(ins), len(small), len(alias), len(after), len(outs)
+    loads = n if load else 0
 
     def wrapped(*refs):
         in_refs, small_refs = refs[:n], refs[n : n + s]
         rest = refs[n + s + a + t :]
         out_refs, rest = rest[:o], rest[o:]
-        held, in_sems, rest = rest[:n], rest[n], rest[n + 1 :]
-        copies = [pltpu.make_async_copy(in_refs[k], held[k], in_sems.at[k]) for k in range(n)]
+        held, in_sems, rest = rest[:loads], rest[loads], rest[loads + 1 :]
+        copies = [pltpu.make_async_copy(in_refs[k], held[k], in_sems.at[k]) for k in range(loads)]
         for copy in copies:
             copy.start()
         waited = set()
 
         def get(k):
+            if not load:
+                return in_refs[k]
             if k not in waited:
                 copies[k].wait()
                 waited.add(k)
             return held[k]
 
-        emits = [Emit(out_refs[k], rest[2 * k], rest[2 * k + 1], outs[k][1] == outs[k][0][0]) for k in range(o)]
-        kernel(get, small_refs, *emits, *rest[2 * o :])
-        for k in range(n):
+        emits = []
+        for k, (shape, slots, _) in enumerate(outs):
+            if slots:
+                emits.append(Emit(out_refs[k], rest[0], rest[1], slots == shape[0]))
+                rest = rest[2:]
+            else:
+                emits.append(Emit(out_refs[k], out_refs[k], None, True))
+        kernel(get, small_refs, *emits, *rest)
+        for k in range(loads):
             get(k)
         for emit in emits:
             emit.finish()
 
     hbm, vmem = pl.BlockSpec(memory_space=pltpu.HBM), pl.BlockSpec(memory_space=pltpu.VMEM)
-    space = [pltpu.VMEM(x.shape, x.dtype) for x in ins] + [pltpu.SemaphoreType.DMA((max(n, 1),))]
+    space = [pltpu.VMEM(x.shape, x.dtype) for x in ins[:loads]] + [pltpu.SemaphoreType.DMA((max(loads, 1),))]
     for shape, slots, dtype in outs:
-        space += [pltpu.VMEM((slots,) + shape[1:], dtype), pltpu.SemaphoreType.DMA((max(slots, shape[0]),))]
+        if slots:
+            space += [pltpu.VMEM((slots,) + shape[1:], dtype), pltpu.SemaphoreType.DMA((max(slots, shape[0]),))]
+    out_specs = [hbm if slots else vmem for _, slots, _ in outs]
     size = sum(x.size * x.dtype.itemsize for x in ins)
     return pl.pallas_call(
         wrapped,
         out_shape=[jax.ShapeDtypeStruct(shape, dtype) for shape, _, dtype in outs],
-        in_specs=[hbm] * n + [vmem] * s + [hbm] * (a + t),
-        out_specs=[hbm] * o,
+        in_specs=[hbm if load else vmem] * n + [vmem] * s + out_specs[:a] + [hbm] * t,
+        out_specs=out_specs,
         scratch_shapes=space + [pltpu.VMEM(shape, dtype) for shape, dtype in scratch],
         input_output_aliases={n + s + k: k for k in range(a)},
         compiler_params=pltpu.CompilerParams(vmem_limit_bytes=20 * 2**20),
@@ -201,7 +212,7 @@
     up1, down1 = shift(act, "z", 1), shift(act, "z", -1)
     grad_flip = shift(grad, "xh", 1)
     act_flip = shift(act, "xh", 1)
-    rows = call(reorder_kernel, [basis_out[0], basis_in[0]], [((1, width, full), 1, bf16)] * 2)
+    rows = call(reorder_kernel, [basis_out[0], basis_in[0]], [((1, width, full), 0, bf16)] * 2, load=True)
     up1, down1, rows_out, rows_in = order(up1, down1, *rows)
     up2, down2 = shift(up1, "z", 1), shift(down1, "z", -1)
     rows_out = lax.ppermute(rows_out[0], AXES, pairs_of(cross_core))
@@ -237,7 +248,7 @@
                 cov_out(steps[distance][0], product(0))
                 cov_out(steps[distance][1], product(1))
 
-        shapes = [(chunked, 2 * len(blocks), bf16)] * 2
+        shapes = [(chunked, 2 * len(blocks), bf16), (chunked, 0, bf16)]
         flops = 4 * len(blocks) * pair_flops
         return call(kernel, [], shapes, (), [act, act_flip, grad, grad_flip, *pieces], alias, flops=flops)
 
@@ -246,8 +257,9 @@
     up3, down3, rows_out, *parts = order(up3, down3, rows_out, *parts)
     down4, up4 = shift(down3[:half], "z", -1), shift(up3[half:], "z", 1)
     parts = products({3: [down3], 5: [up3]}, parts)
-    grad_late, rows_in, *parts = order(grad, rows_in, *parts)
+    grad_late, *parts = order(grad, *parts)
     weight_parts, in_parts = products({4: [down4, up4]}, parts)
+    weight_parts, rows_in = order(weight_parts, rows_in)
 
     grad_up1, grad_down1 = shift(grad_late, "z", 1), shift(grad_late, "z", -1)
     eigs = lax.ppermute(
@@ -311,36 +323,35 @@
     (eigen,) = call(mixed_kernel, [got, rows_in], [(chunked, count, bf16)], flops=square_flops)
     grad_up2, grad_down2 = shift(grad_up1, "z", 1), shift(grad_down1, "z", -1)
     got = exchange(eigen, ROW)
-    in_got = [in_sum[0]] + [shift(in_sum[k], "y", k) for k in range(1, 4)]
-    got, *in_got = order(got, *in_got)
     def eigen_kernel(get, small, out):
         eigs_ref, column_ref = small
         scale = 1.0 / (column_ref[...] * eigs_ref[0:1, :] + damping)
         out.everywhere(total_of(get(0)) * scale)
 
     (scaled,) = call(eigen_kernel, [got], [((count // 2,) + packed, count // 2, bf16)], (), [eigs, eigs[1][:, None]])
+    grad_cross = shift(grad_up2, "xh", 1)
+    scaled = exchange(scaled, "z")
+    in_got = [in_sum[0]] + [shift(in_sum[k], "y", k) for k in range(1, 4)]
+    scaled, *in_got = order(scaled, *in_got)
+    scaled_other = shift(scaled, "c", 1)
+
+    def back_kernel(get, small, out, whole):
+        c = lax.axis_index("c")
+        stacked(get(0), whole, lambda k: c * 8 + k)
+        stacked(get(1), whole, lambda k: (1 - c) * 8 + k)
+        out.everywhere(dot(get(2)[...], whole[...], (1, 0)).T)
+
+    space = [((full, width), bf16)]
+    (back,) = call(back_kernel, [scaled, scaled_other, rows_out], [(chunked, count, bf16)], (), (), (), space, square_flops)
     def staged_kernel(get, small, out):
         total = get(0)[...].astype(f32)
         for k in range(1, 4):
             total = total + get(k)[...].astype(f32)
         out.put(0, unpack(total))
 
-    (in_cov,) = call(staged_kernel, in_got, [((1,) + square, 1, bf16)])
-
-    scaled, grad_up2, grad_down2 = order(scaled, grad_up2, grad_down2)
-    grad_cross = shift(grad_up2, "xh", 1)
-    scaled = exchange(scaled, "z")
-    scaled_other = shift(scaled, "c", 1)
-
-    def back_kernel(get, small, out, whole):
-        c = lax.axis_index("c")
-        stacked(get(0), whole, lambda k: c * 8 + k)
-        stacked(get(1), whole, lambda k: (1 - c) * 8 + k)
-        out.everywhere(dot(get(2)[...], whole[...], (1, 0)).T)
-
-    space = [((full, width), bf16)]
-    (back,) = call(back_kernel, [scaled, scaled_other, rows_out], [(chunked, count, bf16)], (), (), (), space, square_flops)
-    back, grad_cross, in_cov = order(back, grad_cross, in_cov)
+    (in_cov,) = call(staged_kernel, in_got, [((1,) + square, 0, bf16)])
+
+    back, grad_cross = order(back, grad_cross)
     back = exchange(back, ROW)
     in_cov = lax.ppermute(in_cov, AXES, pairs_of(swapped))
 
@@ -358,7 +369,7 @@
                     out(index, mirrors[8 - distance].T)
 
     window = [grad_up2, grad_up1, grad_late, grad_down1, grad_down2, grad_cross]
-    (out_parts,) = call(cov_kernel, window, [(chunked, count, bf16)], flops=10 * pair_flops)
+    (out_parts,) = call(cov_kernel, window, [(chunked, 0, bf16)], flops=10 * pair_flops, load=True)
     out_parts = pair_sum(out_parts, "c")
     back, out_parts = order(back, out_parts)
 
@@ -367,22 +378,22 @@
         out.put(0, dot(get(1)[...], whole[...], (1, 0)))
 
     (precond,) = call(
-        last_kernel, [back, rows_in], [((1,) + square, 1, bf16)], (), (), (), space, square_flops
+        last_kernel, [back, rows_in], [((1,) + square, 0, bf16)], (), (), (), space, square_flops
     )
     precond = lax.ppermute(precond, AXES, pairs_of(to_output))
 
     def sum_kernel(get, small, out):
         out.put(0, total_of(get(0)))
 
-    out_got, in_cov = order(exchange(out_parts, ("y", "xl")), in_cov)
-    (out_cov,) = call(sum_kernel, [out_got], [((1,) + square, 1, bf16)])
+    out_got = exchange(out_parts, ("y", "xl"))
+    (out_cov,) = call(sum_kernel, [out_got], [((1,) + square, 0, bf16)])
     out_cov = lax.ppermute(out_cov, AXES, pairs_of(window_place))
 
     def factor(old, cov):
         def kernel(get, small, out):
             out.put(0, decay * small[0][0] + ((1.0 - decay) / total_tokens) * small[1][0].astype(f32))
 
-        return call(kernel, [], [(old.shape, 1, f32)], (), [old, cov])[0]
+        return call(kernel, [], [(old.shape, 0, f32)], (), [old, cov])[0]
 
     return factor(factor_in, in_cov), factor(factor_out, out_cov), precond
 

time: 212 us -> 205 us (0.967)
  Pallas kernels: 35.5 us -> 25.6 us
  waiting for transfers between devices: 84.8 us -> 88.7 us
    pallas_call x18, Pallas kernels: 35.5 us -> 25.6 us  [call(): pl.pallas_call(wrapped, out_shape=[jax.ShapeDtypeStruct(shape, dtype) for...]
    ppermute x23, waiting for transfers between devices: 36.8 us -> 45.8 us  [shift(): lax.ppermute(value, axis, [(i, (i + step) % size) for i in range(size)])]
    ppermute x1, waiting for transfers between devices: 7.66 us -> 3.44 us  [body(): lax.ppermute(rows_in[0], AXES, [(b, a) for a, b in pairs_of(to_output)])]
  transfers between devices with their start and end apart: 35 -> 35, of which waited for: 19 -> 21; matrix products, arithmetic and copies ran while one was open for 0% -> 0% of each run, Pallas kernels for 14% -> 11%
where the time goes in v3:
time: 205 us; the launch traced here: 203 us
  waiting for transfers between devices  88.7 us (43%)
  starting transfers between devices  83.4 us (41%)
  Pallas kernels  25.6 us (12%)
  local copies, waits for them, and re-layouts  4.65 us (2%)
    ppermute x23, waiting for transfers between devices, shift(): lax.ppermute(value, axis, [(i, (i + step) % size) for i in range(size)])  45.8 us
    ppermute x23, starting transfers between devices, shift(): lax.ppermute(value, axis, [(i, (i + step) % size) for i in range(size)])  32.9 us
    all_to_all x6, starting transfers between devices, exchange(): return lax.all_to_all(chunks, axes, 0, 0, tiled=True)  32.8 us
    all_to_all x6, waiting for transfers between devices, exchange(): return lax.all_to_all(chunks, axes, 0, 0, tiled=True)  26.6 us
    pallas_call x18, Pallas kernels, call(): pl.pallas_call(wrapped, out_shape=[jax.ShapeDtypeStruct(shape, dtype) for...  25.6 us
    ppermute x1, waiting for transfers between devices, body(): out_cov = lax.ppermute(out_cov, AXES, pairs_of(window_place))  7.44 us
    ppermute x1, starting transfers between devices, body(): in_cov = lax.ppermute(in_cov, AXES, pairs_of(swapped))  7.07 us
    unnamed x21, local copies, waits for them, and re-layouts  4.28 us
  transfers between devices with their start and end apart: 35, of which 21 were waited for; matrix products, arithmetic and copies ran while one was open for 0% of the time, Pallas kernels for 11%

profile of v3, /device:TPU:6, one launch (start us, length us, event | category | flops | bytes accessed | tf_op | source)
XLA Modules:
  0.0 203.3 jit_solution(14177038989906961963)
XLA Ops:
  2.6 4.0 %collective-permute-start.1 = (bf16[160,2048]{1,0:T(8,128)(2,1)}, bf16[160,2048]{1,0:T(8,128)(2,1)S(1)}, u32[]{:S(2)}, u32[]{:S(2)}) collective-permute-start(bf16[160,2048]{1,0:T(8,128)(2,1)} %bitcast.28), channel_id=1, source_target_pairs={{0,7},{1,0},{2,1},{3,2},{4,3},{5,4},{6,5},{7,6},{8,15},{9,8},{10,9... | collective-permute-start | bytes 1966088 | tf_op jit(solution)/shard_map/ppermute | solution.py:137
  13.5 8.0 %collective-permute-done.refs_6_ = bf16[160,2048]{1,0:T(8,128)(2,1)S(1)} collective-permute-done((bf16[160,2048]{1,0:T(8,128)(2,1)}, bf16[160,2048]{1,0:T(8,128)(2,1)S(1)}, u32[]{:S(2)}, u32[]{:S(2)}) %collective-permute-start) | collective-permute-done | bytes 655392 | tf_op jit(solution)/shard_map/ppermute | solution.py:137
  21.5 3.2 %collective-permute-start.3 = (bf16[160,2048]{1,0:T(8,128)(2,1)S(1)}, bf16[160,2048]{1,0:T(8,128)(2,1)S(1)}, u32[]{:S(2)}, u32[]{:S(2)}) collective-permute-start(bf16[160,2048]{1,0:T(8,128)(2,1)S(1)} %collective-permute-done.1.refs_5_), channel_id=1, source_target_pairs={{0,7},{1,0},{2,1},{3,2},{4,3},{5,4},{6,5},{7,6},{8,15},{9,8},{10,9... | collective-permute-start | bytes 1966088 | tf_op jit(solution)/shard_map/ppermute | solution.py:137
  26.7 13.4 %collective-permute-done.4.refs_3_ = bf16[160,2048]{1,0:T(8,128)(2,1)S(1)} collective-permute-done((bf16[160,2048]{1,0:T(8,128)(2,1)}, bf16[160,2048]{1,0:T(8,128)(2,1)S(1)}, u32[]{:S(2)}, u32[]{:S(2)}) %collective-permute-start.4) | collective-permute-done | bytes 655392 | tf_op jit(solution)/shard_map/ppermute | solution.py:137
  40.5 2.9 %collective-permute-start.7 = (bf16[160,2048]{1,0:T(8,128)(2,1)S(1)}, bf16[160,2048]{1,0:T(8,128)(2,1)S(1)}, u32[]{:S(2)}, u32[]{:S(2)}) collective-permute-start(bf16[160,2048]{1,0:T(8,128)(2,1)S(1)} %collective-permute-done.3.refs_7_), channel_id=1, source_target_pairs={{0,7},{1,0},{2,1},{3,2},{4,3},{5,4},{6,5},{7,6},{8,15},{9,8},{10,9... | collective-permute-start | bytes 1966088 | tf_op jit(solution)/shard_map/ppermute | solution.py:137
  45.3 4.3 %shard_map.104 = (bf16[16,200,128]{2,1,0:T(8,128)(2,1)}, bf16[16,200,128]{2,1,0:T(8,128)(2,1)S(1)}) custom-call(bf16[160,2048]{1,0:T(8,128)(2,1)S(1)} %bitcast.30, bf16[160,2048]{1,0:T(8,128)(2,1)S(1)} %collective-permute-done.5.refs_1_, bf16[160,2048]{1,0:T(8,128)(2,1)S(1)} %bitcast.21, bf16[160,2048]{1,0:T(8,128)(2,1)S(1)} %collective-permute-done.4.refs_3_, ...), custom_call_target="tpu_custom_call" | custom-call | flops 2097152000 | tf_op jit(solution)/shard_map/pallas_call | solution.py:123
  49.6 5.5 %collective-permute-done.6.refs_5_ = bf16[160,2048]{1,0:T(8,128)(2,1)S(1)} collective-permute-done((bf16[160,2048]{1,0:T(8,128)(2,1)S(1)}, bf16[160,2048]{1,0:T(8,128)(2,1)S(1)}, u32[]{:S(2)}, u32[]{:S(2)}) %collective-permute-start.6) | collective-permute-done | bytes 655392 | tf_op jit(solution)/shard_map/ppermute | solution.py:137
  56.5 2.2 %collective-permute-start.9 = (bf16[80,2048]{1,0:T(8,128)(2,1)S(1)}, bf16[80,2048]{1,0:T(8,128)(2,1)S(1)}, u32[]{:S(2)}, u32[]{:S(2)}) collective-permute-start(bf16[80,2048]{1,0:T(8,128)(2,1)S(1)} %slice.45), channel_id=1, source_target_pairs={{0,7},{1,0},{2,1},{3,2},{4,3},{5,4},{6,5},{7,6},{8,15},{9,8},{10,9... | collective-permute-start | bytes 983048 | tf_op jit(solution)/shard_map/ppermute | solution.py:137
  58.7 2.3 %shard_map.105 = (bf16[16,200,128]{2,1,0:T(8,128)(2,1)}, bf16[16,200,128]{2,1,0:T(8,128)(2,1)S(1)}) custom-call(bf16[160,2048]{1,0:T(8,128)(2,1)S(1)} %bitcast.32, bf16[160,2048]{1,0:T(8,128)(2,1)S(1)} %collective-permute-done.5.refs_1_, bf16[160,2048]{1,0:T(8,128)(2,1)S(1)} %bitcast.22, ...), custom_call_target="tpu_custom_call", output_to_operand_aliasing={{0}: (6, {}), {1}: (7, {})} | custom-call | flops 838860800 | tf_op jit(solution)/shard_map/pallas_call | solution.py:123
  61.0 2.5 %collective-permute-done.10.refs_5_ = bf16[80,2048]{1,0:T(8,128)(2,1)S(1)} collective-permute-done((bf16[80,2048]{1,0:T(8,128)(2,1)S(1)}, bf16[80,2048]{1,0:T(8,128)(2,1)S(1)}, u32[]{:S(2)}, u32[]{:S(2)}) %collective-permute-start.10) | collective-permute-done | bytes 327712 | tf_op jit(solution)/shard_map/ppermute | solution.py:137
  63.9 2.6 %shard_map.106 = (bf16[16,200,128]{2,1,0:T(8,128)(2,1)}, bf16[16,200,128]{2,1,0:T(8,128)(2,1)S(1)}) custom-call(bf16[160,2048]{1,0:T(8,128)(2,1)S(1)} %bitcast.33, bf16[160,2048]{1,0:T(8,128)(2,1)S(1)} %collective-permute-done.5.refs_1_, bf16[160,2048]{1,0:T(8,128)(2,1)S(1)} %bitcast.23, ...), custom_call_target="tpu_custom_call", output_to_operand_aliasing={{0}: (6, {}), {1}: (7, {})} | custom-call | flops 419430400 | tf_op jit(solution)/shard_map/pallas_call | solution.py:123
  66.4 3.4 %collective-permute-done.11.refs_1_ = bf16[160,2560]{1,0:T(8,128)(2,1)S(1)} collective-permute-done((bf16[160,2560]{1,0:T(8,128)(2,1)S(1)}, bf16[160,2560]{1,0:T(8,128)(2,1)S(1)}, u32[]{:S(2)}, u32[]{:S(2)}) %collective-permute-start.11) | collective-permute-done | bytes 819232 | tf_op jit(solution)/shard_map/ppermute | solution.py:256
  70.8 4.2 %all-to-all-start = ((bf16[16,200,128]{2,1,0:T(8,128)(2,1)}), bf16[16,200,128]{2,1,0:T(8,128)(2,1)S(1)}, u32[]{:S(2)}, u32[]{:S(2)}) async-start(bf16[16,200,128]{2,1,0:T(8,128)(2,1)} %get-tuple-element.69), calls=%async_computation | async-start | bytes 1638400 | tf_op jit(solution)/shard_map/all_to_all | solution.py:141
  75.7 2.9 %collective-permute-start.15 = (bf16[160,2048]{1,0:T(8,128)(2,1)S(1)}, bf16[160,2048]{1,0:T(8,128)(2,1)}, u32[]{:S(2)}, u32[]{:S(2)}) collective-permute-start(bf16[160,2048]{1,0:T(8,128)(2,1)S(1)} %bitcast.25), channel_id=1, source_target_pairs={{0,7},{1,0},{2,1},{3,2},{4,3},{5,4},{6,5},{7,6},{8,15},{9,8},{10,9... | collective-permute-start | bytes 1966088 | tf_op jit(solution)/shard_map/ppermute | solution.py:137
  79.0 9.0 %all-to-all-done.refs_0_ = bf16[16,200,128]{2,1,0:T(8,128)(2,1)S(1)} async-done(((bf16[16,200,128]{2,1,0:T(8,128)(2,1)}), bf16[16,200,128]{2,1,0:T(8,128)(2,1)S(1)}, u32[]{:S(2)}, u32[]{:S(2)}) %all-to-all-start) | async-done | bytes 819232 | tf_op jit(solution)/shard_map/all_to_all | solution.py:141
  93.6 6.2 %all-to-all-start.1 = ((bf16[8,200,128]{2,1,0:T(8,128)(2,1)}), bf16[8,200,128]{2,1,0:T(8,128)(2,1)S(1)}, u32[]{:S(2)}, u32[]{:S(2)}) async-start(bf16[8,200,128]{2,1,0:T(8,128)(2,1)} %shard_map.109), calls=%async_computation.1 | async-start | bytes 819200 | tf_op jit(solution)/shard_map/all_to_all | solution.py:141
  102.5 3.4 %collective-permute-done.16.refs_1_ = bf16[4,200,128]{2,1,0:T(8,128)(2,1)S(1)} collective-permute-done((bf16[4,200,128]{2,1,0:T(8,128)(2,1)S(1)}, bf16[4,200,128]{2,1,0:T(8,128)(2,1)S(1)}, u32[]{:S(2)}, u32[]{:S(2)}) %collective-permute-start.16) | collective-permute-done | bytes 204832 | tf_op jit(solution)/shard_map/ppermute | solution.py:137
  106.3 3.7 %collective-permute-done.17.refs_1_ = f32[2,160]{1,0:T(2,128)S(1)} collective-permute-done((f32[2,160]{1,0:T(2,128)S(1)}, f32[2,160]{1,0:T(2,128)S(1)}, u32[]{:S(2)}, u32[]{:S(2)}) %collective-permute-start.17) | collective-permute-done | bytes 1312 | tf_op jit(solution)/shard_map/ppermute | solution.py:265
  110.0 4.3 %all-to-all-done.1.refs_0_ = bf16[8,200,128]{2,1,0:T(8,128)(2,1)S(1)} async-done(((bf16[8,200,128]{2,1,0:T(8,128)(2,1)}), bf16[8,200,128]{2,1,0:T(8,128)(2,1)S(1)}, u32[]{:S(2)}, u32[]{:S(2)}) %all-to-all-start.1) | async-done | bytes 409632 | tf_op jit(solution)/shard_map/all_to_all | solution.py:141
  115.9 7.0 %all-to-all-start.2 = ((bf16[16,200,128]{2,1,0:T(8,128)(2,1)}), bf16[16,200,128]{2,1,0:T(8,128)(2,1)S(1)}, u32[]{:S(2)}, u32[]{:S(2)}) async-start(bf16[16,200,128]{2,1,0:T(8,128)(2,1)} %shard_map.111), calls=%async_computation.2 | async-start | bytes 1638400 | tf_op jit(solution)/shard_map/all_to_all | solution.py:141
  123.6 10.4 %all-to-all-done.2.refs_0_ = bf16[16,200,128]{2,1,0:T(8,128)(2,1)S(1)} async-done(((bf16[16,200,128]{2,1,0:T(8,128)(2,1)}), bf16[16,200,128]{2,1,0:T(8,128)(2,1)S(1)}, u32[]{:S(2)}, u32[]{:S(2)}) %all-to-all-start.2) | async-done | bytes 819232 | tf_op jit(solution)/shard_map/all_to_all | solution.py:141
  135.0 3.5 %all-to-all-start.3 = ((bf16[8,200,128]{2,1,0:T(8,128)(2,1)}), bf16[8,200,128]{2,1,0:T(8,128)(2,1)S(1)}, u32[]{:S(2)}, u32[]{:S(2)}) async-start(bf16[8,200,128]{2,1,0:T(8,128)(2,1)} %shard_map.112), calls=%async_computation.3 | async-start | bytes 819200 | tf_op jit(solution)/shard_map/all_to_all | solution.py:141
  138.5 3.2 %collective-permute-start.25 = (bf16[160,2048]{1,0:T(8,128)(2,1)}, bf16[160,2048]{1,0:T(8,128)(2,1)}, u32[]{:S(2)}, u32[]{:S(2)}) collective-permute-start(bf16[160,2048]{1,0:T(8,128)(2,1)} %collective-permute-done.15.refs_3_), channel_id=1, source_target_pairs={{0,7},{1,0},{2,1},{3,2},{4,3},{5,4},{6,5},{7,6},{8,15},{9,8},{10,9... | collective-permute-start | bytes 1966088 | tf_op jit(solution)/shard_map/ppermute | solution.py:137
  143.9 2.8 %collective-permute-start.19 = (bf16[200,128]{1,0:T(8,128)(2,1)S(1)}, bf16[200,128]{1,0:T(8,128)(2,1)S(1)}, u32[]{:S(2)}, u32[]{:S(2)}) collective-permute-start(bf16[200,128]{1,0:T(8,128)(2,1)S(1)} %get-tuple-element.102), channel_id=1, source_target_pairs={{0,128},{64,192},{128,0},{192,64},{1,129},{65,193},{129,1},{193,65... | collective-permute-start | bytes 153608 | tf_op jit(solution)/shard_map/ppermute | solution.py:137
  147.2 2.5 %collective-permute-done.18.refs_1_ = bf16[200,128]{1,0:T(8,128)(2,1)S(1)} collective-permute-done((bf16[200,128]{1,0:T(8,128)(2,1)S(1)}, bf16[200,128]{1,0:T(8,128)(2,1)S(1)}, u32[]{:S(2)}, u32[]{:S(2)}) %collective-permute-start.18) | collective-permute-done | bytes 51232 | tf_op jit(solution)/shard_map/ppermute | solution.py:137
  156.4 7.7 %all-to-all-start.4 = ((bf16[16,200,128]{2,1,0:T(8,128)(2,1)}), bf16[16,200,128]{2,1,0:T(8,128)(2,1)S(1)}, u32[]{:S(2)}, u32[]{:S(2)}) async-start(bf16[16,200,128]{2,1,0:T(8,128)(2,1)} %shard_map.115), calls=%async_computation.4 | async-start | bytes 1638400 | tf_op jit(solution)/shard_map/all_to_all | solution.py:141
  164.1 5.4 %shard_map.116 = bf16[16,200,128]{2,1,0:T(8,128)(2,1)S(1)} custom-call(bf16[160,2048]{1,0:T(8,128)(2,1)} %collective-permute-done.23.refs_0_, bf16[160,2048]{1,0:T(8,128)(2,1)} %collective-permute-done.14.refs_1_, bf16[160,2048]{1,0:T(8,128)(2,1)S(1)} %bitcast.26, bf16[160,2048]{1,0:T(8,128)(2,1)} %collective-permute-done.15.refs_3_, ...), custom_call_target="tpu_custom_call" | custom-call | flops 1048576000 | bytes 3932160 | tf_op jit(solution)/shard_map/pallas_call | solution.py:123
  172.3 3.0 %all-to-all-done.4.refs_0_ = bf16[16,200,128]{2,1,0:T(8,128)(2,1)S(1)} async-done(((bf16[16,200,128]{2,1,0:T(8,128)(2,1)}), bf16[16,200,128]{2,1,0:T(8,128)(2,1)S(1)}, u32[]{:S(2)}, u32[]{:S(2)}) %all-to-all-start.4) | async-done | bytes 819232 | tf_op jit(solution)/shard_map/all_to_all | solution.py:141
  175.3 4.1 %all-to-all-start.5 = ((bf16[8,200,128]{2,1,0:T(8,128)(2,1)}), bf16[8,200,128]{2,1,0:T(8,128)(2,1)S(1)}, u32[]{:S(2)}, u32[]{:S(2)}) async-start(bf16[8,200,128]{2,1,0:T(8,128)(2,1)} %shard_map.117), calls=%async_computation.5 | async-start | bytes 819200 | tf_op jit(solution)/shard_map/all_to_all | solution.py:141
  179.6 7.1 %collective-permute-start.21 = (bf16[1,160,160]{2,1,0:T(8,128)(2,1)S(1)}, bf16[1,160,160]{2,1,0:T(8,128)(2,1)S(1)}, u32[]{:S(2)}, u32[]{:S(2)}) collective-permute-start(bf16[1,160,160]{2,1,0:T(8,128)(2,1)S(1)} %shard_map.113), channel_id=1, source_target_pairs={{0,0},{1,1},{2,2},{3,3},{4,4},{5,5},{6,6},{7,7},{8,128},{9,129},{1... | collective-permute-start | bytes 153608 | tf_op jit(solution)/shard_map/ppermute | solution.py:356
  187.2 2.8 %collective-permute-start.28 = (bf16[1,160,160]{2,1,0:T(8,128)(2,1)S(1)}, bf16[1,160,160]{2,1,0:T(8,128)(2,1)S(1)}, u32[]{:S(2)}, u32[]{:S(2)}) collective-permute-start(bf16[1,160,160]{2,1,0:T(8,128)(2,1)S(1)} %shard_map.120), channel_id=1, source_target_pairs={{0,0},{1,1},{2,2},{3,3},{4,4},{5,5},{6,6},{7,7},{8,128},{9,129},{1... | collective-permute-start | bytes 153608 | tf_op jit(solution)/shard_map/ppermute | solution.py:383
  194.5 7.4 %collective-permute-done.27.refs_1_ = bf16[1,160,160]{2,1,0:T(8,128)(2,1)S(1)} collective-permute-done((bf16[1,160,160]{2,1,0:T(8,128)(2,1)S(1)}, bf16[1,160,160]{2,1,0:T(8,128)(2,1)S(1)}, u32[]{:S(2)}, u32[]{:S(2)}) %collective-permute-start.27) | collective-permute-done | bytes 51232 | tf_op jit(solution)/shard_map/ppermute | solution.py:390
  (87 shorter events, 47.4 us)
Async XLA Ops:
  0.6 20.9 %collective-permute-start = (bf16[160,2048]{1,0:T(8,128)(2,1)}, bf16[160,2048]{1,0:T(8,128)(2,1)S(1)}, u32[]{:S(2)}, u32[]{:S(2)}) collective-permute-start(bf16[160,2048]{1,0:T(8,128)(2,1)} %bitcast.27), channel_id=1, source_target_pairs={{0,1},{1,2},{2,3},{3,4},{4,5},{5,6},{6,7},{7,0},{8,9},{9,10},{10,1... | collective-permute-start | bytes 1966088 | tf_op jit(solution)/shard_map/ppermute | solution.py:137
  2.6 18.9 %collective-permute-start.1 = (bf16[160,2048]{1,0:T(8,128)(2,1)}, bf16[160,2048]{1,0:T(8,128)(2,1)S(1)}, u32[]{:S(2)}, u32[]{:S(2)}) collective-permute-start(bf16[160,2048]{1,0:T(8,128)(2,1)} %bitcast.28), channel_id=1, source_target_pairs={{0,7},{1,0},{2,1},{3,2},{4,3},{5,4},{6,5},{7,6},{8,15},{9,8},{10,9... | collective-permute-start | bytes 1966088 | tf_op jit(solution)/shard_map/ppermute | solution.py:137
  6.7 20.0 %collective-permute-start.5 = (bf16[160,2048]{1,0:T(8,128)(2,1)}, bf16[160,2048]{1,0:T(8,128)(2,1)S(1)}, u32[]{:S(2)}, u32[]{:S(2)}) collective-permute-start(bf16[160,2048]{1,0:T(8,128)(2,1)} %bitcast.29), channel_id=1, source_target_pairs={{0,8},{8,0},{1,9},{9,1},{2,10},{10,2},{3,11},{11,3},{4,12},{12,4},... | collective-permute-start | bytes 1966088 | tf_op jit(solution)/shard_map/ppermute | solution.py:137
  8.1 32.0 %collective-permute-start.4 = (bf16[160,2048]{1,0:T(8,128)(2,1)}, bf16[160,2048]{1,0:T(8,128)(2,1)S(1)}, u32[]{:S(2)}, u32[]{:S(2)}) collective-permute-start(bf16[160,2048]{1,0:T(8,128)(2,1)} %bitcast.20), channel_id=1, source_target_pairs={{0,8},{8,0},{1,9},{9,1},{2,10},{10,2},{3,11},{11,3},{4,12},{12,4},... | collective-permute-start | bytes 1966088 | tf_op jit(solution)/shard_map/ppermute | solution.py:137
  21.5 18.6 %collective-permute-start.2 = (bf16[160,2048]{1,0:T(8,128)(2,1)S(1)}, bf16[160,2048]{1,0:T(8,128)(2,1)S(1)}, u32[]{:S(2)}, u32[]{:S(2)}) collective-permute-start(bf16[160,2048]{1,0:T(8,128)(2,1)S(1)} %collective-permute-done.refs_6_), channel_id=1, source_target_pairs={{0,1},{1,2},{2,3},{3,4},{4,5},{5,6},{6,7},{7,0},{8,9},{9,10},{10,1... | collective-permute-start | bytes 1966088 | tf_op jit(solution)/shard_map/ppermute | solution.py:137
  21.5 18.6 %collective-permute-start.3 = (bf16[160,2048]{1,0:T(8,128)(2,1)S(1)}, bf16[160,2048]{1,0:T(8,128)(2,1)S(1)}, u32[]{:S(2)}, u32[]{:S(2)}) collective-permute-start(bf16[160,2048]{1,0:T(8,128)(2,1)S(1)} %collective-permute-done.1.refs_5_), channel_id=1, source_target_pairs={{0,7},{1,0},{2,1},{3,2},{4,3},{5,4},{6,5},{7,6},{8,15},{9,8},{10,9... | collective-permute-start | bytes 1966088 | tf_op jit(solution)/shard_map/ppermute | solution.py:137
  24.7 24.8 %collective-permute-start.8 = (bf16[160,2560]{1,0:T(8,128)(2,1)S(1)}, bf16[160,2560]{1,0:T(8,128)(2,1)S(1)}, u32[]{:S(2)}, u32[]{:S(2)}) collective-permute-start(bf16[160,2560]{1,0:T(8,128)(2,1)S(1)} %bitcast.37), channel_id=1, source_target_pairs={{0,0},{1,1},{2,2},{3,3},{4,4},{5,5},{6,6},{7,7},{8,16},{9,17},{10,... | collective-permute-start | bytes 2457608 | tf_op jit(solution)/shard_map/ppermute | solution.py:218
  40.1 15.0 %collective-permute-start.6 = (bf16[160,2048]{1,0:T(8,128)(2,1)S(1)}, bf16[160,2048]{1,0:T(8,128)(2,1)S(1)}, u32[]{:S(2)}, u32[]{:S(2)}) collective-permute-start(bf16[160,2048]{1,0:T(8,128)(2,1)S(1)} %collective-permute-done.2.refs_8_), channel_id=1, source_target_pairs={{0,1},{1,2},{2,3},{3,4},{4,5},{5,6},{6,7},{7,0},{8,9},{9,10},{10,1... | collective-permute-start | bytes 1966088 | tf_op jit(solution)/shard_map/ppermute | solution.py:137
  40.5 14.6 %collective-permute-start.7 = (bf16[160,2048]{1,0:T(8,128)(2,1)S(1)}, bf16[160,2048]{1,0:T(8,128)(2,1)S(1)}, u32[]{:S(2)}, u32[]{:S(2)}) collective-permute-start(bf16[160,2048]{1,0:T(8,128)(2,1)S(1)} %collective-permute-done.3.refs_7_), channel_id=1, source_target_pairs={{0,7},{1,0},{2,1},{3,2},{4,3},{5,4},{6,5},{7,6},{8,15},{9,8},{10,9... | collective-permute-start | bytes 1966088 | tf_op jit(solution)/shard_map/ppermute | solution.py:137
  43.3 26.6 %collective-permute-start.11 = (bf16[160,2560]{1,0:T(8,128)(2,1)S(1)}, bf16[160,2560]{1,0:T(8,128)(2,1)S(1)}, u32[]{:S(2)}, u32[]{:S(2)}) collective-permute-start(bf16[160,2560]{1,0:T(8,128)(2,1)S(1)} %bitcast.36), channel_id=1, source_target_pairs={{0,0},{1,1},{2,2},{3,3},{4,4},{5,5},{6,6},{7,7},{128,8},{129,9},{1... | collective-permute-start | bytes 2457608 | tf_op jit(solution)/shard_map/ppermute | solution.py:256
  55.1 8.4 %collective-permute-start.10 = (bf16[80,2048]{1,0:T(8,128)(2,1)S(1)}, bf16[80,2048]{1,0:T(8,128)(2,1)S(1)}, u32[]{:S(2)}, u32[]{:S(2)}) collective-permute-start(bf16[80,2048]{1,0:T(8,128)(2,1)S(1)} %slice.46), channel_id=1, source_target_pairs={{0,1},{1,2},{2,3},{3,4},{4,5},{5,6},{6,7},{7,0},{8,9},{9,10},{10,1... | collective-permute-start | bytes 983048 | tf_op jit(solution)/shard_map/ppermute | solution.py:137
  56.5 7.3 %collective-permute-start.9 = (bf16[80,2048]{1,0:T(8,128)(2,1)S(1)}, bf16[80,2048]{1,0:T(8,128)(2,1)S(1)}, u32[]{:S(2)}, u32[]{:S(2)}) collective-permute-start(bf16[80,2048]{1,0:T(8,128)(2,1)S(1)} %slice.45), channel_id=1, source_target_pairs={{0,7},{1,0},{2,1},{3,2},{4,3},{5,4},{6,5},{7,6},{8,15},{9,8},{10,9... | collective-permute-start | bytes 983048 | tf_op jit(solution)/shard_map/ppermute | solution.py:137
  70.8 17.2 %all-to-all-start = ((bf16[16,200,128]{2,1,0:T(8,128)(2,1)}), bf16[16,200,128]{2,1,0:T(8,128)(2,1)S(1)}, u32[]{:S(2)}, u32[]{:S(2)}) async-start(bf16[16,200,128]{2,1,0:T(8,128)(2,1)} %get-tuple-element.69), calls=%async_computation | async-start | bytes 1638400 | tf_op jit(solution)/shard_map/all_to_all | solution.py:141
  75.1 3.5 %collective-permute-start.12 = (bf16[8,200,128]{2,1,0:T(8,128)(2,1)S(1)}, bf16[8,200,128]{2,1,0:T(8,128)(2,1)S(1)}, u32[]{:S(2)}, u32[]{:S(2)}) collective-permute-start(bf16[8,200,128]{2,1,0:T(8,128)(2,1)S(1)} %get-tuple-element.97), channel_id=1, source_target_pairs={{0,16},{16,0},{1,17},{17,1},{2,18},{18,2},{3,19},{19,3},{4,20},{20... | collective-permute-start | bytes 1228808 | tf_op jit(solution)/shard_map/ppermute | solution.py:137
  75.3 18.3 %collective-permute-start.14 = (bf16[160,2048]{1,0:T(8,128)(2,1)S(1)}, bf16[160,2048]{1,0:T(8,128)(2,1)}, u32[]{:S(2)}, u32[]{:S(2)}) collective-permute-start(bf16[160,2048]{1,0:T(8,128)(2,1)S(1)} %bitcast.24), channel_id=1, source_target_pairs={{0,1},{1,2},{2,3},{3,4},{4,5},{5,6},{6,7},{7,0},{8,9},{9,10},{10,1... | collective-permute-start | bytes 1966088 | tf_op jit(solution)/shard_map/ppermute | solution.py:137
  75.7 18.0 %collective-permute-start.15 = (bf16[160,2048]{1,0:T(8,128)(2,1)S(1)}, bf16[160,2048]{1,0:T(8,128)(2,1)}, u32[]{:S(2)}, u32[]{:S(2)}) collective-permute-start(bf16[160,2048]{1,0:T(8,128)(2,1)S(1)} %bitcast.25), channel_id=1, source_target_pairs={{0,7},{1,0},{2,1},{3,2},{4,3},{5,4},{6,5},{7,6},{8,15},{9,8},{10,9... | collective-permute-start | bytes 1966088 | tf_op jit(solution)/shard_map/ppermute | solution.py:137
  93.6 20.7 %all-to-all-start.1 = ((bf16[8,200,128]{2,1,0:T(8,128)(2,1)}), bf16[8,200,128]{2,1,0:T(8,128)(2,1)S(1)}, u32[]{:S(2)}, u32[]{:S(2)}) async-start(bf16[8,200,128]{2,1,0:T(8,128)(2,1)} %shard_map.109), calls=%async_computation.1 | async-start | bytes 819200 | tf_op jit(solution)/shard_map/all_to_all | solution.py:141
  99.9 6.1 %collective-permute-start.16 = (bf16[4,200,128]{2,1,0:T(8,128)(2,1)S(1)}, bf16[4,200,128]{2,1,0:T(8,128)(2,1)S(1)}, u32[]{:S(2)}, u32[]{:S(2)}) collective-permute-start(bf16[4,200,128]{2,1,0:T(8,128)(2,1)S(1)} %get-tuple-element.99), channel_id=1, source_target_pairs={{0,32},{32,0},{1,33},{33,1},{2,34},{34,2},{3,35},{35,3},{4,36},{36... | collective-permute-start | bytes 614408 | tf_op jit(solution)/shard_map/ppermute | solution.py:137
  100.6 9.4 %collective-permute-start.17 = (f32[2,160]{1,0:T(2,128)S(1)}, f32[2,160]{1,0:T(2,128)S(1)}, u32[]{:S(2)}, u32[]{:S(2)}) collective-permute-start(f32[2,160]{1,0:T(2,128)S(1)} %pad_maximum_fusion), channel_id=1, source_target_pairs={{0,0},{1,1},{2,2},{3,3},{4,4},{5,5},{6,6},{7,7},{128,8},{129,9},{1... | collective-permute-start | bytes 3848 | tf_op jit(solution)/shard_map/ppermute | solution.py:265
  115.9 18.1 %all-to-all-start.2 = ((bf16[16,200,128]{2,1,0:T(8,128)(2,1)}), bf16[16,200,128]{2,1,0:T(8,128)(2,1)S(1)}, u32[]{:S(2)}, u32[]{:S(2)}) async-start(bf16[16,200,128]{2,1,0:T(8,128)(2,1)} %shard_map.111), calls=%async_computation.2 | async-start | bytes 1638400 | tf_op jit(solution)/shard_map/all_to_all | solution.py:141
  122.9 18.8 %collective-permute-start.23 = (bf16[160,2048]{1,0:T(8,128)(2,1)}, bf16[160,2048]{1,0:T(8,128)(2,1)}, u32[]{:S(2)}, u32[]{:S(2)}) collective-permute-start(bf16[160,2048]{1,0:T(8,128)(2,1)} %collective-permute-done.14.refs_1_), channel_id=1, source_target_pairs={{0,1},{1,2},{2,3},{3,4},{4,5},{5,6},{6,7},{7,0},{8,9},{9,10},{10,1... | collective-permute-start | bytes 1966088 | tf_op jit(solution)/shard_map/ppermute | solution.py:137
  135.0 15.8 %all-to-all-start.3 = ((bf16[8,200,128]{2,1,0:T(8,128)(2,1)}), bf16[8,200,128]{2,1,0:T(8,128)(2,1)S(1)}, u32[]{:S(2)}, u32[]{:S(2)}) async-start(bf16[8,200,128]{2,1,0:T(8,128)(2,1)} %shard_map.112), calls=%async_computation.3 | async-start | bytes 819200 | tf_op jit(solution)/shard_map/all_to_all | solution.py:141
  138.5 25.6 %collective-permute-start.25 = (bf16[160,2048]{1,0:T(8,128)(2,1)}, bf16[160,2048]{1,0:T(8,128)(2,1)}, u32[]{:S(2)}, u32[]{:S(2)}) collective-permute-start(bf16[160,2048]{1,0:T(8,128)(2,1)} %collective-permute-done.15.refs_3_), channel_id=1, source_target_pairs={{0,7},{1,0},{2,1},{3,2},{4,3},{5,4},{6,5},{7,6},{8,15},{9,8},{10,9... | collective-permute-start | bytes 1966088 | tf_op jit(solution)/shard_map/ppermute | solution.py:137
  141.7 14.7 %collective-permute-start.24 = (bf16[160,2048]{1,0:T(8,128)(2,1)}, bf16[160,2048]{1,0:T(8,128)(2,1)}, u32[]{:S(2)}, u32[]{:S(2)}) collective-permute-start(bf16[160,2048]{1,0:T(8,128)(2,1)} %collective-permute-done.23.refs_0_), channel_id=1, source_target_pairs={{0,8},{8,0},{1,9},{9,1},{2,10},{10,2},{3,11},{11,3},{4,12},{12,4},... | collective-permute-start | bytes 1966088 | tf_op jit(solution)/shard_map/ppermute | solution.py:137
  143.8 5.9 %collective-permute-start.18 = (bf16[200,128]{1,0:T(8,128)(2,1)S(1)}, bf16[200,128]{1,0:T(8,128)(2,1)S(1)}, u32[]{:S(2)}, u32[]{:S(2)}) collective-permute-start(bf16[200,128]{1,0:T(8,128)(2,1)S(1)} %get-tuple-element.103), channel_id=1, source_target_pairs={{0,64},{64,128},{128,192},{192,0},{1,65},{65,129},{129,193},{193,1... | collective-permute-start | bytes 153608 | tf_op jit(solution)/shard_map/ppermute | solution.py:137
  143.9 5.8 %collective-permute-start.19 = (bf16[200,128]{1,0:T(8,128)(2,1)S(1)}, bf16[200,128]{1,0:T(8,128)(2,1)S(1)}, u32[]{:S(2)}, u32[]{:S(2)}) collective-permute-start(bf16[200,128]{1,0:T(8,128)(2,1)S(1)} %get-tuple-element.102), channel_id=1, source_target_pairs={{0,128},{64,192},{128,0},{192,64},{1,129},{65,193},{129,1},{193,65... | collective-permute-start | bytes 153608 | tf_op jit(solution)/shard_map/ppermute | solution.py:137
  146.7 4.1 %collective-permute-start.20 = (bf16[200,128]{1,0:T(8,128)(2,1)S(1)}, bf16[200,128]{1,0:T(8,128)(2,1)S(1)}, u32[]{:S(2)}, u32[]{:S(2)}) collective-permute-start(bf16[200,128]{1,0:T(8,128)(2,1)S(1)} %get-tuple-element.101), channel_id=1, source_target_pairs={{0,192},{64,0},{128,64},{192,128},{1,193},{65,1},{129,65},{193,129... | collective-permute-start | bytes 153608 | tf_op jit(solution)/shard_map/ppermute | solution.py:137
  156.4 18.9 %all-to-all-start.4 = ((bf16[16,200,128]{2,1,0:T(8,128)(2,1)}), bf16[16,200,128]{2,1,0:T(8,128)(2,1)S(1)}, u32[]{:S(2)}, u32[]{:S(2)}) async-start(bf16[16,200,128]{2,1,0:T(8,128)(2,1)} %shard_map.115), calls=%async_computation.4 | async-start | bytes 1638400 | tf_op jit(solution)/shard_map/all_to_all | solution.py:141
  175.3 14.7 %all-to-all-start.5 = ((bf16[8,200,128]{2,1,0:T(8,128)(2,1)}), bf16[8,200,128]{2,1,0:T(8,128)(2,1)S(1)}, u32[]{:S(2)}, u32[]{:S(2)}) async-start(bf16[8,200,128]{2,1,0:T(8,128)(2,1)} %shard_map.117), calls=%async_computation.5 | async-start | bytes 819200 | tf_op jit(solution)/shard_map/all_to_all | solution.py:141
  179.6 12.6 %collective-permute-start.21 = (bf16[1,160,160]{2,1,0:T(8,128)(2,1)S(1)}, bf16[1,160,160]{2,1,0:T(8,128)(2,1)S(1)}, u32[]{:S(2)}, u32[]{:S(2)}) collective-permute-start(bf16[1,160,160]{2,1,0:T(8,128)(2,1)S(1)} %shard_map.113), channel_id=1, source_target_pairs={{0,0},{1,1},{2,2},{3,3},{4,4},{5,5},{6,6},{7,7},{8,128},{9,129},{1... | collective-permute-start | bytes 153608 | tf_op jit(solution)/shard_map/ppermute | solution.py:356
  187.2 7.4 %collective-permute-start.28 = (bf16[1,160,160]{2,1,0:T(8,128)(2,1)S(1)}, bf16[1,160,160]{2,1,0:T(8,128)(2,1)S(1)}, u32[]{:S(2)}, u32[]{:S(2)}) collective-permute-start(bf16[1,160,160]{2,1,0:T(8,128)(2,1)S(1)} %shard_map.120), channel_id=1, source_target_pairs={{0,0},{1,1},{2,2},{3,3},{4,4},{5,5},{6,6},{7,7},{8,128},{9,129},{1... | collective-permute-start | bytes 153608 | tf_op jit(solution)/shard_map/ppermute | solution.py:383
  190.1 11.9 %collective-permute-start.27 = (bf16[1,160,160]{2,1,0:T(8,128)(2,1)S(1)}, bf16[1,160,160]{2,1,0:T(8,128)(2,1)S(1)}, u32[]{:S(2)}, u32[]{:S(2)}) collective-permute-start(bf16[1,160,160]{2,1,0:T(8,128)(2,1)S(1)} %shard_map.118), channel_id=1, source_target_pairs={{0,102},{1,119},{2,0},{3,17},{4,34},{5,51},{6,68},{7,85},{8,238},{... | collective-permute-start | bytes 153608 | tf_op jit(solution)/shard_map/ppermute | solution.py:390
  (13 other events, 112.8 us)

commit v4 on v3

--- a/solution.py
+++ b/solution.py
@@ -22,15 +22,19 @@
     return lax.dot_general(left, right, ((contract[:1], contract[1:]), ((), ())), preferred_element_type=f32)
 
 
+SPARE = 48
+
+
 def pack(rest):
     rows = rest.shape[0] // 4
-    return jnp.concatenate([rest[rows * q : rows * (q + 1)] for q in range(4)], axis=1)
+    zeros = jnp.zeros((SPARE - rows, 4 * rest.shape[1]), rest.dtype)
+    return jnp.concatenate([jnp.concatenate([rest[rows * q : rows * (q + 1)] for q in range(4)], axis=1), zeros], axis=0)
 
 
 def unpack(value):
-    rows, lanes = value.shape[0] * 4 // 5, value.shape[1]
-    part = lanes // 4
-    rest = jnp.concatenate([value[rows:, part * q : part * (q + 1)] for q in range(4)], axis=0)
+    rows, part = value.shape[0] - SPARE, value.shape[1] // 4
+    rest = value[rows : rows + rows // 4]
+    rest = jnp.concatenate([rest[:, part * q : part * (q + 1)] for q in range(4)], axis=0)
     return jnp.concatenate([value[:rows], rest], axis=1)
 
 
@@ -193,7 +197,7 @@
     count = full // width
     rest = width - 128
     square = (width, width)
-    packed = (width * width // 128, 128)
+    packed = (width + SPARE, 128)
     chunked = (count,) + packed
     act, grad = acts[0].T, out_grads[0].T
     square_flops = 2 * count * width**3

time: 205 us -> 207 us (level)
    unnamed x21 -> x23, local copies, waits for them, and re-layouts: 4.28 us -> 5.04 us
  transfers between devices with their start and end apart: 35 -> 35, of which waited for: 21 -> 22; matrix products, arithmetic and copies ran while one was open for 0% -> 0% of each run, Pallas kernels for 11% -> 11%
where the time goes in v4:
time: 207 us; the launch traced here: 205 us
  waiting for transfers between devices  89.8 us (43%)
  starting transfers between devices  83.6 us (40%)
  Pallas kernels  25.2 us (12%)
  local copies, waits for them, and re-layouts  5.41 us (3%)
    ppermute x23, waiting for transfers between devices, shift(): lax.ppermute(value, axis, [(i, (i + step) % size) for i in range(size)])  45.4 us
    all_to_all x6, starting transfers between devices, exchange(): return lax.all_to_all(chunks, axes, 0, 0, tiled=True)  33 us
    ppermute x23, starting transfers between devices, shift(): lax.ppermute(value, axis, [(i, (i + step) % size) for i in range(size)])  33 us
    all_to_all x6, waiting for transfers between devices, exchange(): return lax.all_to_all(chunks, axes, 0, 0, tiled=True)  28.4 us
    pallas_call x18, Pallas kernels, call(): pl.pallas_call(wrapped, out_shape=[jax.ShapeDtypeStruct(shape, dtype) for...  25.2 us
    ppermute x1, waiting for transfers between devices, body(): out_cov = lax.ppermute(out_cov, AXES, pairs_of(window_place))  7.47 us
    ppermute x1, starting transfers between devices, body(): in_cov = lax.ppermute(in_cov, AXES, pairs_of(swapped))  7.03 us
    unnamed x23, local copies, waits for them, and re-layouts  5.04 us
  transfers between devices with their start and end apart: 35, of which 22 were waited for; matrix products, arithmetic and copies ran while one was open for 0% of the time, Pallas kernels for 11%

profile of v4, /device:TPU:6, one launch (start us, length us, event | category | flops | bytes accessed | tf_op | source)
XLA Modules:
  0.0 205.1 jit_solution(16026379800079477513)
XLA Ops:
  2.6 4.0 %collective-permute-start.1 = (bf16[160,2048]{1,0:T(8,128)(2,1)}, bf16[160,2048]{1,0:T(8,128)(2,1)S(1)}, u32[]{:S(2)}, u32[]{:S(2)}) collective-permute-start(bf16[160,2048]{1,0:T(8,128)(2,1)} %bitcast.28), channel_id=1, source_target_pairs={{0,7},{1,0},{2,1},{3,2},{4,3},{5,4},{6,5},{7,6},{8,15},{9,8},{10,9... | collective-permute-start | bytes 1966088 | tf_op jit(solution)/shard_map/ppermute | solution.py:141
  8.1 2.1 %collective-permute-start.4 = (bf16[160,2048]{1,0:T(8,128)(2,1)}, bf16[160,2048]{1,0:T(8,128)(2,1)S(1)}, u32[]{:S(2)}, u32[]{:S(2)}) collective-permute-start(bf16[160,2048]{1,0:T(8,128)(2,1)} %bitcast.20), channel_id=1, source_target_pairs={{0,8},{8,0},{1,9},{9,1},{2,10},{10,2},{3,11},{11,3},{4,12},{12,4},... | collective-permute-start | bytes 1966088 | tf_op jit(solution)/shard_map/ppermute | solution.py:141
  13.5 8.0 %collective-permute-done.refs_6_ = bf16[160,2048]{1,0:T(8,128)(2,1)S(1)} collective-permute-done((bf16[160,2048]{1,0:T(8,128)(2,1)}, bf16[160,2048]{1,0:T(8,128)(2,1)S(1)}, u32[]{:S(2)}, u32[]{:S(2)}) %collective-permute-start) | collective-permute-done | bytes 655392 | tf_op jit(solution)/shard_map/ppermute | solution.py:141
  21.5 3.2 %collective-permute-start.3 = (bf16[160,2048]{1,0:T(8,128)(2,1)S(1)}, bf16[160,2048]{1,0:T(8,128)(2,1)S(1)}, u32[]{:S(2)}, u32[]{:S(2)}) collective-permute-start(bf16[160,2048]{1,0:T(8,128)(2,1)S(1)} %collective-permute-done.1.refs_5_), channel_id=1, source_target_pairs={{0,7},{1,0},{2,1},{3,2},{4,3},{5,4},{6,5},{7,6},{8,15},{9,8},{10,9... | collective-permute-start | bytes 1966088 | tf_op jit(solution)/shard_map/ppermute | solution.py:141
  26.7 13.4 %collective-permute-done.4.refs_3_ = bf16[160,2048]{1,0:T(8,128)(2,1)S(1)} collective-permute-done((bf16[160,2048]{1,0:T(8,128)(2,1)}, bf16[160,2048]{1,0:T(8,128)(2,1)S(1)}, u32[]{:S(2)}, u32[]{:S(2)}) %collective-permute-start.4) | collective-permute-done | bytes 655392 | tf_op jit(solution)/shard_map/ppermute | solution.py:141
  40.5 2.9 %collective-permute-start.7 = (bf16[160,2048]{1,0:T(8,128)(2,1)S(1)}, bf16[160,2048]{1,0:T(8,128)(2,1)S(1)}, u32[]{:S(2)}, u32[]{:S(2)}) collective-permute-start(bf16[160,2048]{1,0:T(8,128)(2,1)S(1)} %collective-permute-done.3.refs_7_), channel_id=1, source_target_pairs={{0,7},{1,0},{2,1},{3,2},{4,3},{5,4},{6,5},{7,6},{8,15},{9,8},{10,9... | collective-permute-start | bytes 1966088 | tf_op jit(solution)/shard_map/ppermute | solution.py:141
  45.3 4.3 %shard_map.104 = (bf16[16,208,128]{2,1,0:T(8,128)(2,1)}, bf16[16,208,128]{2,1,0:T(8,128)(2,1)S(1)}) custom-call(bf16[160,2048]{1,0:T(8,128)(2,1)S(1)} %bitcast.30, bf16[160,2048]{1,0:T(8,128)(2,1)S(1)} %collective-permute-done.5.refs_1_, bf16[160,2048]{1,0:T(8,128)(2,1)S(1)} %bitcast.21, bf16[160,2048]{1,0:T(8,128)(2,1)S(1)} %collective-permute-done.4.refs_3_, ...), custom_call_target="tpu_custom_call" | custom-call | flops 2097152000 | tf_op jit(solution)/shard_map/pallas_call | solution.py:127
  49.6 5.5 %collective-permute-done.6.refs_5_ = bf16[160,2048]{1,0:T(8,128)(2,1)S(1)} collective-permute-done((bf16[160,2048]{1,0:T(8,128)(2,1)S(1)}, bf16[160,2048]{1,0:T(8,128)(2,1)S(1)}, u32[]{:S(2)}, u32[]{:S(2)}) %collective-permute-start.6) | collective-permute-done | bytes 655392 | tf_op jit(solution)/shard_map/ppermute | solution.py:141
  56.5 2.2 %collective-permute-start.9 = (bf16[80,2048]{1,0:T(8,128)(2,1)S(1)}, bf16[80,2048]{1,0:T(8,128)(2,1)S(1)}, u32[]{:S(2)}, u32[]{:S(2)}) collective-permute-start(bf16[80,2048]{1,0:T(8,128)(2,1)S(1)} %slice.45), channel_id=1, source_target_pairs={{0,7},{1,0},{2,1},{3,2},{4,3},{5,4},{6,5},{7,6},{8,15},{9,8},{10,9... | collective-permute-start | bytes 983048 | tf_op jit(solution)/shard_map/ppermute | solution.py:141
  58.7 2.3 %shard_map.105 = (bf16[16,208,128]{2,1,0:T(8,128)(2,1)}, bf16[16,208,128]{2,1,0:T(8,128)(2,1)S(1)}) custom-call(bf16[160,2048]{1,0:T(8,128)(2,1)S(1)} %bitcast.32, bf16[160,2048]{1,0:T(8,128)(2,1)S(1)} %collective-permute-done.5.refs_1_, bf16[160,2048]{1,0:T(8,128)(2,1)S(1)} %bitcast.22, ...), custom_call_target="tpu_custom_call", output_to_operand_aliasing={{0}: (6, {}), {1}: (7, {})} | custom-call | flops 838860800 | tf_op jit(solution)/shard_map/pallas_call | solution.py:127
  61.0 2.5 %collective-permute-done.10.refs_5_ = bf16[80,2048]{1,0:T(8,128)(2,1)S(1)} collective-permute-done((bf16[80,2048]{1,0:T(8,128)(2,1)S(1)}, bf16[80,2048]{1,0:T(8,128)(2,1)S(1)}, u32[]{:S(2)}, u32[]{:S(2)}) %collective-permute-start.10) | collective-permute-done | bytes 327712 | tf_op jit(solution)/shard_map/ppermute | solution.py:141
  63.9 2.6 %shard_map.106 = (bf16[16,208,128]{2,1,0:T(8,128)(2,1)}, bf16[16,208,128]{2,1,0:T(8,128)(2,1)S(1)}) custom-call(bf16[160,2048]{1,0:T(8,128)(2,1)S(1)} %bitcast.33, bf16[160,2048]{1,0:T(8,128)(2,1)S(1)} %collective-permute-done.5.refs_1_, bf16[160,2048]{1,0:T(8,128)(2,1)S(1)} %bitcast.23, ...), custom_call_target="tpu_custom_call", output_to_operand_aliasing={{0}: (6, {}), {1}: (7, {})} | custom-call | flops 419430400 | tf_op jit(solution)/shard_map/pallas_call | solution.py:127
  66.5 3.4 %collective-permute-done.11.refs_1_ = bf16[160,2560]{1,0:T(8,128)(2,1)S(1)} collective-permute-done((bf16[160,2560]{1,0:T(8,128)(2,1)S(1)}, bf16[160,2560]{1,0:T(8,128)(2,1)S(1)}, u32[]{:S(2)}, u32[]{:S(2)}) %collective-permute-start.11) | collective-permute-done | bytes 819232 | tf_op jit(solution)/shard_map/ppermute | solution.py:260
  70.8 4.2 %all-to-all-start = ((bf16[16,208,128]{2,1,0:T(8,128)(2,1)}), bf16[16,208,128]{2,1,0:T(8,128)(2,1)S(1)}, u32[]{:S(2)}, u32[]{:S(2)}) async-start(bf16[16,208,128]{2,1,0:T(8,128)(2,1)} %get-tuple-element.69), calls=%async_computation | async-start | bytes 1703936 | tf_op jit(solution)/shard_map/all_to_all | solution.py:145
  75.7 2.9 %collective-permute-start.15 = (bf16[160,2048]{1,0:T(8,128)(2,1)S(1)}, bf16[160,2048]{1,0:T(8,128)(2,1)}, u32[]{:S(2)}, u32[]{:S(2)}) collective-permute-start(bf16[160,2048]{1,0:T(8,128)(2,1)S(1)} %bitcast.25), channel_id=1, source_target_pairs={{0,7},{1,0},{2,1},{3,2},{4,3},{5,4},{6,5},{7,6},{8,15},{9,8},{10,9... | collective-permute-start | bytes 1966088 | tf_op jit(solution)/shard_map/ppermute | solution.py:141
  79.0 9.3 %all-to-all-done.refs_0_ = bf16[16,208,128]{2,1,0:T(8,128)(2,1)S(1)} async-done(((bf16[16,208,128]{2,1,0:T(8,128)(2,1)}), bf16[16,208,128]{2,1,0:T(8,128)(2,1)S(1)}, u32[]{:S(2)}, u32[]{:S(2)}) %all-to-all-start) | async-done | bytes 852000 | tf_op jit(solution)/shard_map/all_to_all | solution.py:145
  93.6 6.1 %all-to-all-start.1 = ((bf16[8,208,128]{2,1,0:T(8,128)(2,1)}), bf16[8,208,128]{2,1,0:T(8,128)(2,1)S(1)}, u32[]{:S(2)}, u32[]{:S(2)}) async-start(bf16[8,208,128]{2,1,0:T(8,128)(2,1)} %shard_map.109), calls=%async_computation.1 | async-start | bytes 851968 | tf_op jit(solution)/shard_map/all_to_all | solution.py:145
  102.4 3.6 %collective-permute-done.16.refs_1_ = bf16[4,208,128]{2,1,0:T(8,128)(2,1)S(1)} collective-permute-done((bf16[4,208,128]{2,1,0:T(8,128)(2,1)S(1)}, bf16[4,208,128]{2,1,0:T(8,128)(2,1)S(1)}, u32[]{:S(2)}, u32[]{:S(2)}) %collective-permute-start.16) | collective-permute-done | bytes 213024 | tf_op jit(solution)/shard_map/ppermute | solution.py:141
  106.4 3.5 %collective-permute-done.17.refs_1_ = f32[2,160]{1,0:T(2,128)S(1)} collective-permute-done((f32[2,160]{1,0:T(2,128)S(1)}, f32[2,160]{1,0:T(2,128)S(1)}, u32[]{:S(2)}, u32[]{:S(2)}) %collective-permute-start.17) | collective-permute-done | bytes 1312 | tf_op jit(solution)/shard_map/ppermute | solution.py:269
  109.9 4.6 %all-to-all-done.1.refs_0_ = bf16[8,208,128]{2,1,0:T(8,128)(2,1)S(1)} async-done(((bf16[8,208,128]{2,1,0:T(8,128)(2,1)}), bf16[8,208,128]{2,1,0:T(8,128)(2,1)S(1)}, u32[]{:S(2)}, u32[]{:S(2)}) %all-to-all-start.1) | async-done | bytes 426016 | tf_op jit(solution)/shard_map/all_to_all | solution.py:145
  116.2 7.0 %all-to-all-start.2 = ((bf16[16,208,128]{2,1,0:T(8,128)(2,1)}), bf16[16,208,128]{2,1,0:T(8,128)(2,1)S(1)}, u32[]{:S(2)}, u32[]{:S(2)}) async-start(bf16[16,208,128]{2,1,0:T(8,128)(2,1)} %shard_map.111), calls=%async_computation.2 | async-start | bytes 1703936 | tf_op jit(solution)/shard_map/all_to_all | solution.py:145
  123.8 10.8 %all-to-all-done.2.refs_0_ = bf16[16,208,128]{2,1,0:T(8,128)(2,1)S(1)} async-done(((bf16[16,208,128]{2,1,0:T(8,128)(2,1)}), bf16[16,208,128]{2,1,0:T(8,128)(2,1)S(1)}, u32[]{:S(2)}, u32[]{:S(2)}) %all-to-all-start.2) | async-done | bytes 852000 | tf_op jit(solution)/shard_map/all_to_all | solution.py:145
  135.9 3.5 %all-to-all-start.3 = ((bf16[8,208,128]{2,1,0:T(8,128)(2,1)}), bf16[8,208,128]{2,1,0:T(8,128)(2,1)S(1)}, u32[]{:S(2)}, u32[]{:S(2)}) async-start(bf16[8,208,128]{2,1,0:T(8,128)(2,1)} %copy-done.4), calls=%async_computation.3 | async-start | bytes 851968 | tf_op jit(solution)/shard_map/all_to_all | solution.py:145
  139.4 3.2 %collective-permute-start.25 = (bf16[160,2048]{1,0:T(8,128)(2,1)}, bf16[160,2048]{1,0:T(8,128)(2,1)}, u32[]{:S(2)}, u32[]{:S(2)}) collective-permute-start(bf16[160,2048]{1,0:T(8,128)(2,1)} %collective-permute-done.15.refs_3_), channel_id=1, source_target_pairs={{0,7},{1,0},{2,1},{3,2},{4,3},{5,4},{6,5},{7,6},{8,15},{9,8},{10,9... | collective-permute-start | bytes 1966088 | tf_op jit(solution)/shard_map/ppermute | solution.py:141
  144.8 3.3 %collective-permute-start.19 = (bf16[208,128]{1,0:T(8,128)(2,1)S(1)}, bf16[208,128]{1,0:T(8,128)(2,1)S(1)}, u32[]{:S(2)}, u32[]{:S(2)}) collective-permute-start(bf16[208,128]{1,0:T(8,128)(2,1)S(1)} %get-tuple-element.102), channel_id=1, source_target_pairs={{0,128},{64,192},{128,0},{192,64},{1,129},{65,193},{129,1},{193,65... | collective-permute-start | bytes 159752 | tf_op jit(solution)/shard_map/ppermute | solution.py:141
  157.1 8.0 %all-to-all-start.4 = ((bf16[16,208,128]{2,1,0:T(8,128)(2,1)}), bf16[16,208,128]{2,1,0:T(8,128)(2,1)S(1)}, u32[]{:S(2)}, u32[]{:S(2)}) async-start(bf16[16,208,128]{2,1,0:T(8,128)(2,1)} %shard_map.115), calls=%async_computation.4 | async-start | bytes 1703936 | tf_op jit(solution)/shard_map/all_to_all | solution.py:145
  165.1 5.4 %shard_map.116 = bf16[16,208,128]{2,1,0:T(8,128)(2,1)S(1)} custom-call(bf16[160,2048]{1,0:T(8,128)(2,1)} %collective-permute-done.23.refs_0_, bf16[160,2048]{1,0:T(8,128)(2,1)} %collective-permute-done.14.refs_1_, bf16[160,2048]{1,0:T(8,128)(2,1)S(1)} %bitcast.26, bf16[160,2048]{1,0:T(8,128)(2,1)} %collective-permute-done.15.refs_3_, ...), custom_call_target="tpu_custom_call" | custom-call | flops 1048576000 | bytes 3932160 | tf_op jit(solution)/shard_map/pallas_call | solution.py:127
  173.4 3.6 %all-to-all-done.4.refs_0_ = bf16[16,208,128]{2,1,0:T(8,128)(2,1)S(1)} async-done(((bf16[16,208,128]{2,1,0:T(8,128)(2,1)}), bf16[16,208,128]{2,1,0:T(8,128)(2,1)S(1)}, u32[]{:S(2)}, u32[]{:S(2)}) %all-to-all-start.4) | async-done | bytes 852000 | tf_op jit(solution)/shard_map/all_to_all | solution.py:145
  177.0 4.3 %all-to-all-start.5 = ((bf16[8,208,128]{2,1,0:T(8,128)(2,1)}), bf16[8,208,128]{2,1,0:T(8,128)(2,1)S(1)}, u32[]{:S(2)}, u32[]{:S(2)}) async-start(bf16[8,208,128]{2,1,0:T(8,128)(2,1)} %shard_map.117), calls=%async_computation.5 | async-start | bytes 851968 | tf_op jit(solution)/shard_map/all_to_all | solution.py:145
  181.4 7.0 %collective-permute-start.21 = (bf16[1,160,160]{2,1,0:T(8,128)(2,1)S(1)}, bf16[1,160,160]{2,1,0:T(8,128)(2,1)S(1)}, u32[]{:S(2)}, u32[]{:S(2)}) collective-permute-start(bf16[1,160,160]{2,1,0:T(8,128)(2,1)S(1)} %shard_map.113), channel_id=1, source_target_pairs={{0,0},{1,1},{2,2},{3,3},{4,4},{5,5},{6,6},{7,7},{8,128},{9,129},{1... | collective-permute-start | bytes 153608 | tf_op jit(solution)/shard_map/ppermute | solution.py:360
  188.9 2.8 %collective-permute-start.28 = (bf16[1,160,160]{2,1,0:T(8,128)(2,1)S(1)}, bf16[1,160,160]{2,1,0:T(8,128)(2,1)S(1)}, u32[]{:S(2)}, u32[]{:S(2)}) collective-permute-start(bf16[1,160,160]{2,1,0:T(8,128)(2,1)S(1)} %shard_map.120), channel_id=1, source_target_pairs={{0,0},{1,1},{2,2},{3,3},{4,4},{5,5},{6,6},{7,7},{8,128},{9,129},{1... | collective-permute-start | bytes 153608 | tf_op jit(solution)/shard_map/ppermute | solution.py:387
  196.3 7.5 %collective-permute-done.27.refs_1_ = bf16[1,160,160]{2,1,0:T(8,128)(2,1)S(1)} collective-permute-done((bf16[1,160,160]{2,1,0:T(8,128)(2,1)S(1)}, bf16[1,160,160]{2,1,0:T(8,128)(2,1)S(1)}, u32[]{:S(2)}, u32[]{:S(2)}) %collective-permute-start.27) | collective-permute-done | bytes 51232 | tf_op jit(solution)/shard_map/ppermute | solution.py:394
  (89 shorter events, 47.1 us)
Async XLA Ops:
  0.6 20.9 %collective-permute-start = (bf16[160,2048]{1,0:T(8,128)(2,1)}, bf16[160,2048]{1,0:T(8,128)(2,1)S(1)}, u32[]{:S(2)}, u32[]{:S(2)}) collective-permute-start(bf16[160,2048]{1,0:T(8,128)(2,1)} %bitcast.27), channel_id=1, source_target_pairs={{0,1},{1,2},{2,3},{3,4},{4,5},{5,6},{6,7},{7,0},{8,9},{9,10},{10,1... | collective-permute-start | bytes 1966088 | tf_op jit(solution)/shard_map/ppermute | solution.py:141
  2.6 18.9 %collective-permute-start.1 = (bf16[160,2048]{1,0:T(8,128)(2,1)}, bf16[160,2048]{1,0:T(8,128)(2,1)S(1)}, u32[]{:S(2)}, u32[]{:S(2)}) collective-permute-start(bf16[160,2048]{1,0:T(8,128)(2,1)} %bitcast.28), channel_id=1, source_target_pairs={{0,7},{1,0},{2,1},{3,2},{4,3},{5,4},{6,5},{7,6},{8,15},{9,8},{10,9... | collective-permute-start | bytes 1966088 | tf_op jit(solution)/shard_map/ppermute | solution.py:141
  6.7 20.0 %collective-permute-start.5 = (bf16[160,2048]{1,0:T(8,128)(2,1)}, bf16[160,2048]{1,0:T(8,128)(2,1)S(1)}, u32[]{:S(2)}, u32[]{:S(2)}) collective-permute-start(bf16[160,2048]{1,0:T(8,128)(2,1)} %bitcast.29), channel_id=1, source_target_pairs={{0,8},{8,0},{1,9},{9,1},{2,10},{10,2},{3,11},{11,3},{4,12},{12,4},... | collective-permute-start | bytes 1966088 | tf_op jit(solution)/shard_map/ppermute | solution.py:141
  8.1 32.0 %collective-permute-start.4 = (bf16[160,2048]{1,0:T(8,128)(2,1)}, bf16[160,2048]{1,0:T(8,128)(2,1)S(1)}, u32[]{:S(2)}, u32[]{:S(2)}) collective-permute-start(bf16[160,2048]{1,0:T(8,128)(2,1)} %bitcast.20), channel_id=1, source_target_pairs={{0,8},{8,0},{1,9},{9,1},{2,10},{10,2},{3,11},{11,3},{4,12},{12,4},... | collective-permute-start | bytes 1966088 | tf_op jit(solution)/shard_map/ppermute | solution.py:141
  21.5 18.6 %collective-permute-start.2 = (bf16[160,2048]{1,0:T(8,128)(2,1)S(1)}, bf16[160,2048]{1,0:T(8,128)(2,1)S(1)}, u32[]{:S(2)}, u32[]{:S(2)}) collective-permute-start(bf16[160,2048]{1,0:T(8,128)(2,1)S(1)} %collective-permute-done.refs_6_), channel_id=1, source_target_pairs={{0,1},{1,2},{2,3},{3,4},{4,5},{5,6},{6,7},{7,0},{8,9},{9,10},{10,1... | collective-permute-start | bytes 1966088 | tf_op jit(solution)/shard_map/ppermute | solution.py:141
  21.5 18.6 %collective-permute-start.3 = (bf16[160,2048]{1,0:T(8,128)(2,1)S(1)}, bf16[160,2048]{1,0:T(8,128)(2,1)S(1)}, u32[]{:S(2)}, u32[]{:S(2)}) collective-permute-start(bf16[160,2048]{1,0:T(8,128)(2,1)S(1)} %collective-permute-done.1.refs_5_), channel_id=1, source_target_pairs={{0,7},{1,0},{2,1},{3,2},{4,3},{5,4},{6,5},{7,6},{8,15},{9,8},{10,9... | collective-permute-start | bytes 1966088 | tf_op jit(solution)/shard_map/ppermute | solution.py:141
  24.7 24.8 %collective-permute-start.8 = (bf16[160,2560]{1,0:T(8,128)(2,1)S(1)}, bf16[160,2560]{1,0:T(8,128)(2,1)S(1)}, u32[]{:S(2)}, u32[]{:S(2)}) collective-permute-start(bf16[160,2560]{1,0:T(8,128)(2,1)S(1)} %bitcast.37), channel_id=1, source_target_pairs={{0,0},{1,1},{2,2},{3,3},{4,4},{5,5},{6,6},{7,7},{8,16},{9,17},{10,... | collective-permute-start | bytes 2457608 | tf_op jit(solution)/shard_map/ppermute | solution.py:222
  40.1 15.0 %collective-permute-start.6 = (bf16[160,2048]{1,0:T(8,128)(2,1)S(1)}, bf16[160,2048]{1,0:T(8,128)(2,1)S(1)}, u32[]{:S(2)}, u32[]{:S(2)}) collective-permute-start(bf16[160,2048]{1,0:T(8,128)(2,1)S(1)} %collective-permute-done.2.refs_8_), channel_id=1, source_target_pairs={{0,1},{1,2},{2,3},{3,4},{4,5},{5,6},{6,7},{7,0},{8,9},{9,10},{10,1... | collective-permute-start | bytes 1966088 | tf_op jit(solution)/shard_map/ppermute | solution.py:141
  40.5 14.6 %collective-permute-start.7 = (bf16[160,2048]{1,0:T(8,128)(2,1)S(1)}, bf16[160,2048]{1,0:T(8,128)(2,1)S(1)}, u32[]{:S(2)}, u32[]{:S(2)}) collective-permute-start(bf16[160,2048]{1,0:T(8,128)(2,1)S(1)} %collective-permute-done.3.refs_7_), channel_id=1, source_target_pairs={{0,7},{1,0},{2,1},{3,2},{4,3},{5,4},{6,5},{7,6},{8,15},{9,8},{10,9... | collective-permute-start | bytes 1966088 | tf_op jit(solution)/shard_map/ppermute | solution.py:141
  43.3 26.6 %collective-permute-start.11 = (bf16[160,2560]{1,0:T(8,128)(2,1)S(1)}, bf16[160,2560]{1,0:T(8,128)(2,1)S(1)}, u32[]{:S(2)}, u32[]{:S(2)}) collective-permute-start(bf16[160,2560]{1,0:T(8,128)(2,1)S(1)} %bitcast.36), channel_id=1, source_target_pairs={{0,0},{1,1},{2,2},{3,3},{4,4},{5,5},{6,6},{7,7},{128,8},{129,9},{1... | collective-permute-start | bytes 2457608 | tf_op jit(solution)/shard_map/ppermute | solution.py:260
  55.1 8.4 %collective-permute-start.10 = (bf16[80,2048]{1,0:T(8,128)(2,1)S(1)}, bf16[80,2048]{1,0:T(8,128)(2,1)S(1)}, u32[]{:S(2)}, u32[]{:S(2)}) collective-permute-start(bf16[80,2048]{1,0:T(8,128)(2,1)S(1)} %slice.46), channel_id=1, source_target_pairs={{0,1},{1,2},{2,3},{3,4},{4,5},{5,6},{6,7},{7,0},{8,9},{9,10},{10,1... | collective-permute-start | bytes 983048 | tf_op jit(solution)/shard_map/ppermute | solution.py:141
  56.5 7.3 %collective-permute-start.9 = (bf16[80,2048]{1,0:T(8,128)(2,1)S(1)}, bf16[80,2048]{1,0:T(8,128)(2,1)S(1)}, u32[]{:S(2)}, u32[]{:S(2)}) collective-permute-start(bf16[80,2048]{1,0:T(8,128)(2,1)S(1)} %slice.45), channel_id=1, source_target_pairs={{0,7},{1,0},{2,1},{3,2},{4,3},{5,4},{6,5},{7,6},{8,15},{9,8},{10,9... | collective-permute-start | bytes 983048 | tf_op jit(solution)/shard_map/ppermute | solution.py:141
  70.8 17.5 %all-to-all-start = ((bf16[16,208,128]{2,1,0:T(8,128)(2,1)}), bf16[16,208,128]{2,1,0:T(8,128)(2,1)S(1)}, u32[]{:S(2)}, u32[]{:S(2)}) async-start(bf16[16,208,128]{2,1,0:T(8,128)(2,1)} %get-tuple-element.69), calls=%async_computation | async-start | bytes 1703936 | tf_op jit(solution)/shard_map/all_to_all | solution.py:145
  75.1 3.5 %collective-permute-start.12 = (bf16[8,208,128]{2,1,0:T(8,128)(2,1)S(1)}, bf16[8,208,128]{2,1,0:T(8,128)(2,1)S(1)}, u32[]{:S(2)}, u32[]{:S(2)}) collective-permute-start(bf16[8,208,128]{2,1,0:T(8,128)(2,1)S(1)} %get-tuple-element.97), channel_id=1, source_target_pairs={{0,16},{16,0},{1,17},{17,1},{2,18},{18,2},{3,19},{19,3},{4,20},{20... | collective-permute-start | bytes 1277960 | tf_op jit(solution)/shard_map/ppermute | solution.py:141
  75.3 18.3 %collective-permute-start.14 = (bf16[160,2048]{1,0:T(8,128)(2,1)S(1)}, bf16[160,2048]{1,0:T(8,128)(2,1)}, u32[]{:S(2)}, u32[]{:S(2)}) collective-permute-start(bf16[160,2048]{1,0:T(8,128)(2,1)S(1)} %bitcast.24), channel_id=1, source_target_pairs={{0,1},{1,2},{2,3},{3,4},{4,5},{5,6},{6,7},{7,0},{8,9},{9,10},{10,1... | collective-permute-start | bytes 1966088 | tf_op jit(solution)/shard_map/ppermute | solution.py:141
  75.7 18.0 %collective-permute-start.15 = (bf16[160,2048]{1,0:T(8,128)(2,1)S(1)}, bf16[160,2048]{1,0:T(8,128)(2,1)}, u32[]{:S(2)}, u32[]{:S(2)}) collective-permute-start(bf16[160,2048]{1,0:T(8,128)(2,1)S(1)} %bitcast.25), channel_id=1, source_target_pairs={{0,7},{1,0},{2,1},{3,2},{4,3},{5,4},{6,5},{7,6},{8,15},{9,8},{10,9... | collective-permute-start | bytes 1966088 | tf_op jit(solution)/shard_map/ppermute | solution.py:141
  93.6 20.9 %all-to-all-start.1 = ((bf16[8,208,128]{2,1,0:T(8,128)(2,1)}), bf16[8,208,128]{2,1,0:T(8,128)(2,1)S(1)}, u32[]{:S(2)}, u32[]{:S(2)}) async-start(bf16[8,208,128]{2,1,0:T(8,128)(2,1)} %shard_map.109), calls=%async_computation.1 | async-start | bytes 851968 | tf_op jit(solution)/shard_map/all_to_all | solution.py:145
  99.7 6.3 %collective-permute-start.16 = (bf16[4,208,128]{2,1,0:T(8,128)(2,1)S(1)}, bf16[4,208,128]{2,1,0:T(8,128)(2,1)S(1)}, u32[]{:S(2)}, u32[]{:S(2)}) collective-permute-start(bf16[4,208,128]{2,1,0:T(8,128)(2,1)S(1)} %get-tuple-element.99), channel_id=1, source_target_pairs={{0,32},{32,0},{1,33},{33,1},{2,34},{34,2},{3,35},{35,3},{4,36},{36... | collective-permute-start | bytes 638984 | tf_op jit(solution)/shard_map/ppermute | solution.py:141
  100.5 9.4 %collective-permute-start.17 = (f32[2,160]{1,0:T(2,128)S(1)}, f32[2,160]{1,0:T(2,128)S(1)}, u32[]{:S(2)}, u32[]{:S(2)}) collective-permute-start(f32[2,160]{1,0:T(2,128)S(1)} %pad_maximum_fusion), channel_id=1, source_target_pairs={{0,0},{1,1},{2,2},{3,3},{4,4},{5,5},{6,6},{7,7},{128,8},{129,9},{1... | collective-permute-start | bytes 3848 | tf_op jit(solution)/shard_map/ppermute | solution.py:269
  116.2 18.5 %all-to-all-start.2 = ((bf16[16,208,128]{2,1,0:T(8,128)(2,1)}), bf16[16,208,128]{2,1,0:T(8,128)(2,1)S(1)}, u32[]{:S(2)}, u32[]{:S(2)}) async-start(bf16[16,208,128]{2,1,0:T(8,128)(2,1)} %shard_map.111), calls=%async_computation.2 | async-start | bytes 1703936 | tf_op jit(solution)/shard_map/all_to_all | solution.py:145
  123.2 19.4 %collective-permute-start.23 = (bf16[160,2048]{1,0:T(8,128)(2,1)}, bf16[160,2048]{1,0:T(8,128)(2,1)}, u32[]{:S(2)}, u32[]{:S(2)}) collective-permute-start(bf16[160,2048]{1,0:T(8,128)(2,1)} %collective-permute-done.14.refs_1_), channel_id=1, source_target_pairs={{0,1},{1,2},{2,3},{3,4},{4,5},{5,6},{6,7},{7,0},{8,9},{9,10},{10,1... | collective-permute-start | bytes 1966088 | tf_op jit(solution)/shard_map/ppermute | solution.py:141
  135.9 16.3 %all-to-all-start.3 = ((bf16[8,208,128]{2,1,0:T(8,128)(2,1)}), bf16[8,208,128]{2,1,0:T(8,128)(2,1)S(1)}, u32[]{:S(2)}, u32[]{:S(2)}) async-start(bf16[8,208,128]{2,1,0:T(8,128)(2,1)} %copy-done.4), calls=%async_computation.3 | async-start | bytes 851968 | tf_op jit(solution)/shard_map/all_to_all | solution.py:145
  139.4 25.7 %collective-permute-start.25 = (bf16[160,2048]{1,0:T(8,128)(2,1)}, bf16[160,2048]{1,0:T(8,128)(2,1)}, u32[]{:S(2)}, u32[]{:S(2)}) collective-permute-start(bf16[160,2048]{1,0:T(8,128)(2,1)} %collective-permute-done.15.refs_3_), channel_id=1, source_target_pairs={{0,7},{1,0},{2,1},{3,2},{4,3},{5,4},{6,5},{7,6},{8,15},{9,8},{10,9... | collective-permute-start | bytes 1966088 | tf_op jit(solution)/shard_map/ppermute | solution.py:141
  142.6 14.6 %collective-permute-start.24 = (bf16[160,2048]{1,0:T(8,128)(2,1)}, bf16[160,2048]{1,0:T(8,128)(2,1)}, u32[]{:S(2)}, u32[]{:S(2)}) collective-permute-start(bf16[160,2048]{1,0:T(8,128)(2,1)} %collective-permute-done.23.refs_0_), channel_id=1, source_target_pairs={{0,8},{8,0},{1,9},{9,1},{2,10},{10,2},{3,11},{11,3},{4,12},{12,4},... | collective-permute-start | bytes 1966088 | tf_op jit(solution)/shard_map/ppermute | solution.py:141
  144.7 5.4 %collective-permute-start.18 = (bf16[208,128]{1,0:T(8,128)(2,1)S(1)}, bf16[208,128]{1,0:T(8,128)(2,1)S(1)}, u32[]{:S(2)}, u32[]{:S(2)}) collective-permute-start(bf16[208,128]{1,0:T(8,128)(2,1)S(1)} %get-tuple-element.103), channel_id=1, source_target_pairs={{0,64},{64,128},{128,192},{192,0},{1,65},{65,129},{129,193},{193,1... | collective-permute-start | bytes 159752 | tf_op jit(solution)/shard_map/ppermute | solution.py:141
  144.8 5.9 %collective-permute-start.19 = (bf16[208,128]{1,0:T(8,128)(2,1)S(1)}, bf16[208,128]{1,0:T(8,128)(2,1)S(1)}, u32[]{:S(2)}, u32[]{:S(2)}) collective-permute-start(bf16[208,128]{1,0:T(8,128)(2,1)S(1)} %get-tuple-element.102), channel_id=1, source_target_pairs={{0,128},{64,192},{128,0},{192,64},{1,129},{65,193},{129,1},{193,65... | collective-permute-start | bytes 159752 | tf_op jit(solution)/shard_map/ppermute | solution.py:141
  148.0 4.1 %collective-permute-start.20 = (bf16[208,128]{1,0:T(8,128)(2,1)S(1)}, bf16[208,128]{1,0:T(8,128)(2,1)S(1)}, u32[]{:S(2)}, u32[]{:S(2)}) collective-permute-start(bf16[208,128]{1,0:T(8,128)(2,1)S(1)} %get-tuple-element.101), channel_id=1, source_target_pairs={{0,192},{64,0},{128,64},{192,128},{1,193},{65,1},{129,65},{193,129... | collective-permute-start | bytes 159752 | tf_op jit(solution)/shard_map/ppermute | solution.py:141
  157.1 19.9 %all-to-all-start.4 = ((bf16[16,208,128]{2,1,0:T(8,128)(2,1)}), bf16[16,208,128]{2,1,0:T(8,128)(2,1)S(1)}, u32[]{:S(2)}, u32[]{:S(2)}) async-start(bf16[16,208,128]{2,1,0:T(8,128)(2,1)} %shard_map.115), calls=%async_computation.4 | async-start | bytes 1703936 | tf_op jit(solution)/shard_map/all_to_all | solution.py:145
  177.0 14.8 %all-to-all-start.5 = ((bf16[8,208,128]{2,1,0:T(8,128)(2,1)}), bf16[8,208,128]{2,1,0:T(8,128)(2,1)S(1)}, u32[]{:S(2)}, u32[]{:S(2)}) async-start(bf16[8,208,128]{2,1,0:T(8,128)(2,1)} %shard_map.117), calls=%async_computation.5 | async-start | bytes 851968 | tf_op jit(solution)/shard_map/all_to_all | solution.py:145
  181.4 12.6 %collective-permute-start.21 = (bf16[1,160,160]{2,1,0:T(8,128)(2,1)S(1)}, bf16[1,160,160]{2,1,0:T(8,128)(2,1)S(1)}, u32[]{:S(2)}, u32[]{:S(2)}) collective-permute-start(bf16[1,160,160]{2,1,0:T(8,128)(2,1)S(1)} %shard_map.113), channel_id=1, source_target_pairs={{0,0},{1,1},{2,2},{3,3},{4,4},{5,5},{6,6},{7,7},{8,128},{9,129},{1... | collective-permute-start | bytes 153608 | tf_op jit(solution)/shard_map/ppermute | solution.py:360
  188.9 7.4 %collective-permute-start.28 = (bf16[1,160,160]{2,1,0:T(8,128)(2,1)S(1)}, bf16[1,160,160]{2,1,0:T(8,128)(2,1)S(1)}, u32[]{:S(2)}, u32[]{:S(2)}) collective-permute-start(bf16[1,160,160]{2,1,0:T(8,128)(2,1)S(1)} %shard_map.120), channel_id=1, source_target_pairs={{0,0},{1,1},{2,2},{3,3},{4,4},{5,5},{6,6},{7,7},{8,128},{9,129},{1... | collective-permute-start | bytes 153608 | tf_op jit(solution)/shard_map/ppermute | solution.py:387
  191.9 11.9 %collective-permute-start.27 = (bf16[1,160,160]{2,1,0:T(8,128)(2,1)S(1)}, bf16[1,160,160]{2,1,0:T(8,128)(2,1)S(1)}, u32[]{:S(2)}, u32[]{:S(2)}) collective-permute-start(bf16[1,160,160]{2,1,0:T(8,128)(2,1)S(1)} %shard_map.118), channel_id=1, source_target_pairs={{0,102},{1,119},{2,0},{3,17},{4,34},{5,51},{6,68},{7,85},{8,238},{... | collective-permute-start | bytes 153608 | tf_op jit(solution)/shard_map/ppermute | solution.py:394
  (14 other events, 108.2 us)
